TPU v7x, 256 devices: a whole 4x4x8 slice. The times are simulated.
256 devices in a mesh: seq: 64 (over z, x, core), head: 4 (over y).
Axes of the slice: x: 4, y: 4, z: 8, core: 2. Of those that a mesh axis runs over, the one named last changes fastest.
Arguments:
- queries: bfloat16 [65536, 2048], P('seq', 'head'), may hold values from -5 to 5
- token_keys: bfloat16 [65536, 2048], P('seq', 'head'), may hold values from -5 to 5
- values: bfloat16 [65536, 2048], P('seq', 'head'), may hold values from -120 to 120
- norm_gain: float32 [2048], P('head'), may hold values from 0.25 to 1.75
- out_grad: bfloat16 [65536, 2048], P('seq', 'head'), may hold values from -6 to 6
Outputs:
- normed_out: bfloat16 [65536, 2048], P('seq', 'head')
- grad_queries: bfloat16 [65536, 2048], P('seq', 'head')
- grad_keys: bfloat16 [65536, 2048], P('seq', 'head')
- grad_values: bfloat16 [65536, 2048], P('seq', 'head')
All inputs are finite; a program needn't handle non-finite values.
Results may differ from a plain program's by a relative error of at most 0.006.
Values sent between devices are 32-bit elements; how exact they have to be, the bound alone decides.
No kernel may reach another device: no remote copies, remote signals or barrier semaphores. Data moves between devices by JAX's collectives and lax.ppermute only.
A program may use at most 128 MiB of HBM per device.

v0:
```python
import jax
import jax.numpy as jnp
from jax import lax
from jax.sharding import PartitionSpec as P

DK = 128
DV = 128
BLOCK = 512


def entering(part, axis, combine, identity, reverse):
    count = lax.axis_size(axis)
    place = lax.axis_index(axis)
    ahead = count - 1 - place if reverse else place
    gathered = lax.all_gather(part, axis)
    state = jnp.zeros_like(part) + jnp.asarray(identity, part.dtype)

    def one(turn, state):
        source = count - 1 - turn if reverse else turn
        return combine(state, lax.dynamic_index_in_dim(gathered, source, 0, False))

    return lax.fori_loop(0, ahead, one, state)


def add_states(earlier, later):
    return earlier + later


def on_device(queries, token_keys, values, norm_gain, out_grad):
    length = queries.shape[0]
    head_count = queries.shape[1] // DK
    block_count = length // BLOCK
    query_blocks = queries.reshape(block_count, BLOCK, head_count, DK)
    key_blocks = token_keys.reshape(block_count, BLOCK, head_count, DK)
    value_blocks = values.reshape(block_count, BLOCK, head_count, DV)
    position = lax.iota(jnp.int32, BLOCK)
    causal = (position[:, None] >= position[None, :])[None, None]
    empty_state = jnp.zeros((head_count, DK, DV), jnp.float32)
    kv_terms = jnp.einsum(
        "cthd,cthe->chde", key_blocks, value_blocks, preferred_element_type=jnp.float32
    )
    local_total = jnp.sum(kv_terms, axis=0)
    before = entering(local_total, "seq", add_states, empty_state, False)
    earlier_blocks = jnp.concatenate([empty_state[None], jnp.cumsum(kv_terms[:-1], axis=0)], axis=0)
    prefix_bf = (before[None] + earlier_blocks).astype(jnp.bfloat16)
    scores = jnp.einsum(
        "cthd,cshd->chts", query_blocks, key_blocks, preferred_element_type=jnp.float32
    )
    score_bf = jnp.where(causal, scores, 0.0).astype(jnp.bfloat16)
    block_out = jnp.einsum(
        "chts,cshe->cthe", score_bf, value_blocks, preferred_element_type=jnp.float32
    )
    block_out = block_out + jnp.einsum(
        "cthd,chde->cthe", query_blocks, prefix_bf, preferred_element_type=jnp.float32
    )
    flat_out = block_out.reshape(length, head_count * DV)
    features = lax.axis_size("head") * head_count * DV
    scaled = norm_gain[None, :] * out_grad.astype(jnp.float32)
    local_square = jnp.sum(flat_out * flat_out, axis=1)
    local_inner = jnp.sum(flat_out * scaled, axis=1)
    total_square = lax.psum(local_square, "head")
    total_inner = lax.psum(local_inner, "head")
    root_mean = jnp.sqrt(total_square[:, None] / features + 1e-05)
    normed_out = (norm_gain[None, :] * (flat_out / root_mean)).astype(jnp.bfloat16)
    grad_attn = (
        scaled / root_mean - flat_out * total_inner[:, None] / (features * root_mean**3)
    ).astype(jnp.bfloat16)
    grad_blocks = grad_attn.reshape(block_count, BLOCK, head_count, DV)
    grad_terms = jnp.einsum(
        "cthd,cthe->chde", query_blocks, grad_blocks, preferred_element_type=jnp.float32
    )
    later_sum = entering(jnp.sum(grad_terms, axis=0), "seq", add_states, empty_state, True)
    later_blocks = jnp.flip(jnp.cumsum(jnp.flip(grad_terms[1:], axis=0), axis=0), axis=0)
    suffix_blocks = jnp.concatenate([later_blocks, empty_state[None]], axis=0)
    suffix_bf = (later_sum[None] + suffix_blocks).astype(jnp.bfloat16)
    grad_scores = jnp.einsum(
        "cthe,cshe->chts", grad_blocks, value_blocks, preferred_element_type=jnp.float32
    )
    grad_score_bf = jnp.where(causal, grad_scores, 0.0).astype(jnp.bfloat16)
    grad_query = jnp.einsum(
        "chts,cshd->cthd", grad_score_bf, key_blocks, preferred_element_type=jnp.float32
    )
    grad_query = grad_query + jnp.einsum(
        "cthe,chde->cthd", grad_blocks, prefix_bf, preferred_element_type=jnp.float32
    )
    grad_key = jnp.einsum(
        "chts,cthd->cshd", grad_score_bf, query_blocks, preferred_element_type=jnp.float32
    )
    grad_key = grad_key + jnp.einsum(
        "cshe,chde->cshd", value_blocks, suffix_bf, preferred_element_type=jnp.float32
    )
    grad_value = jnp.einsum(
        "chts,cthe->cshe", score_bf, grad_blocks, preferred_element_type=jnp.float32
    )
    grad_value = grad_value + jnp.einsum(
        "cshd,chde->cshe", key_blocks, suffix_bf, preferred_element_type=jnp.float32
    )
    return (
        normed_out,
        grad_query.reshape(length, head_count * DK).astype(jnp.bfloat16),
        grad_key.reshape(length, head_count * DK).astype(jnp.bfloat16),
        grad_value.reshape(length, head_count * DV).astype(jnp.bfloat16),
    )


def solution(mesh):
    placed = (P("seq", "head"), P("seq", "head"), P("seq", "head"), P("head"), P("seq", "head"))
    return jax.shard_map(
        on_device,
        mesh=mesh,
        in_specs=placed,
        out_specs=(P("seq", "head"), P("seq", "head"), P("seq", "head"), P("seq", "head")),
        check_vma=False,
    )
```

profile of v0, /device:TPU:1, one launch (start us, length us, event | category | flops | bytes accessed | tf_op | source)
XLA Modules:
  0.0 378.2 jit_solution(5106989930794832557)
XLA Ops:
  7.2 1.4 reshape.55
  9.0 2.0 fusion.30
  11.1 1.3 reshape.54
  14.3 1.3 select_convert_fusion.1
  15.6 1.9 copy-done
  17.6 2.8 fusion.9
  20.4 94.9 %all-gather.5.cloned.1.call-done = f32[256,128,128]{2,1,0:T(8,128)} async-done(((f32[4,128,128]{2,1,0:T(8,128)}), f32[256,128,128]{2,1,0:T(8,128)}) %all-gather.5.cloned.1.call-update) | async-done | bytes 16777232 | tf_op jit(solution)/shard_map/all_gather | solution.py:15
  116.4 3.5 multiply_reduce_fusion
  119.8 2.0 copy.64
  121.9 1.6 fusion.2
  123.5 8.7 %all-reduce.2 = (f32[1024]{0:T(1024)S(1)}, f32[1024]{0:T(1024)S(1)}) all-reduce(f32[1024]{0:T(1024)S(1)} %bitcast.80, f32[1024]{0:T(1024)S(1)} %fusion.2), channel_id=1, replica_groups=mesh['seq'=64,'head'=4] {'head'}, use_global_device_ids=true, to_apply=%region_4.5 | all-reduce | flops 2048 | bytes 16384 | tf_op jit(solution)/shard_map/psum | solution.py:61
  132.2 3.0 fusion.5
  135.2 1.3 reshape.58
  137.2 1.9 fusion.31
  139.2 1.8 copy.75
  141.0 1.7 slice.9
  142.7 2.5 select_convert_fusion
  149.6 2.0 fusion.32
  151.6 2.9 fusion.21
  154.4 144.1 %all-gather.7.cloned.1.call-done = f32[256,128,128]{2,1,0:T(8,128)} async-done(((f32[4,128,128]{2,1,0:T(8,128)}), f32[256,128,128]{2,1,0:T(8,128)}) %all-gather.7.cloned.1.call-update) | async-done | bytes 16777232 | tf_op jit(solution)/shard_map/all_gather | solution.py:15
  298.5 64.1 %while.23 = (s32[]{:T(128)}, f32[4,128,128]{2,1,0:T(8,128)S(1)}, s32[]{:T(128)}, f32[64,4,128,128]{3,2,1,0:T(8,128)}, s32[]{:T(128)}, /*index=5*/s32[]{:T(128)}, s32[]{:T(128)}, s32[]{:T(128)}) while((s32[]{:T(128)}, f32[4,128,128]{2,1,0:T(8,128)S(1)}, s32[]{:T(128)}, f32[64,4,128,128]{3,2,1,0:T(8,128)}, s32[]{:T(128)}, /*index=5*/s32[]{:T(128)}, ...), condition=%wide.region_9.10_spmd, body=%wide.region_8.9_spmd.sunk | while | flops 65542 | bytes 786575 | solution.py:22
  363.5 2.2 fusion.8
  366.7 2.1 fusion.6
  369.6 1.7 copy_bitcast_fusion
  (108 shorter events, 74.6 us)
Async XLA Ops:
  7.2 1.5 copy-start.10
  7.2 108.1 %all-gather.5.cloned.1.call-start = ((), (), s32[]{:S(2)}) async-start(), calls=%async_computation | async-start | bytes 17039360 | tf_op jit(solution)/shard_map/all_gather | solution.py:15
  8.7 4.8 %copy-start.4 = (bf16[2,512,4,128]{3,2,1,0:T(4,128)(2,1)}, bf16[2,512,4,128]{3,2,1,0:T(4,128)(2,1)S(1)}, u32[]{:S(2)}) copy-start(bf16[2,512,4,128]{3,2,1,0:T(4,128)(2,1)S(1)} %reshape.55) | copy-start | bytes 3145732
  9.0 6.6 %copy-start.2 = (bf16[2,512,4,128]{3,2,1,0:T(4,128)(2,1)}, bf16[2,512,4,128]{3,2,1,0:T(4,128)(2,1)S(1)}, u32[]{:S(2)}) copy-start(bf16[2,512,4,128]{3,2,1,0:T(4,128)(2,1)S(1)} %reshape.56) | copy-start | bytes 3145732
  11.1 287.4 %all-gather.7.cloned.1.call-start = ((), (), s32[]{:S(2)}) async-start(), calls=%async_computation.1 | async-start | bytes 17039360 | tf_op jit(solution)/shard_map/all_gather | solution.py:15
  13.4 102.9 %copy-start.7 = (f32[1,4,128,128]{3,2,1,0:T(8,128)}, f32[1,4,128,128]{3,2,1,0:T(8,128)S(1)}, u32[]{:S(2)}) copy-start(f32[1,4,128,128]{3,2,1,0:T(8,128)S(1)} %slice.8) | copy-start | bytes 786436
  13.6 0.7 copy-start.11
  15.6 1.9 copy-start
  119.8 2.0 copy-start.12
  137.2 5.4 %copy-start.3 = (bf16[2,512,4,128]{3,2,1,0:T(4,128)(2,1)S(1)}, bf16[2,512,4,128]{3,2,1,0:T(4,128)(2,1)}, u32[]{:S(2)}) copy-start(bf16[2,512,4,128]{3,2,1,0:T(4,128)(2,1)} %copy-done.2) | copy-start | bytes 3145732
  142.7 2.5 copy-start.5
  145.2 1.3 copy-start.8
  147.0 2.6 copy-start.1
  298.5 65.0 %copy-start.6 = (bf16[2,512,4,128]{3,2,1,0:T(4,128)(2,1)S(1)}, bf16[2,512,4,128]{3,2,1,0:T(4,128)(2,1)}, u32[]{:S(2)}) copy-start(bf16[2,512,4,128]{3,2,1,0:T(4,128)(2,1)} %copy-done.4) | copy-start | bytes 3145732
  365.8 1.0 copy-start.9
Sparse Core Ops, SparseCore 0:
  11.4 103.9 all-gather.4
  141.1 157.3 all-gather.6
where the time goes:
time: 381 us; the launch traced here: 378 us
  waiting for transfers between devices  239 us (63%)
  other arithmetic  68.4 us (18%)
  matrix products  25.1 us (7%)
  local copies, waits for them, and re-layouts  21.1 us (6%)
  between operations  14.3 us (4%)
  blocking collectives  8.75 us (2%)
    all_gather x2, waiting for transfers between devices, entering(): gathered = lax.all_gather(part, axis)  239 us
    add x63, other arithmetic, add_states(): return earlier + later  63.7 us
    psum x1, blocking collectives, on_device(): total_square = lax.psum(local_square, 'head')  8.75 us
  transfers between devices with their start and end apart: 2, of which 2 were waited for; matrix products, arithmetic and copies ran while one was open for 5% of the time, Pallas kernels for 0%

commit v1 on v0

v1 whole, which is shorter than its diff:
```python
import jax
import jax.numpy as jnp
from jax import lax
from jax.experimental import pallas as pl
from jax.experimental.pallas import tpu as pltpu
from jax.sharding import PartitionSpec as P

D = 128
BLOCK = 512
HALF = 256
F32 = jnp.float32
BF16 = jnp.bfloat16
PLANES, LINE, CORES = 8, 4, 2


def dot_nn(a, b):
    return lax.dot_general(a, b, (((1,), (0,)), ((), ())), preferred_element_type=F32)


def dot_nt(a, b):
    return lax.dot_general(a, b, (((1,), (1,)), ((), ())), preferred_element_type=F32)


def dot_tn(a, b):
    return lax.dot_general(a, b, (((0,), (0,)), ((), ())), preferred_element_type=F32)


def head_cols(h):
    return slice(h * D, (h + 1) * D)


def params(mib):
    return pltpu.CompilerParams(vmem_limit_bytes=mib * 2**20)


def lower(x):
    t = lax.broadcasted_iota(jnp.int32, x.shape, 0)
    s = lax.broadcasted_iota(jnp.int32, x.shape, 1)
    return jnp.where(t >= s, x, 0.0).astype(BF16)


def masked_product(left, right):
    top, bottom = slice(0, HALF), slice(HALF, BLOCK)
    full = dot_nt(left[bottom], right)
    first = lower(dot_nt(left[top], right[top]))
    return first, full[:, :HALF].astype(BF16), lower(full[:, HALF:])


def per_token(row):
    return jnp.transpose(jnp.broadcast_to(row, (D, row.shape[1])))


def places():
    me = lax.axis_index("seq")
    return me // (LINE * CORES), me // CORES % LINE, me % CORES


def shift(value, plane=0, line=0, swap=False):
    pairs = []
    for z in range(PLANES):
        for x in range(LINE):
            for c in range(CORES):
                source = (z * LINE + x) * CORES + c
                target = ((z + plane) % PLANES * LINE + (x + line) % LINE) * CORES + (1 - c if swap else c)
                pairs.append((source, target))
    return lax.ppermute(value, "seq", pairs)


def small(body, outs, rows, name, *args):
    vmem = pl.BlockSpec(memory_space=pltpu.VMEM)
    return pl.pallas_call(
        body,
        in_specs=[vmem] * len(args),
        out_specs=[vmem] * outs,
        out_shape=[jax.ShapeDtypeStruct((rows, D), F32)] * outs,
        compiler_params=params(4),
        name=name,
    )(*args)


def when(condition, value):
    return jnp.where(condition, value, 0.0)


def entering(mine, theirs, reverse):
    def ahead(other, me):
        return other > me if reverse else other < me

    half = mine.shape[0]
    piece = half // LINE
    partner = shift(theirs, swap=True)

    def split(mine, partner, *outs):
        _, x, _ = places()
        for k, out in enumerate(outs):
            at = pl.ds(pl.multiple_of((x + k) % LINE * piece, piece), piece)
            out[...] = mine[at] + partner[at]

    parts = small(split, LINE, piece, "split", mine, partner)
    parts = [parts[0]] + [shift(parts[k], line=k) for k in range(1, LINE)]

    def add(a, b, c, d, out):
        out[...] = a[...] + b[...] + c[...] + d[...]

    (plane,) = small(add, 1, piece, "add", *parts)
    below, above = shift(plane, plane=1), shift(plane, plane=-1)

    def windows(plane, below, above, to_up, to_down):
        z, _, _ = places()
        before, after = (z + PLANES - 1) % PLANES, (z + 1) % PLANES
        up, down = (z + 3) % PLANES, (z + PLANES - 3) % PLANES
        to_up[...] = (
            when(ahead(before, up), below[...]) + when(ahead(z, up), plane[...]) + when(ahead(after, up), above[...])
        )
        to_down[...] = when(ahead(before, down), below[...]) + when(ahead(z, down), plane[...])

    to_up, to_down = small(windows, 2, piece, "windows", plane, below, above)
    from_down, from_up = shift(to_up, plane=3), shift(to_down, plane=-3)

    def spread(below, above, from_down, from_up, *refs):
        parts, outs = refs[:LINE], refs[LINE:]
        z, x, _ = places()
        before, after = (z + PLANES - 1) % PLANES, (z + 1) % PLANES
        planes = (
            when(ahead(before, z), below[...]) + when(ahead(after, z), above[...]) + from_down[...] + from_up[...]
        )
        for j, out in enumerate(outs):
            target = (x + j) % LINE
            total = planes
            for k, part in enumerate(parts):
                total += when(ahead((x + LINE - k) % LINE, target), part[...])
            out[...] = total

    sent = small(spread, LINE, piece, "spread", below, above, from_down, from_up, *parts)
    got = [sent[0]] + [shift(sent[j], line=j) for j in range(1, LINE)]

    def collect(mine, partner, *refs):
        got, (kept, other) = refs[:LINE], refs[LINE:]
        _, x, c = places()
        for k, part in enumerate(got):
            at = pl.ds(pl.multiple_of((x + LINE - k) % LINE * piece, piece), piece)
            kept[at] = part[...] + when(ahead(1 - c, c), partner[at])
            other[at] = part[...] + when(ahead(c, 1 - c), mine[at])

    kept, other = small(collect, 2, half, "collect", mine, partner, *got)
    return kept, shift(other, swap=True)


def state_of(h, kept, other):
    _, _, c = places()
    heads = kept.shape[0] // D
    at = slice(h % heads * D, (h % heads + 1) * D)
    return jnp.where(c == h // heads, kept[at], other[at])


def products(left, right):
    width = left.shape[1]
    heads = width // D

    def body(a, b, first, mine, theirs):
        h = pl.program_id(0)
        _, _, c = places()
        one = dot_tn(a[:BLOCK], b[:BLOCK])
        total = one + dot_tn(a[BLOCK:], b[BLOCK:])
        first[...] = one
        at = pl.ds(pl.multiple_of(h % (heads // CORES) * D, D), D)

        @pl.when(h // (heads // CORES) == c)
        def _():
            mine[at] = total

        @pl.when(h // (heads // CORES) != c)
        def _():
            theirs[at] = total

    column = pl.BlockSpec((2 * BLOCK, D), lambda h: (0, h))
    half = pl.BlockSpec((width // CORES, D), lambda h: (0, 0))
    half_shape = jax.ShapeDtypeStruct((width // CORES, D), F32)
    return pl.pallas_call(
        body,
        grid=(heads,),
        in_specs=[column, column],
        out_specs=[pl.BlockSpec((D, D), lambda h: (h, 0)), half, half],
        out_shape=[jax.ShapeDtypeStruct((width, D), F32), half_shape, half_shape],
        compiler_params=params(8),
        name="products",
    )(left, right)


def local_attention(q, k, v, heads, first_head, cost=True):
    length = q.shape[0]

    def body(q, k, v, out):
        qv, kv, vv = q[...], k[...], v[...]
        a, b, c = masked_product(qv, kv)
        out[:HALF] = dot_nn(a, vv[:HALF])
        out[HALF:] = dot_nn(b, vv[:HALF]) + dot_nn(c, vv[HALF:])

    spec = pl.BlockSpec((BLOCK, D), lambda c, h: (c, first_head + h))
    return pl.pallas_call(
        body,
        grid=(length // BLOCK, heads),
        in_specs=[spec, spec, spec],
        out_specs=pl.BlockSpec((BLOCK, D), lambda c, h: (c, h)),
        out_shape=jax.ShapeDtypeStruct((length, heads * D), F32),
        compiler_params=params(8),
        cost_estimate=pl.CostEstimate(
            flops=length // BLOCK * heads * 4 * BLOCK * BLOCK * D,
            bytes_accessed=length * heads * D * 10,
            transcendentals=0,
        ),
        name="local_attention",
    )(q, k, v)


def attention_sums(q, grad, local, gain, kept, other, first):
    length, width = q.shape
    heads = width // D

    def body(q, grad, local, gain, kept, other, first, attn, sums):
        later = (pl.program_id(0) > 0).astype(F32)
        square = jnp.zeros((BLOCK, D), F32)
        inner = jnp.zeros((BLOCK, D), F32)
        for h in range(heads):
            cols = head_cols(h)
            prefix = (state_of(h, kept, other) + later * first[cols]).astype(BF16)
            a = local[:, cols] + dot_nn(q[:, cols], prefix)
            attn[:, cols] = a
            square += a * a
            inner += a * (gain[:, cols] * grad[:, cols].astype(F32))
        sums[0:1] = jnp.sum(jnp.transpose(square), axis=0, keepdims=True)
        sums[1:2] = jnp.sum(jnp.transpose(inner), axis=0, keepdims=True)

    rows = pl.BlockSpec((BLOCK, width), lambda c: (c, 0))
    whole = pl.BlockSpec((width, D), lambda c: (0, 0))
    half = pl.BlockSpec((width // CORES, D), lambda c: (0, 0))
    return pl.pallas_call(
        body,
        grid=(length // BLOCK,),
        in_specs=[rows, rows, rows, pl.BlockSpec((1, width), lambda c: (0, 0)), half, half, whole],
        out_specs=[rows, pl.BlockSpec((2, BLOCK), lambda c: (0, c))],
        out_shape=[
            jax.ShapeDtypeStruct((length, width), F32),
            jax.ShapeDtypeStruct((2, length), F32),
        ],
        compiler_params=params(12),
        name="attention_sums",
    )(q, grad, local, gain, kept, other, first)


def token_scales(sums, features):
    root = jnp.sqrt(sums[0:1] / features + 1e-05)
    inverse = 1.0 / root
    weight = sums[1:2] / (features * root**3)
    return per_token(inverse), per_token(weight)


def gradient(q, grad, attn, gain, sums, features):
    length, width = q.shape
    heads = width // D
    per_core = heads // CORES

    def body(q, grad, attn, gain, sums, out, last, mine, theirs):
        step = pl.program_id(0)
        _, _, c = places()
        inverse, weight = token_scales(sums[...], features)
        for h in range(heads):
            cols = head_cols(h)
            scaled = gain[:, cols] * grad[:, cols].astype(F32)
            g = (scaled * inverse - attn[:, cols] * weight).astype(BF16)
            out[:, cols] = g
            term = dot_tn(q[:, cols], g)
            last[cols] = term
            at = head_cols(h % per_core)
            for owned, half in ((c, mine), (1 - c, theirs)):

                @pl.when((owned == h // per_core) & (step == 0))
                def _(half=half):
                    half[at] = term

                @pl.when((owned == h // per_core) & (step > 0))
                def _(half=half):
                    half[at] += term

    rows = pl.BlockSpec((BLOCK, width), lambda c: (c, 0))
    whole = pl.BlockSpec((width, D), lambda c: (0, 0))
    half = pl.BlockSpec((width // CORES, D), lambda c: (0, 0))
    half_shape = jax.ShapeDtypeStruct((width // CORES, D), F32)
    return pl.pallas_call(
        body,
        grid=(length // BLOCK,),
        in_specs=[
            rows,
            rows,
            rows,
            pl.BlockSpec((1, width), lambda c: (0, 0)),
            pl.BlockSpec((2, BLOCK), lambda c: (0, c)),
        ],
        out_specs=[rows, whole, half, half],
        out_shape=[
            jax.ShapeDtypeStruct((length, width), BF16),
            jax.ShapeDtypeStruct((width, D), F32),
            half_shape,
            half_shape,
        ],
        compiler_params=params(12),
        name="gradient",
    )(q, grad, attn, gain, sums)


def local_gradients(q, k, v, g, attn, gain, sums, kept, other, first, features):
    length, width = q.shape
    heads = width // D
    per_core = heads // CORES

    def body(q, k, v, g, attn, gain, sums, kept, other, first, normed, dq, dk, dv):
        later = (pl.program_id(0) > 0).astype(F32)
        root = jnp.sqrt(sums[0:1] / features + 1e-05)
        normed[...] = (gain[...] * (attn[...] * per_token(1.0 / root))).astype(BF16)
        h = pl.program_id(1)
        _, _, core = places()
        at = pl.ds(pl.multiple_of(h % per_core * D, D), D)
        state = jnp.where(core == h // per_core, kept[at], other[at])
        prefix = (state + later * first[...]).astype(BF16)
        top, bottom = slice(0, HALF), slice(HALF, BLOCK)
        qv, kv, vv, gv = q[...], k[...], v[...], g[...]
        a, b, c = masked_product(gv, vv)
        carried = dot_nt(gv, prefix)
        dq[top] = (dot_nn(a, kv[top]) + carried[top]).astype(BF16)
        dq[bottom] = (dot_nn(b, kv[top]) + dot_nn(c, kv[bottom]) + carried[bottom]).astype(BF16)
        dk[top] = dot_tn(a, qv[top]) + dot_tn(b, qv[bottom])
        dk[bottom] = dot_tn(c, qv[bottom])
        a, b, c = masked_product(qv, kv)
        dv[top] = dot_tn(a, gv[top]) + dot_tn(b, gv[bottom])
        dv[bottom] = dot_tn(c, gv[bottom])

    tile = pl.BlockSpec((BLOCK, D), lambda c, h: (c, h))
    one = pl.BlockSpec((D, D), lambda c, h: (h, 0))
    half = pl.BlockSpec((width // CORES, D), lambda c, h: (0, 0))
    return pl.pallas_call(
        body,
        grid=(length // BLOCK, heads),
        in_specs=[tile] * 5
        + [
            pl.BlockSpec((1, D), lambda c, h: (0, h)),
            pl.BlockSpec((2, BLOCK), lambda c, h: (0, c)),
            half,
            half,
            one,
        ],
        out_specs=[tile] * 4,
        out_shape=[jax.ShapeDtypeStruct((length, width), t) for t in (BF16, BF16, F32, F32)],
        compiler_params=params(12),
        cost_estimate=pl.CostEstimate(
            flops=length // BLOCK * heads * 10 * BLOCK * BLOCK * D,
            bytes_accessed=length * width * 24,
            transcendentals=0,
        ),
        name="local_gradients",
    )(q, k, v, g, attn, gain, sums, kept, other, first)


def add_suffix(k, v, dk, dv, kept, other, last):
    length, width = k.shape
    heads = width // D
    rows_of = HALF

    def body(k, v, dk, dv, kept, other, last, out_k, out_v):
        earlier = (pl.program_id(0) < BLOCK // rows_of).astype(F32)
        for h in range(heads):
            cols = head_cols(h)
            suffix = (state_of(h, kept, other) + earlier * last[cols]).astype(BF16)
            out_k[:, cols] = (dk[:, cols] + dot_nt(v[:, cols], suffix)).astype(BF16)
            out_v[:, cols] = (dv[:, cols] + dot_nn(k[:, cols], suffix)).astype(BF16)

    rows = pl.BlockSpec((rows_of, width), lambda c: (c, 0))
    whole = pl.BlockSpec((width, D), lambda c: (0, 0))
    half = pl.BlockSpec((width // CORES, D), lambda c: (0, 0))
    shape = jax.ShapeDtypeStruct((length, width), BF16)
    return pl.pallas_call(
        body,
        grid=(length // rows_of,),
        in_specs=[rows, rows, rows, rows, half, half, whole],
        out_specs=[rows, rows],
        out_shape=[shape, shape],
        compiler_params=params(12),
        name="add_suffix",
    )(k, v, dk, dv, kept, other, last)


def head_sum(part):
    count = lax.axis_size("head")
    total = part
    for k in range(1, count):
        total = total + lax.ppermute(part, "head", [(i, (i + k) % count) for i in range(count)])
    return total


def on_device(queries, token_keys, values, norm_gain, out_grad):
    heads = queries.shape[1] // D
    features = lax.axis_size("head") * heads * D
    gain = norm_gain.reshape(1, heads * D)
    first, mine, theirs = products(token_keys, values)
    local = local_attention(queries, token_keys, values, heads, 0)
    kept, other = entering(mine, theirs, False)
    attn, sums = attention_sums(queries, out_grad, local, gain, kept, other, first)
    sums = head_sum(sums)
    grad_attn, last, mine, theirs = gradient(queries, out_grad, attn, gain, sums, features)
    normed_out, grad_query, key_part, value_part = local_gradients(
        queries, token_keys, values, grad_attn, attn, gain, sums, kept, other, first, features
    )
    kept, other = entering(mine, theirs, True)
    grad_key, grad_value = add_suffix(token_keys, values, key_part, value_part, kept, other, last)
    return normed_out, grad_query, grad_key, grad_value


def solution(mesh):
    placed = (P("seq", "head"), P("seq", "head"), P("seq", "head"), P("head"), P("seq", "head"))
    return jax.shard_map(
        on_device,
        mesh=mesh,
        in_specs=placed,
        out_specs=(P("seq", "head"), P("seq", "head"), P("seq", "head"), P("seq", "head")),
        check_vma=False,
    )
```

time: 381 us -> 104 us (0.27)
  waiting for transfers between devices: 239 us -> 24.4 us
  other arithmetic: 68.4 us -> 0.01 us
  starting transfers between devices: 0.08 us -> 51.9 us
  matrix products: 25.1 us -> 0 us
  Pallas kernels: 0 us -> 22.5 us
  local copies, waits for them, and re-layouts: 21.1 us -> 2.47 us
  between operations: 14.3 us -> 0.82 us
  blocking collectives: 8.75 us -> 0 us
    all_gather x2 -> x0, waiting for transfers between devices: 239 us -> none  [entering(): gathered = lax.all_gather(part, axis)]
    add x63 -> x1, other arithmetic: 63.7 us -> 0.01 us  [head_sum(): total + lax.ppermute(part, 'head', [(i, (i + k) % count) for i in range(c...]
    ppermute x0 -> x27, starting transfers between devices: none -> 51.9 us  [the longest x24 48.1 us: shift(): return lax.ppermute(value, 'seq', pairs)]
    dot_general x12 -> x0, matrix products: 25.1 us -> none  [the longest x1 3.45 us: on_device(): jnp.einsum('cthd,chde->cthe', query_blocks, prefix_bf, preferred_element_...]
    ppermute x0 -> x27, waiting for transfers between devices: none -> 24.4 us  [the longest x24 21.3 us: shift(): return lax.ppermute(value, 'seq', pairs)]
    pallas_call x0 -> x16, Pallas kernels: none -> 22.5 us  [the longest x1 9.81 us: local_gradients(): pl.pallas_call(body, grid=(length // BLOCK, heads), in_specs=[tile] * 5 +...]
    psum x1 -> x0, blocking collectives: 8.75 us -> none  [on_device(): total_square = lax.psum(local_square, 'head')]
    reshape x5 -> x0, local copies, waits for them, and re-layouts: 5.05 us -> none  [the longest x2 2.01 us: on_device(): grad_blocks = grad_attn.reshape(block_count, BLOCK, head_count, DV)]
  transfers between devices with their start and end apart: 2 -> 27, of which waited for: 2 -> 23; matrix products, arithmetic and copies ran while one was open for 5% -> 0% of each run, Pallas kernels for 0% -> 14%
where the time goes in v1:
time: 104 us; the launch traced here: 102 us
  starting transfers between devices  51.9 us (50%)
  waiting for transfers between devices  24.4 us (23%)
  Pallas kernels  22.5 us (22%)
  local copies, waits for them, and re-layouts  2.47 us (2%)
    ppermute x24, starting transfers between devices, shift(): return lax.ppermute(value, 'seq', pairs)  48.1 us
    ppermute x24, waiting for transfers between devices, shift(): return lax.ppermute(value, 'seq', pairs)  21.3 us
    pallas_call x1, Pallas kernels, local_gradients(): pl.pallas_call(body, grid=(length // BLOCK, heads), in_specs=[tile] * 5 +...  9.81 us
    pallas_call x1, Pallas kernels, local_attention(): pl.pallas_call(body, grid=(length // BLOCK, heads), in_specs=[spec, spec,...  4.74 us
    ppermute x3, starting transfers between devices, head_sum(): lax.ppermute(part, 'head', [(i, (i + k) % count) for i in range(count)])  3.85 us
    ppermute x3, waiting for transfers between devices, head_sum(): lax.ppermute(part, 'head', [(i, (i + k) % count) for i in range(count)])  3.05 us
    pallas_call x1, Pallas kernels, add_suffix(): pl.pallas_call(body, grid=(length // rows_of,), in_specs=[rows, rows, row...  2.52 us
    unnamed x14, local copies, waits for them, and re-layouts  2.47 us
  transfers between devices with their start and end apart: 27, of which 23 were waited for; matrix products, arithmetic and copies ran while one was open for 0% of the time, Pallas kernels for 14%

profile of v1, /device:TPU:1, one launch (start us, length us, event | category | flops | bytes accessed | tf_op | source)
XLA Modules:
  0.0 102.1 jit_solution(17238813807710376513)
XLA Ops:
  3.1 1.5 %products.1 = (f32[512,128]{1,0:T(8,128)S(1)}, f32[256,128]{1,0:T(8,128)S(1)}, f32[256,128]{1,0:T(8,128)S(1)}) custom-call(bf16[1024,512]{1,0:T(8,128)(2,1)S(1)} %copy-done, bf16[1024,512]{1,0:T(8,128)(2,1)S(1)} %copy-done.2), custom_call_target="tpu_custom_call" | custom-call | tf_op jit(solution)/shard_map/products/pallas_call | solution.py:179
  4.6 3.3 %collective-permute-start = (f32[256,128]{1,0:T(8,128)S(1)}, f32[256,128]{1,0:T(8,128)S(1)}, u32[]{:S(2)}, u32[]{:S(2)}) collective-permute-start(f32[256,128]{1,0:T(8,128)S(1)} %get-tuple-element.44), channel_id=1, source_target_pairs={{0,4},{4,0},{8,12},{12,8},{16,20},{20,16},{24,28},{28,24},{32,36},... | collective-permute-start | bytes 393224 | tf_op jit(solution)/shard_map/ppermute | solution.py:66
  9.1 1.9 %collective-permute-start.2 = (f32[64,128]{1,0:T(8,128)S(1)}, f32[64,128]{1,0:T(8,128)S(1)}, u32[]{:S(2)}, u32[]{:S(2)}) collective-permute-start(f32[64,128]{1,0:T(8,128)S(1)} %get-tuple-element.47), channel_id=1, source_target_pairs={{0,16},{4,20},{8,24},{12,28},{16,0},{20,4},{24,8},{28,12},{32,48},... | collective-permute-start | bytes 98312 | tf_op jit(solution)/shard_map/ppermute | solution.py:66
  14.3 5.4 %collective-permute-start.5 = (f32[64,128]{1,0:T(8,128)S(1)}, f32[64,128]{1,0:T(8,128)S(1)}, u32[]{:S(2)}, u32[]{:S(2)}) collective-permute-start(f32[64,128]{1,0:T(8,128)S(1)} %add.17.plane), channel_id=1, source_target_pairs={{0,224},{4,228},{8,232},{12,236},{16,240},{20,244},{24,248},{28,25... | collective-permute-start | bytes 98312 | tf_op jit(solution)/shard_map/ppermute | solution.py:66
  20.7 3.0 %collective-permute-done.4.below = f32[64,128]{1,0:T(8,128)S(1)} collective-permute-done((f32[64,128]{1,0:T(8,128)S(1)}, f32[64,128]{1,0:T(8,128)S(1)}, u32[]{:S(2)}, u32[]{:S(2)}) %collective-permute-start.4) | collective-permute-done | bytes 32800 | tf_op jit(solution)/shard_map/ppermute | solution.py:66
  23.8 4.5 %collective-permute-start.7 = (f32[64,128]{1,0:T(8,128)S(1)}, f32[64,128]{1,0:T(8,128)S(1)}, u32[]{:S(2)}, u32[]{:S(2)}) collective-permute-start(f32[64,128]{1,0:T(8,128)S(1)} %get-tuple-element.50), channel_id=1, source_target_pairs={{0,160},{4,164},{8,168},{12,172},{16,176},{20,180},{24,184},{28,18... | collective-permute-start | bytes 98312 | tf_op jit(solution)/shard_map/ppermute | solution.py:66
  28.2 1.3 %collective-permute-done.6.from_down = f32[64,128]{1,0:T(8,128)S(1)} collective-permute-done((f32[64,128]{1,0:T(8,128)S(1)}, f32[64,128]{1,0:T(8,128)S(1)}, u32[]{:S(2)}, u32[]{:S(2)}) %collective-permute-start.6) | collective-permute-done | bytes 32800 | tf_op jit(solution)/shard_map/ppermute | solution.py:66
  29.7 3.2 %collective-permute-start.9 = (f32[64,128]{1,0:T(8,128)S(1)}, f32[64,128]{1,0:T(8,128)S(1)}, u32[]{:S(2)}, u32[]{:S(2)}) collective-permute-start(f32[64,128]{1,0:T(8,128)S(1)} %get-tuple-element.53), channel_id=1, source_target_pairs={{0,16},{4,20},{8,24},{12,28},{16,0},{20,4},{24,8},{28,12},{32,48},... | collective-permute-start | bytes 98312 | tf_op jit(solution)/shard_map/ppermute | solution.py:66
  35.8 6.4 %collective-permute-start.11 = (f32[256,128]{1,0:T(8,128)S(1)}, f32[256,128]{1,0:T(8,128)S(1)}, u32[]{:S(2)}, u32[]{:S(2)}) collective-permute-start(f32[256,128]{1,0:T(8,128)S(1)} %get-tuple-element.56), channel_id=1, source_target_pairs={{0,4},{4,0},{8,12},{12,8},{16,20},{20,16},{24,28},{28,24},{32,36},... | collective-permute-start | bytes 393224 | tf_op jit(solution)/shard_map/ppermute | solution.py:66
  42.3 4.7 %local_attention.1.local = f32[1024,512]{1,0:T(8,128)S(1)} custom-call(bf16[1024,512]{1,0:T(8,128)(2,1)S(1)} %copy-done.4, bf16[1024,512]{1,0:T(8,128)(2,1)S(1)} %copy-done.1, bf16[1024,512]{1,0:T(8,128)(2,1)S(1)} %copy-done.2), custom_call_target="tpu_custom_call" | custom-call | flops 1073741824 | bytes 5242880 | tf_op jit(solution)/shard_map/local_attention/pallas_call | solution.py:200
  48.2 2.8 %collective-permute-start.14 = (f32[2,1024]{1,0:T(2,128)S(1)}, f32[2,1024]{1,0:T(2,128)S(1)}, u32[]{:S(2)}, u32[]{:S(2)}) collective-permute-start(f32[2,1024]{1,0:T(2,128)S(1)} %get-tuple-element.59), channel_id=1, source_target_pairs={{0,3},{1,0},{2,1},{3,2},{4,7},{5,4},{6,5},{7,6},{8,11},{9,8},{10,9... | collective-permute-start | bytes 24584 | tf_op jit(solution)/shard_map/ppermute | solution.py:395
  52.0 3.0 %collective-permute-done.13 = f32[2,1024]{1,0:T(2,128)S(1)} collective-permute-done((f32[2,1024]{1,0:T(2,128)S(1)}, f32[2,1024]{1,0:T(2,128)S(1)}, u32[]{:S(2)}, u32[]{:S(2)}) %collective-permute-start.13) | collective-permute-done | bytes 8224 | tf_op jit(solution)/shard_map/ppermute | solution.py:395
  55.1 2.4 %gradient.1 = (bf16[1024,512]{1,0:T(8,128)(2,1)S(1)}, f32[512,128]{1,0:T(8,128)S(1)}, f32[256,128]{1,0:T(8,128)S(1)}, f32[256,128]{1,0:T(8,128)S(1)}) custom-call(bf16[1024,512]{1,0:T(8,128)(2,1)S(1)} %copy-done.4, bf16[1024,512]{1,0:T(8,128)(2,1)S(1)} %copy-done.5, f32[1024,512]{1,0:T(8,128)S(1)} %get-tuple-element.58.attn, f32[1,512]{1,0:T(1,128)S(1)} %bitcast.2, ...), custom_call_target="tpu_custom_call" | custom-call | tf_op jit(solution)/shard_map/gradient/pallas_call | solution.py:289
  57.6 1.8 %collective-permute-start.15 = (f32[256,128]{1,0:T(8,128)S(1)}, f32[256,128]{1,0:T(8,128)S(1)}, u32[]{:S(2)}, u32[]{:S(2)}) collective-permute-start(f32[256,128]{1,0:T(8,128)S(1)} %get-tuple-element.66), channel_id=1, source_target_pairs={{0,4},{4,0},{8,12},{12,8},{16,20},{20,16},{24,28},{28,24},{32,36},... | collective-permute-start | bytes 393224 | tf_op jit(solution)/shard_map/ppermute | solution.py:66
  60.5 2.1 %collective-permute-start.17 = (f32[64,128]{1,0:T(8,128)S(1)}, f32[64,128]{1,0:T(8,128)S(1)}, u32[]{:S(2)}, u32[]{:S(2)}) collective-permute-start(f32[64,128]{1,0:T(8,128)S(1)} %get-tuple-element.69), channel_id=1, source_target_pairs={{0,16},{4,20},{8,24},{12,28},{16,0},{20,4},{24,8},{28,12},{32,48},... | collective-permute-start | bytes 98312 | tf_op jit(solution)/shard_map/ppermute | solution.py:66
  65.9 1.9 %collective-permute-start.19 = (f32[64,128]{1,0:T(8,128)S(1)}, f32[64,128]{1,0:T(8,128)S(1)}, u32[]{:S(2)}, u32[]{:S(2)}) collective-permute-start(f32[64,128]{1,0:T(8,128)S(1)} %add.18.plane), channel_id=1, source_target_pairs={{0,32},{4,36},{8,40},{12,44},{16,48},{20,52},{24,56},{28,60},{32,6... | collective-permute-start | bytes 98312 | tf_op jit(solution)/shard_map/ppermute | solution.py:66
  69.9 2.5 %collective-permute-start.21 = (f32[64,128]{1,0:T(8,128)S(1)}, f32[64,128]{1,0:T(8,128)S(1)}, u32[]{:S(2)}, u32[]{:S(2)}) collective-permute-start(f32[64,128]{1,0:T(8,128)S(1)} %get-tuple-element.71), channel_id=1, source_target_pairs={{0,96},{4,100},{8,104},{12,108},{16,112},{20,116},{24,120},{28,124... | collective-permute-start | bytes 98312 | tf_op jit(solution)/shard_map/ppermute | solution.py:66
  72.3 2.1 %collective-permute-start.22 = (f32[64,128]{1,0:T(8,128)S(1)}, f32[64,128]{1,0:T(8,128)S(1)}, u32[]{:S(2)}, u32[]{:S(2)}) collective-permute-start(f32[64,128]{1,0:T(8,128)S(1)} %get-tuple-element.72), channel_id=1, source_target_pairs={{0,160},{4,164},{8,168},{12,172},{16,176},{20,180},{24,184},{28,18... | collective-permute-start | bytes 98312 | tf_op jit(solution)/shard_map/ppermute | solution.py:66
  74.4 1.6 %collective-permute-done.21.from_down = f32[64,128]{1,0:T(8,128)S(1)} collective-permute-done((f32[64,128]{1,0:T(8,128)S(1)}, f32[64,128]{1,0:T(8,128)S(1)}, u32[]{:S(2)}, u32[]{:S(2)}) %collective-permute-start.21) | collective-permute-done | bytes 32800 | tf_op jit(solution)/shard_map/ppermute | solution.py:66
  78.2 2.4 %collective-permute-start.24 = (f32[64,128]{1,0:T(8,128)S(1)}, f32[64,128]{1,0:T(8,128)S(1)}, u32[]{:S(2)}, u32[]{:S(2)}) collective-permute-start(f32[64,128]{1,0:T(8,128)S(1)} %get-tuple-element.75), channel_id=1, source_target_pairs={{0,16},{4,20},{8,24},{12,28},{16,0},{20,4},{24,8},{28,12},{32,48},... | collective-permute-start | bytes 98312 | tf_op jit(solution)/shard_map/ppermute | solution.py:66
  81.3 1.2 %collective-permute-done.24.refs_2_ = f32[64,128]{1,0:T(8,128)S(1)} collective-permute-done((f32[64,128]{1,0:T(8,128)S(1)}, f32[64,128]{1,0:T(8,128)S(1)}, u32[]{:S(2)}, u32[]{:S(2)}) %collective-permute-start.24) | collective-permute-done | bytes 32800 | tf_op jit(solution)/shard_map/ppermute | solution.py:66
  83.5 6.3 %collective-permute-start.26 = (f32[256,128]{1,0:T(8,128)S(1)}, f32[256,128]{1,0:T(8,128)S(1)}, u32[]{:S(2)}, u32[]{:S(2)}) collective-permute-start(f32[256,128]{1,0:T(8,128)S(1)} %get-tuple-element.78), channel_id=1, source_target_pairs={{0,4},{4,0},{8,12},{12,8},{16,20},{20,16},{24,28},{28,24},{32,36},... | collective-permute-start | bytes 393224 | tf_op jit(solution)/shard_map/ppermute | solution.py:66
  89.7 9.8 %local_gradients.1 = (bf16[1024,512]{1,0:T(8,128)(2,1)}, bf16[1024,512]{1,0:T(8,128)(2,1)}, f32[1024,512]{1,0:T(8,128)S(1)}, f32[1024,512]{1,0:T(8,128)S(1)}) custom-call(bf16[1024,512]{1,0:T(8,128)(2,1)S(1)} %copy-done.4, bf16[1024,512]{1,0:T(8,128)(2,1)S(1)} %copy-done.1, bf16[1024,512]{1,0:T(8,128)(2,1)S(1)} %copy-done.3, ...), custom_call_target="tpu_custom_call" | custom-call | flops 2684354560 | bytes 12582912 | tf_op jit(solution)/shard_map/local_gradients/pallas_call | solution.py:340
  99.5 2.5 %add_suffix.1 = (bf16[1024,512]{1,0:T(8,128)(2,1)}, bf16[1024,512]{1,0:T(8,128)(2,1)}) custom-call(bf16[1024,512]{1,0:T(8,128)(2,1)S(1)} %copy-done.1, bf16[1024,512]{1,0:T(8,128)(2,1)S(1)} %copy-done.3, f32[1024,512]{1,0:T(8,128)S(1)} %get-tuple-element.63.dk, f32[1024,512]{1,0:T(8,128)S(1)} %get-tuple-element.64.dv, ...), custom_call_target="tpu_custom_call" | custom-call | tf_op jit(solution)/shard_map/add_suffix/pallas_call | solution.py:380
  (61 shorter events, 23.3 us)
Async XLA Ops:
  4.6 4.3 %collective-permute-start = (f32[256,128]{1,0:T(8,128)S(1)}, f32[256,128]{1,0:T(8,128)S(1)}, u32[]{:S(2)}, u32[]{:S(2)}) collective-permute-start(f32[256,128]{1,0:T(8,128)S(1)} %get-tuple-element.44), channel_id=1, source_target_pairs={{0,4},{4,0},{8,12},{12,8},{16,20},{20,16},{24,28},{28,24},{32,36},... | collective-permute-start | bytes 393224 | tf_op jit(solution)/shard_map/ppermute | solution.py:66
  9.0 4.1 %collective-permute-start.1 = (f32[64,128]{1,0:T(8,128)S(1)}, f32[64,128]{1,0:T(8,128)S(1)}, u32[]{:S(2)}, u32[]{:S(2)}) collective-permute-start(f32[64,128]{1,0:T(8,128)S(1)} %get-tuple-element.46), channel_id=1, source_target_pairs={{0,8},{4,12},{8,16},{12,20},{16,24},{20,28},{24,0},{28,4},{32,40},... | collective-permute-start | bytes 98312 | tf_op jit(solution)/shard_map/ppermute | solution.py:66
  9.1 4.4 %collective-permute-start.2 = (f32[64,128]{1,0:T(8,128)S(1)}, f32[64,128]{1,0:T(8,128)S(1)}, u32[]{:S(2)}, u32[]{:S(2)}) collective-permute-start(f32[64,128]{1,0:T(8,128)S(1)} %get-tuple-element.47), channel_id=1, source_target_pairs={{0,16},{4,20},{8,24},{12,28},{16,0},{20,4},{24,8},{28,12},{32,48},... | collective-permute-start | bytes 98312 | tf_op jit(solution)/shard_map/ppermute | solution.py:66
  11.0 3.3 %collective-permute-start.3 = (f32[64,128]{1,0:T(8,128)S(1)}, f32[64,128]{1,0:T(8,128)S(1)}, u32[]{:S(2)}, u32[]{:S(2)}) collective-permute-start(f32[64,128]{1,0:T(8,128)S(1)} %get-tuple-element.48), channel_id=1, source_target_pairs={{0,24},{4,28},{8,0},{12,4},{16,8},{20,12},{24,16},{28,20},{32,56},... | collective-permute-start | bytes 98312 | tf_op jit(solution)/shard_map/ppermute | solution.py:66
  14.3 6.5 %collective-permute-start.5 = (f32[64,128]{1,0:T(8,128)S(1)}, f32[64,128]{1,0:T(8,128)S(1)}, u32[]{:S(2)}, u32[]{:S(2)}) collective-permute-start(f32[64,128]{1,0:T(8,128)S(1)} %add.17.plane), channel_id=1, source_target_pairs={{0,224},{4,228},{8,232},{12,236},{16,240},{20,244},{24,248},{28,25... | collective-permute-start | bytes 98312 | tf_op jit(solution)/shard_map/ppermute | solution.py:66
  19.7 4.0 %collective-permute-start.4 = (f32[64,128]{1,0:T(8,128)S(1)}, f32[64,128]{1,0:T(8,128)S(1)}, u32[]{:S(2)}, u32[]{:S(2)}) collective-permute-start(f32[64,128]{1,0:T(8,128)S(1)} %add.17.plane), channel_id=1, source_target_pairs={{0,32},{4,36},{8,40},{12,44},{16,48},{20,52},{24,56},{28,60},{32,6... | collective-permute-start | bytes 98312 | tf_op jit(solution)/shard_map/ppermute | solution.py:66
  23.7 5.9 %collective-permute-start.6 = (f32[64,128]{1,0:T(8,128)S(1)}, f32[64,128]{1,0:T(8,128)S(1)}, u32[]{:S(2)}, u32[]{:S(2)}) collective-permute-start(f32[64,128]{1,0:T(8,128)S(1)} %get-tuple-element.49), channel_id=1, source_target_pairs={{0,96},{4,100},{8,104},{12,108},{16,112},{20,116},{24,120},{28,124... | collective-permute-start | bytes 98312 | tf_op jit(solution)/shard_map/ppermute | solution.py:66
  23.8 5.8 %collective-permute-start.7 = (f32[64,128]{1,0:T(8,128)S(1)}, f32[64,128]{1,0:T(8,128)S(1)}, u32[]{:S(2)}, u32[]{:S(2)}) collective-permute-start(f32[64,128]{1,0:T(8,128)S(1)} %get-tuple-element.50), channel_id=1, source_target_pairs={{0,160},{4,164},{8,168},{12,172},{16,176},{20,180},{24,184},{28,18... | collective-permute-start | bytes 98312 | tf_op jit(solution)/shard_map/ppermute | solution.py:66
  29.7 4.1 %collective-permute-start.8 = (f32[64,128]{1,0:T(8,128)S(1)}, f32[64,128]{1,0:T(8,128)S(1)}, u32[]{:S(2)}, u32[]{:S(2)}) collective-permute-start(f32[64,128]{1,0:T(8,128)S(1)} %get-tuple-element.52), channel_id=1, source_target_pairs={{0,8},{4,12},{8,16},{12,20},{16,24},{20,28},{24,0},{28,4},{32,40},... | collective-permute-start | bytes 98312 | tf_op jit(solution)/shard_map/ppermute | solution.py:66
  29.7 4.9 %collective-permute-start.9 = (f32[64,128]{1,0:T(8,128)S(1)}, f32[64,128]{1,0:T(8,128)S(1)}, u32[]{:S(2)}, u32[]{:S(2)}) collective-permute-start(f32[64,128]{1,0:T(8,128)S(1)} %get-tuple-element.53), channel_id=1, source_target_pairs={{0,16},{4,20},{8,24},{12,28},{16,0},{20,4},{24,8},{28,12},{32,48},... | collective-permute-start | bytes 98312 | tf_op jit(solution)/shard_map/ppermute | solution.py:66
  35.8 11.2 %collective-permute-start.11 = (f32[256,128]{1,0:T(8,128)S(1)}, f32[256,128]{1,0:T(8,128)S(1)}, u32[]{:S(2)}, u32[]{:S(2)}) collective-permute-start(f32[256,128]{1,0:T(8,128)S(1)} %get-tuple-element.56), channel_id=1, source_target_pairs={{0,4},{4,0},{8,12},{12,8},{16,20},{20,16},{24,28},{28,24},{32,36},... | collective-permute-start | bytes 393224 | tf_op jit(solution)/shard_map/ppermute | solution.py:66
  48.2 3.9 %collective-permute-start.14 = (f32[2,1024]{1,0:T(2,128)S(1)}, f32[2,1024]{1,0:T(2,128)S(1)}, u32[]{:S(2)}, u32[]{:S(2)}) collective-permute-start(f32[2,1024]{1,0:T(2,128)S(1)} %get-tuple-element.59), channel_id=1, source_target_pairs={{0,3},{1,0},{2,1},{3,2},{4,7},{5,4},{6,5},{7,6},{8,11},{9,8},{10,9... | collective-permute-start | bytes 24584 | tf_op jit(solution)/shard_map/ppermute | solution.py:395
  51.0 4.0 %collective-permute-start.13 = (f32[2,1024]{1,0:T(2,128)S(1)}, f32[2,1024]{1,0:T(2,128)S(1)}, u32[]{:S(2)}, u32[]{:S(2)}) collective-permute-start(f32[2,1024]{1,0:T(2,128)S(1)} %get-tuple-element.59), channel_id=1, source_target_pairs={{0,2},{1,3},{2,0},{3,1},{4,6},{5,7},{6,4},{7,5},{8,10},{9,11},{10,... | collective-permute-start | bytes 24584 | tf_op jit(solution)/shard_map/ppermute | solution.py:395
  51.3 3.7 %collective-permute-start.12 = (f32[2,1024]{1,0:T(2,128)S(1)}, f32[2,1024]{1,0:T(2,128)S(1)}, u32[]{:S(2)}, u32[]{:S(2)}) collective-permute-start(f32[2,1024]{1,0:T(2,128)S(1)} %get-tuple-element.59), channel_id=1, source_target_pairs={{0,1},{1,2},{2,3},{3,0},{4,5},{5,6},{6,7},{7,4},{8,9},{9,10},{10,1... | collective-permute-start | bytes 24584 | tf_op jit(solution)/shard_map/ppermute | solution.py:395
  60.4 4.1 %collective-permute-start.16 = (f32[64,128]{1,0:T(8,128)S(1)}, f32[64,128]{1,0:T(8,128)S(1)}, u32[]{:S(2)}, u32[]{:S(2)}) collective-permute-start(f32[64,128]{1,0:T(8,128)S(1)} %get-tuple-element.68), channel_id=1, source_target_pairs={{0,8},{4,12},{8,16},{12,20},{16,24},{20,28},{24,0},{28,4},{32,40},... | collective-permute-start | bytes 98312 | tf_op jit(solution)/shard_map/ppermute | solution.py:66
  60.5 4.7 %collective-permute-start.17 = (f32[64,128]{1,0:T(8,128)S(1)}, f32[64,128]{1,0:T(8,128)S(1)}, u32[]{:S(2)}, u32[]{:S(2)}) collective-permute-start(f32[64,128]{1,0:T(8,128)S(1)} %get-tuple-element.69), channel_id=1, source_target_pairs={{0,16},{4,20},{8,24},{12,28},{16,0},{20,4},{24,8},{28,12},{32,48},... | collective-permute-start | bytes 98312 | tf_op jit(solution)/shard_map/ppermute | solution.py:66
  62.6 3.1 %collective-permute-start.18 = (f32[64,128]{1,0:T(8,128)S(1)}, f32[64,128]{1,0:T(8,128)S(1)}, u32[]{:S(2)}, u32[]{:S(2)}) collective-permute-start(f32[64,128]{1,0:T(8,128)S(1)} %get-tuple-element.70), channel_id=1, source_target_pairs={{0,24},{4,28},{8,0},{12,4},{16,8},{20,12},{24,16},{28,20},{32,56},... | collective-permute-start | bytes 98312 | tf_op jit(solution)/shard_map/ppermute | solution.py:66
  65.7 3.3 %collective-permute-start.20 = (f32[64,128]{1,0:T(8,128)S(1)}, f32[64,128]{1,0:T(8,128)S(1)}, u32[]{:S(2)}, u32[]{:S(2)}) collective-permute-start(f32[64,128]{1,0:T(8,128)S(1)} %add.18.plane), channel_id=1, source_target_pairs={{0,224},{4,228},{8,232},{12,236},{16,240},{20,244},{24,248},{28,25... | collective-permute-start | bytes 98312 | tf_op jit(solution)/shard_map/ppermute | solution.py:66
  65.9 4.0 %collective-permute-start.19 = (f32[64,128]{1,0:T(8,128)S(1)}, f32[64,128]{1,0:T(8,128)S(1)}, u32[]{:S(2)}, u32[]{:S(2)}) collective-permute-start(f32[64,128]{1,0:T(8,128)S(1)} %add.18.plane), channel_id=1, source_target_pairs={{0,32},{4,36},{8,40},{12,44},{16,48},{20,52},{24,56},{28,60},{32,6... | collective-permute-start | bytes 98312 | tf_op jit(solution)/shard_map/ppermute | solution.py:66
  69.9 6.2 %collective-permute-start.21 = (f32[64,128]{1,0:T(8,128)S(1)}, f32[64,128]{1,0:T(8,128)S(1)}, u32[]{:S(2)}, u32[]{:S(2)}) collective-permute-start(f32[64,128]{1,0:T(8,128)S(1)} %get-tuple-element.71), channel_id=1, source_target_pairs={{0,96},{4,100},{8,104},{12,108},{16,112},{20,116},{24,120},{28,124... | collective-permute-start | bytes 98312 | tf_op jit(solution)/shard_map/ppermute | solution.py:66
  72.3 4.7 %collective-permute-start.22 = (f32[64,128]{1,0:T(8,128)S(1)}, f32[64,128]{1,0:T(8,128)S(1)}, u32[]{:S(2)}, u32[]{:S(2)}) collective-permute-start(f32[64,128]{1,0:T(8,128)S(1)} %get-tuple-element.72), channel_id=1, source_target_pairs={{0,160},{4,164},{8,168},{12,172},{16,176},{20,180},{24,184},{28,18... | collective-permute-start | bytes 98312 | tf_op jit(solution)/shard_map/ppermute | solution.py:66
  77.0 4.2 %collective-permute-start.23 = (f32[64,128]{1,0:T(8,128)S(1)}, f32[64,128]{1,0:T(8,128)S(1)}, u32[]{:S(2)}, u32[]{:S(2)}) collective-permute-start(f32[64,128]{1,0:T(8,128)S(1)} %get-tuple-element.74), channel_id=1, source_target_pairs={{0,8},{4,12},{8,16},{12,20},{16,24},{20,28},{24,0},{28,4},{32,40},... | collective-permute-start | bytes 98312 | tf_op jit(solution)/shard_map/ppermute | solution.py:66
  78.2 4.3 %collective-permute-start.24 = (f32[64,128]{1,0:T(8,128)S(1)}, f32[64,128]{1,0:T(8,128)S(1)}, u32[]{:S(2)}, u32[]{:S(2)}) collective-permute-start(f32[64,128]{1,0:T(8,128)S(1)} %get-tuple-element.75), channel_id=1, source_target_pairs={{0,16},{4,20},{8,24},{12,28},{16,0},{20,4},{24,8},{28,12},{32,48},... | collective-permute-start | bytes 98312 | tf_op jit(solution)/shard_map/ppermute | solution.py:66
  83.5 16.1 %collective-permute-start.26 = (f32[256,128]{1,0:T(8,128)S(1)}, f32[256,128]{1,0:T(8,128)S(1)}, u32[]{:S(2)}, u32[]{:S(2)}) collective-permute-start(f32[256,128]{1,0:T(8,128)S(1)} %get-tuple-element.78), channel_id=1, source_target_pairs={{0,4},{4,0},{8,12},{12,8},{16,20},{20,16},{24,28},{28,24},{32,36},... | collective-permute-start | bytes 393224 | tf_op jit(solution)/shard_map/ppermute | solution.py:66
  (10 other events, 146.3 us)

commit v2 on v1

v2 whole, which is shorter than its diff:
```python
import jax
import jax.numpy as jnp
from jax import lax
from jax.experimental import pallas as pl
from jax.experimental.pallas import tpu as pltpu
from jax.sharding import PartitionSpec as P

D = 128
BLOCK = 512
HALF = 256
F32 = jnp.float32
BF16 = jnp.bfloat16
PLANES, LINE, CORES = 8, 4, 2


def dot_nn(a, b):
    return lax.dot_general(a, b, (((1,), (0,)), ((), ())), preferred_element_type=F32)


def dot_nt(a, b):
    return lax.dot_general(a, b, (((1,), (1,)), ((), ())), preferred_element_type=F32)


def dot_tn(a, b):
    return lax.dot_general(a, b, (((0,), (0,)), ((), ())), preferred_element_type=F32)


def head_cols(h):
    return slice(h * D, (h + 1) * D)


def params(mib):
    return pltpu.CompilerParams(vmem_limit_bytes=mib * 2**20)


def lower(x):
    t = lax.broadcasted_iota(jnp.int32, x.shape, 0)
    s = lax.broadcasted_iota(jnp.int32, x.shape, 1)
    return jnp.where(t >= s, x, 0.0).astype(BF16)


def upper(x):
    s = lax.broadcasted_iota(jnp.int32, x.shape, 0)
    t = lax.broadcasted_iota(jnp.int32, x.shape, 1)
    return jnp.where(t >= s, x, 0.0).astype(BF16)


TOP, BOTTOM = slice(0, HALF), slice(HALF, BLOCK)
VMEM = pl.BlockSpec(memory_space=pltpu.VMEM)
HBM = pl.BlockSpec(memory_space=pltpu.HBM)
ANY = pl.BlockSpec(memory_space=pl.ANY)


def lower_product(left, right):
    full = dot_nt(left[BOTTOM], right)
    first = lower(dot_nt(left[TOP], right[TOP]))
    return first, full[:, :HALF].astype(BF16), lower(full[:, HALF:])


def upper_product(left, right):
    full = dot_nt(left[TOP], right)
    last = upper(dot_nt(left[BOTTOM], right[BOTTOM]))
    return upper(full[:, :HALF]), full[:, HALF:].astype(BF16), last


def per_token(row):
    return jnp.transpose(jnp.broadcast_to(row, (D, row.shape[1])))


def beside(a, b):
    return jnp.concatenate([a, b], axis=1)


def block_rows(c):
    return slice(c * BLOCK, (c + 1) * BLOCK)


def places():
    me = lax.axis_index("seq")
    return me // (LINE * CORES), me // CORES % LINE, me % CORES


def shift(value, plane=0, line=0, swap=False):
    pairs = []
    for z in range(PLANES):
        for x in range(LINE):
            for c in range(CORES):
                source = (z * LINE + x) * CORES + c
                target = ((z + plane) % PLANES * LINE + (x + line) % LINE) * CORES + (1 - c if swap else c)
                pairs.append((source, target))
    return lax.ppermute(value, "seq", pairs)


def small(body, outs, rows, name, args, after=()):
    def waiting(*refs):
        body(*refs[: len(args)], *refs[len(args) + len(after) :])

    return pl.pallas_call(
        waiting,
        in_specs=[VMEM] * len(args) + [ANY] * len(after),
        out_specs=[VMEM] * outs,
        out_shape=[jax.ShapeDtypeStruct((rows, D), F32)] * outs,
        compiler_params=params(4),
        name=name,
    )(*args, *after)


def when(condition, value):
    return jnp.where(condition, value, 0.0)


def entering(mine, theirs, reverse, beside_rounds):
    def ahead(other, me):
        return other > me if reverse else other < me

    half = mine.shape[0]
    piece = half // LINE
    partner = shift(theirs, swap=True)

    def split(mine, partner, *outs):
        _, x, _ = places()
        for k, out in enumerate(outs):
            at = pl.ds(pl.multiple_of((x + k) % LINE * piece, piece), piece)
            out[...] = mine[at] + partner[at]

    parts = small(split, LINE, piece, "split", (mine, partner))
    done = beside_rounds[0](parts[0])
    parts = [parts[0]] + [shift(parts[k], line=k) for k in range(1, LINE)]

    def add(a, b, c, d, out):
        out[...] = a[...] + b[...] + c[...] + d[...]

    (plane,) = small(add, 1, piece, "add", parts, done)
    done = beside_rounds[1](plane)
    below, above = shift(plane, plane=1), shift(plane, plane=-1)

    def windows(plane, below, above, to_up, to_down):
        z, _, _ = places()
        before, after = (z + PLANES - 1) % PLANES, (z + 1) % PLANES
        up, down = (z + 3) % PLANES, (z + PLANES - 3) % PLANES
        to_up[...] = (
            when(ahead(before, up), below[...]) + when(ahead(z, up), plane[...]) + when(ahead(after, up), above[...])
        )
        to_down[...] = when(ahead(before, down), below[...]) + when(ahead(z, down), plane[...])

    to_up, to_down = small(windows, 2, piece, "windows", (plane, below, above), done)
    done = beside_rounds[2](to_up)
    from_down, from_up = shift(to_up, plane=3), shift(to_down, plane=-3)

    def spread(below, above, from_down, from_up, *refs):
        parts, outs = refs[:LINE], refs[LINE:]
        z, x, _ = places()
        before, after = (z + PLANES - 1) % PLANES, (z + 1) % PLANES
        planes = (
            when(ahead(before, z), below[...]) + when(ahead(after, z), above[...]) + from_down[...] + from_up[...]
        )
        for j, out in enumerate(outs):
            target = (x + j) % LINE
            total = planes
            for k, part in enumerate(parts):
                total += when(ahead((x + LINE - k) % LINE, target), part[...])
            out[...] = total

    sent = small(spread, LINE, piece, "spread", (below, above, from_down, from_up, *parts), done)
    done = beside_rounds[3](sent[0])
    got = [sent[0]] + [shift(sent[j], line=j) for j in range(1, LINE)]

    def collect(mine, partner, *refs):
        got, (kept, other) = refs[:LINE], refs[LINE:]
        _, x, c = places()
        for k, part in enumerate(got):
            at = pl.ds(pl.multiple_of((x + LINE - k) % LINE * piece, piece), piece)
            kept[at] = part[...] + when(ahead(1 - c, c), partner[at])
            other[at] = part[...] + when(ahead(c, 1 - c), mine[at])

    kept, other = small(collect, 2, half, "collect", (mine, partner, *got), done)
    return kept, shift(other, swap=True)


def state_of(h, kept, other):
    _, _, c = places()
    heads = kept.shape[0] // D
    at = slice(h % heads * D, (h % heads + 1) * D)
    return jnp.where(c == h // heads, kept[at], other[at])


def products(left, right):
    length, width = left.shape
    heads = width // D
    blocks = length // BLOCK
    per_core = heads // CORES

    def body(left_hbm, right_hbm, left, right, first, mine, theirs, sems):
        copies = []
        for c in range(blocks):
            rows = pl.ds(c * BLOCK, BLOCK)
            pair = [
                pltpu.make_async_copy(left_hbm.at[rows], left.at[rows], sems.at[0, c]),
                pltpu.make_async_copy(right_hbm.at[rows], right.at[rows], sems.at[1, c]),
            ]
            for copy in pair:
                copy.start()
            copies.append(pair)
        total = [None] * heads
        for c in range(blocks):
            for copy in copies[c]:
                copy.wait()
            for h in range(heads):
                term = dot_tn(left[block_rows(c), head_cols(h)], right[block_rows(c), head_cols(h)])
                if c == 0:
                    first[head_cols(h)] = term
                total[h] = term if c == 0 else total[h] + term
        _, _, core = places()
        for h in range(heads):
            store_half(core, h, per_core, total[h], mine, theirs)

    half_shape = jax.ShapeDtypeStruct((width // CORES, D), F32)
    return pl.pallas_call(
        body,
        in_specs=[HBM, HBM],
        out_specs=[VMEM] * 5,
        out_shape=[
            jax.ShapeDtypeStruct(left.shape, BF16),
            jax.ShapeDtypeStruct(right.shape, BF16),
            jax.ShapeDtypeStruct((width, D), F32),
            half_shape,
            half_shape,
        ],
        scratch_shapes=[pltpu.SemaphoreType.DMA((2, blocks))],
        compiler_params=params(12),
        name="products",
    )(pltpu.with_memory_space_constraint(left, pltpu.HBM), pltpu.with_memory_space_constraint(right, pltpu.HBM))


def store_half(core, h, per_core, value, mine, theirs):
    at = head_cols(h % per_core)

    @pl.when(core == h // per_core)
    def _():
        mine[at] = value

    @pl.when(core != h // per_core)
    def _():
        theirs[at] = value


def local_attention(q, k, v, h, after):
    length = q.shape[0]

    def body(q, k, v, _, out):
        for c in range(length // BLOCK):
            rows = block_rows(c)
            qv, kv, vv = (x[rows, head_cols(h)] for x in (q, k, v))
            a, b, d = lower_product(qv, kv)
            out[c * BLOCK : c * BLOCK + HALF] = dot_nn(a, vv[TOP])
            out[c * BLOCK + HALF : (c + 1) * BLOCK] = dot_nn(beside(b, d), vv)

    return pl.pallas_call(
        body,
        in_specs=[VMEM, VMEM, VMEM, ANY],
        out_specs=VMEM,
        out_shape=jax.ShapeDtypeStruct((length, D), F32),
        compiler_params=params(12),
        cost_estimate=pl.CostEstimate(
            flops=length // BLOCK * 4 * BLOCK * BLOCK * D, bytes_accessed=length * D * 10, transcendentals=0
        ),
        name="local_attention",
    )(q, k, v, after)


def attention_sums(q, grad, local, gain, kept, other, first):
    length, width = q.shape
    heads = width // D

    def body(q, grad, *refs):
        local, (gain, kept, other, first, attn, sums) = refs[:heads], refs[heads:]
        for c in range(length // BLOCK):
            rows = block_rows(c)
            square = jnp.zeros((BLOCK, D), F32)
            inner = jnp.zeros((BLOCK, D), F32)
            for h in range(heads):
                cols = head_cols(h)
                prefix = state_of(h, kept, other)
                if c > 0:
                    prefix += first[cols]
                a = local[h][rows] + dot_nn(q[rows, cols], prefix.astype(BF16))
                attn[rows, cols] = a
                square += a * a
                inner += a * (gain[:, cols] * grad[rows, cols].astype(F32))
            sums[0:1, rows] = jnp.sum(jnp.transpose(square), axis=0, keepdims=True)
            sums[1:2, rows] = jnp.sum(jnp.transpose(inner), axis=0, keepdims=True)

    return pl.pallas_call(
        body,
        in_specs=[VMEM] * (6 + heads),
        out_specs=[VMEM] * 2,
        out_shape=[
            jax.ShapeDtypeStruct((length, width), F32),
            jax.ShapeDtypeStruct((2, length), F32),
        ],
        compiler_params=params(16),
        name="attention_sums",
    )(q, grad, *local, gain, kept, other, first)


def gradient(q, grad, attn, gain, sums, features):
    length, width = q.shape
    heads = width // D
    blocks = length // BLOCK

    def body(q, grad, attn, gain, sums, out, last, mine, theirs):
        total = [None] * heads
        for c in range(blocks):
            rows = block_rows(c)
            root = jnp.sqrt(sums[0:1, rows] / features + 1e-05)
            inverse = per_token(1.0 / root)
            weight = per_token(sums[1:2, rows] / (features * root**3))
            for h in range(heads):
                cols = head_cols(h)
                scaled = gain[:, cols] * grad[rows, cols].astype(F32)
                g = (scaled * inverse - attn[rows, cols] * weight).astype(BF16)
                out[rows, cols] = g
                term = dot_tn(q[rows, cols], g)
                total[h] = term if c == 0 else total[h] + term
                if c == blocks - 1:
                    last[cols] = term
        _, _, core = places()
        for h in range(heads):
            store_half(core, h, heads // CORES, total[h], mine, theirs)

    half_shape = jax.ShapeDtypeStruct((width // CORES, D), F32)
    return pl.pallas_call(
        body,
        in_specs=[VMEM] * 5,
        out_specs=[VMEM] * 4,
        out_shape=[
            jax.ShapeDtypeStruct((length, width), BF16),
            jax.ShapeDtypeStruct((width, D), F32),
            half_shape,
            half_shape,
        ],
        compiler_params=params(16),
        name="gradient",
    )(q, grad, attn, gain, sums)


def local_gradients(q, k, v, g, attn, gain, sums, kept, other, first, features, h, outs, after):
    length, width = q.shape
    blocks = length // BLOCK
    cols = head_cols(h)

    def body(q, k, v, g, attn, gain, sums, kept, other, first, *refs):
        normed, dq, dk, dv, normed_here, dq_here, sems = refs[len(outs) + 1 :]
        copies = []

        def send(here, out, i, c):
            copy = pltpu.make_async_copy(here.at[block_rows(c)], out.at[block_rows(c), cols], sems.at[i, c])
            copy.start()
            copies.append(copy)

        state = state_of(h, kept, other)
        for c in range(blocks):
            rows = block_rows(c)
            root = jnp.sqrt(sums[0:1, rows] / features + 1e-05)
            normed_here[rows] = (gain[:, cols] * (attn[rows, cols] * per_token(1.0 / root))).astype(BF16)
            send(normed_here, normed, 0, c)
            qv, kv, vv, gv = (x[rows, cols] for x in (q, k, v, g))
            prefix = state + first[cols] if c > 0 else state
            carried = dot_nt(gv, prefix.astype(BF16))
            a, b, d = lower_product(gv, vv)
            top, bottom = slice(c * BLOCK, c * BLOCK + HALF), slice(c * BLOCK + HALF, (c + 1) * BLOCK)
            dq_here[top] = (dot_nn(a, kv[TOP]) + carried[TOP]).astype(BF16)
            dq_here[bottom] = (dot_nn(beside(b, d), kv) + carried[BOTTOM]).astype(BF16)
            send(dq_here, dq, 1, c)
            a, b, d = upper_product(vv, gv)
            dk[top] = dot_nn(beside(a, b), qv)
            dk[bottom] = dot_nn(d, qv[BOTTOM])
            a, b, d = upper_product(kv, qv)
            dv[top] = dot_nn(beside(a, b), gv)
            dv[bottom] = dot_nn(d, gv[BOTTOM])
        for copy in copies:
            copy.wait()

    return pl.pallas_call(
        body,
        in_specs=[VMEM] * 10 + [HBM] * len(outs) + [ANY],
        out_specs=[HBM, HBM, VMEM, VMEM],
        out_shape=[jax.ShapeDtypeStruct((length, width), BF16)] * 2 + [jax.ShapeDtypeStruct((length, D), F32)] * 2,
        scratch_shapes=[pltpu.VMEM((length, D), BF16)] * 2 + [pltpu.SemaphoreType.DMA((2, blocks))],
        input_output_aliases={10 + i: i for i in range(len(outs))},
        compiler_params=params(20),
        cost_estimate=pl.CostEstimate(
            flops=blocks * 12 * BLOCK * BLOCK * D, bytes_accessed=length * D * 20, transcendentals=0
        ),
        name="local_gradients",
    )(q, k, v, g, attn, gain, sums, kept, other, first, *outs, after)


def add_suffix(k, v, dk, dv, kept, other, last):
    length, width = k.shape
    heads = width // D
    steps = length // HALF

    def body(k, v, *refs):
        dk, dv = refs[:heads], refs[heads : 2 * heads]
        kept, other, last, out_k, out_v, here_k, here_v, sems = refs[2 * heads :]
        copies = []
        for i in range(steps):
            rows = slice(i * HALF, (i + 1) * HALF)
            for h in range(heads):
                cols = head_cols(h)
                suffix = state_of(h, kept, other)
                if (i + 1) * HALF <= length - BLOCK:
                    suffix += last[cols]
                suffix = suffix.astype(BF16)
                here_k[rows, cols] = (dk[h][rows] + dot_nt(v[rows, cols], suffix)).astype(BF16)
                here_v[rows, cols] = (dv[h][rows] + dot_nn(k[rows, cols], suffix)).astype(BF16)
            for here, out, j in ((here_k, out_k, 0), (here_v, out_v, 1)):
                copy = pltpu.make_async_copy(here.at[rows], out.at[rows], sems.at[j, i])
                copy.start()
                copies.append(copy)
        for copy in copies:
            copy.wait()

    shape = jax.ShapeDtypeStruct((length, width), BF16)
    return pl.pallas_call(
        body,
        in_specs=[VMEM] * (5 + 2 * heads),
        out_specs=[HBM, HBM],
        out_shape=[shape, shape],
        scratch_shapes=[pltpu.VMEM((length, width), BF16)] * 2 + [pltpu.SemaphoreType.DMA((2, steps))],
        compiler_params=params(16),
        name="add_suffix",
    )(k, v, *dk, *dv, kept, other, last)


def head_sum(part):
    count = lax.axis_size("head")
    total = part
    for k in range(1, count):
        total = total + lax.ppermute(part, "head", [(i, (i + k) % count) for i in range(count)])
    return total


def on_device(queries, token_keys, values, norm_gain, out_grad):
    heads = queries.shape[1] // D
    features = lax.axis_size("head") * heads * D
    gain = norm_gain.reshape(1, heads * D)
    keys, vals, first, mine, theirs = products(token_keys, values)
    local = []

    def attend(h):
        def run(after):
            local.append(local_attention(queries, keys, vals, h, after))
            return local[-1:]

        return run

    kept, other = entering(mine, theirs, False, [attend(h) for h in range(heads)])
    attn, sums = attention_sums(queries, out_grad, local, gain, kept, other, first)
    sums = head_sum(sums)
    grad_attn, last, mine, theirs = gradient(queries, out_grad, attn, gain, sums, features)
    outs, key_parts, value_parts = [], [], []

    def differentiate(h):
        def run(after):
            normed, query, key, value = local_gradients(
                queries, keys, vals, grad_attn, attn, gain, sums, kept, other, first, features, h, tuple(outs), after
            )
            outs[:] = [normed, query]
            key_parts.append(key)
            value_parts.append(value)
            return [value]

        return run

    kept_later, other_later = entering(mine, theirs, True, [differentiate(h) for h in range(heads)])
    grad_key, grad_value = add_suffix(keys, vals, key_parts, value_parts, kept_later, other_later, last)
    normed_out, grad_query = outs
    return normed_out, grad_query, grad_key, grad_value


def solution(mesh):
    placed = (P("seq", "head"), P("seq", "head"), P("seq", "head"), P("head"), P("seq", "head"))
    return jax.shard_map(
        on_device,
        mesh=mesh,
        in_specs=placed,
        out_specs=(P("seq", "head"), P("seq", "head"), P("seq", "head"), P("seq", "head")),
        check_vma=False,
    )
```

time: 104 us -> 86.9 us (0.84); the launches traced: 102 us -> 86.8 us
  waiting for transfers between devices: 24.4 us -> 17.7 us
  Pallas kernels: 22.5 us -> 18.2 us
  local copies, waits for them, and re-layouts: 2.47 us -> 0.01 us
  starting transfers between devices: 51.9 us -> 49.9 us
    ppermute x24, waiting for transfers between devices: 21.3 us -> 14.6 us  [shift(): return lax.ppermute(value, 'seq', pairs)]
    pallas_call x16 -> x22, Pallas kernels: 22.5 us -> 18.2 us  [the longest x4 9.45 us: local_gradients(): pl.pallas_call(body, in_specs=[VMEM] * 10 + [HBM] * len(outs) + [ANY], ou...]
    unnamed x14 -> x6, local copies, waits for them, and re-layouts: 2.47 us -> 0.01 us
    ppermute x24, starting transfers between devices: 48.1 us -> 46 us  [shift(): return lax.ppermute(value, 'seq', pairs)]
  transfers between devices with their start and end apart: 27 -> 27, of which waited for: 23 -> 18; matrix products, arithmetic and copies ran while one was open for 0% -> 0% of each run, Pallas kernels for 14% -> 14%
where the time goes in v2:
time: 86.9 us; the launch traced here: 86.8 us
  starting transfers between devices  49.9 us (57%)
  Pallas kernels  18.2 us (21%)
  waiting for transfers between devices  17.7 us (20%)
  between operations  1.05 us (1%)
    ppermute x24, starting transfers between devices, shift(): return lax.ppermute(value, 'seq', pairs)  46 us
    ppermute x24, waiting for transfers between devices, shift(): return lax.ppermute(value, 'seq', pairs)  14.6 us
    pallas_call x4, Pallas kernels, local_gradients(): pl.pallas_call(body, in_specs=[VMEM] * 10 + [HBM] * len(outs) + [ANY], ou...  9.45 us
    ppermute x3, starting transfers between devices, head_sum(): lax.ppermute(part, 'head', [(i, (i + k) % count) for i in range(count)])  3.84 us
    ppermute x3, waiting for transfers between devices, head_sum(): lax.ppermute(part, 'head', [(i, (i + k) % count) for i in range(count)])  3.05 us
    pallas_call x4, Pallas kernels, local_attention(): pl.pallas_call(body, in_specs=[VMEM, VMEM, VMEM, ANY], out_specs=VMEM, ou...  2.76 us
    pallas_call x1, Pallas kernels, products(): pl.pallas_call(body, in_specs=[HBM, HBM], out_specs=[VMEM] * 5, out_shape...  2.05 us
  transfers between devices with their start and end apart: 27, of which 18 were waited for; matrix products, arithmetic and copies ran while one was open for 0% of the time, Pallas kernels for 14%

profile of v2, /device:TPU:1, one launch (start us, length us, event | category | flops | bytes accessed | tf_op | source)
XLA Modules:
  0.0 86.8 jit_solution(16685811687076073639)
XLA Ops:
  0.6 2.1 %products.1 = (bf16[1024,512]{1,0:T(8,128)(2,1)S(1)}, bf16[1024,512]{1,0:T(8,128)(2,1)S(1)}, f32[512,128]{1,0:T(8,128)S(1)}, f32[256,128]{1,0:T(8,128)S(1)}, f32[256,128]{1,0:T(8,128)S(1)}) custom-call(bf16[1024,512]{1,0:T(8,128)(2,1)} %left_hbm.1, bf16[1024,512]{1,0:T(8,128)(2,1)} %right_hbm.1), custom_call_target="tpu_custom_call" | custom-call | tf_op jit(solution)/shard_map/products/pallas_call | solution.py:218
  2.7 3.3 %collective-permute-start = (f32[256,128]{1,0:T(8,128)S(1)}, f32[256,128]{1,0:T(8,128)S(1)}, u32[]{:S(2)}, u32[]{:S(2)}) collective-permute-start(f32[256,128]{1,0:T(8,128)S(1)} %get-tuple-element.60), channel_id=1, source_target_pairs={{0,4},{4,0},{8,12},{12,8},{16,20},{20,16},{24,28},{28,24},{32,36},... | collective-permute-start | bytes 393224 | tf_op jit(solution)/shard_map/ppermute | solution.py:91
  7.1 1.9 %collective-permute-start.2 = (f32[64,128]{1,0:T(8,128)S(1)}, f32[64,128]{1,0:T(8,128)S(1)}, u32[]{:S(2)}, u32[]{:S(2)}) collective-permute-start(f32[64,128]{1,0:T(8,128)S(1)} %get-tuple-element.63), channel_id=1, source_target_pairs={{0,16},{4,20},{8,24},{12,28},{16,0},{20,4},{24,8},{28,12},{32,48},... | collective-permute-start | bytes 98312 | tf_op jit(solution)/shard_map/ppermute | solution.py:91
  12.3 5.4 %collective-permute-start.5 = (f32[64,128]{1,0:T(8,128)S(1)}, f32[64,128]{1,0:T(8,128)S(1)}, u32[]{:S(2)}, u32[]{:S(2)}) collective-permute-start(f32[64,128]{1,0:T(8,128)S(1)} %add.17._.refs_0_), channel_id=1, source_target_pairs={{0,224},{4,228},{8,232},{12,236},{16,240},{20,244},{24,248},{28,25... | collective-permute-start | bytes 98312 | tf_op jit(solution)/shard_map/ppermute | solution.py:91
  18.8 3.0 %collective-permute-done.4.refs_1_.refs_0_ = f32[64,128]{1,0:T(8,128)S(1)} collective-permute-done((f32[64,128]{1,0:T(8,128)S(1)}, f32[64,128]{1,0:T(8,128)S(1)}, u32[]{:S(2)}, u32[]{:S(2)}) %collective-permute-start.4) | collective-permute-done | bytes 32800 | tf_op jit(solution)/shard_map/ppermute | solution.py:91
  22.2 2.9 %collective-permute-start.6 = (f32[64,128]{1,0:T(8,128)S(1)}, f32[64,128]{1,0:T(8,128)S(1)}, u32[]{:S(2)}, u32[]{:S(2)}) collective-permute-start(f32[64,128]{1,0:T(8,128)S(1)} %get-tuple-element.65._), channel_id=1, source_target_pairs={{0,96},{4,100},{8,104},{12,108},{16,112},{20,116},{24,120},{28,124... | collective-permute-start | bytes 98312 | tf_op jit(solution)/shard_map/ppermute | solution.py:91
  26.4 1.9 %collective-permute-done.6.refs_2_ = f32[64,128]{1,0:T(8,128)S(1)} collective-permute-done((f32[64,128]{1,0:T(8,128)S(1)}, f32[64,128]{1,0:T(8,128)S(1)}, u32[]{:S(2)}, u32[]{:S(2)}) %collective-permute-start.6) | collective-permute-done | bytes 32800 | tf_op jit(solution)/shard_map/ppermute | solution.py:91
  28.4 3.2 %collective-permute-start.9 = (f32[64,128]{1,0:T(8,128)S(1)}, f32[64,128]{1,0:T(8,128)S(1)}, u32[]{:S(2)}, u32[]{:S(2)}) collective-permute-start(f32[64,128]{1,0:T(8,128)S(1)} %get-tuple-element.69), channel_id=1, source_target_pairs={{0,16},{4,20},{8,24},{12,28},{16,0},{20,4},{24,8},{28,12},{32,48},... | collective-permute-start | bytes 98312 | tf_op jit(solution)/shard_map/ppermute | solution.py:91
  34.5 7.1 %collective-permute-start.11 = (f32[256,128]{1,0:T(8,128)S(1)}, f32[256,128]{1,0:T(8,128)S(1)}, u32[]{:S(2)}, u32[]{:S(2)}) collective-permute-start(f32[256,128]{1,0:T(8,128)S(1)} %get-tuple-element.72), channel_id=1, source_target_pairs={{0,4},{4,0},{8,12},{12,8},{16,20},{20,16},{24,28},{28,24},{32,36},... | collective-permute-start | bytes 393224 | tf_op jit(solution)/shard_map/ppermute | solution.py:91
  43.5 2.8 %collective-permute-start.14 = (f32[2,1024]{1,0:T(2,128)S(1)}, f32[2,1024]{1,0:T(2,128)S(1)}, u32[]{:S(2)}, u32[]{:S(2)}) collective-permute-start(f32[2,1024]{1,0:T(2,128)S(1)} %get-tuple-element.75), channel_id=1, source_target_pairs={{0,3},{1,0},{2,1},{3,2},{4,7},{5,4},{6,5},{7,6},{8,11},{9,8},{10,9... | collective-permute-start | bytes 24584 | tf_op jit(solution)/shard_map/ppermute | solution.py:441
  47.4 3.0 %collective-permute-done.13 = f32[2,1024]{1,0:T(2,128)S(1)} collective-permute-done((f32[2,1024]{1,0:T(2,128)S(1)}, f32[2,1024]{1,0:T(2,128)S(1)}, u32[]{:S(2)}, u32[]{:S(2)}) %collective-permute-start.13) | collective-permute-done | bytes 8224 | tf_op jit(solution)/shard_map/ppermute | solution.py:441
  51.5 2.1 %collective-permute-start.15 = (f32[256,128]{1,0:T(8,128)S(1)}, f32[256,128]{1,0:T(8,128)S(1)}, u32[]{:S(2)}, u32[]{:S(2)}) collective-permute-start(f32[256,128]{1,0:T(8,128)S(1)} %get-tuple-element.78), channel_id=1, source_target_pairs={{0,4},{4,0},{8,12},{12,8},{16,20},{20,16},{24,28},{28,24},{32,36},... | collective-permute-start | bytes 393224 | tf_op jit(solution)/shard_map/ppermute | solution.py:91
  54.7 2.1 %collective-permute-start.17 = (f32[64,128]{1,0:T(8,128)S(1)}, f32[64,128]{1,0:T(8,128)S(1)}, u32[]{:S(2)}, u32[]{:S(2)}) collective-permute-start(f32[64,128]{1,0:T(8,128)S(1)} %get-tuple-element.83), channel_id=1, source_target_pairs={{0,16},{4,20},{8,24},{12,28},{16,0},{20,4},{24,8},{28,12},{32,48},... | collective-permute-start | bytes 98312 | tf_op jit(solution)/shard_map/ppermute | solution.py:91
  56.8 1.2 %collective-permute-start.18 = (f32[64,128]{1,0:T(8,128)S(1)}, f32[64,128]{1,0:T(8,128)S(1)}, u32[]{:S(2)}, u32[]{:S(2)}) collective-permute-start(f32[64,128]{1,0:T(8,128)S(1)} %get-tuple-element.84), channel_id=1, source_target_pairs={{0,24},{4,28},{8,0},{12,4},{16,8},{20,12},{24,16},{28,20},{32,56},... | collective-permute-start | bytes 98312 | tf_op jit(solution)/shard_map/ppermute | solution.py:91
  58.0 2.4 %local_gradients.4 = (bf16[1024,512]{1,0:T(8,128)(2,1)}, bf16[1024,512]{1,0:T(8,128)(2,1)}, f32[1024,128]{1,0:T(8,128)S(1)}, f32[1024,128]{1,0:T(8,128)S(1)}) custom-call(bf16[1024,512]{1,0:T(8,128)(2,1)S(1)} %copy-done, bf16[1024,512]{1,0:T(8,128)(2,1)S(1)} %get-tuple-element.57.k, bf16[1024,512]{1,0:T(8,128)(2,1)S(1)} %get-tuple-element.58.v, ...), custom_call_target="tpu_custom_call" | custom-call | flops 805306368 | bytes 2621440 | tf_op jit(solution)/shard_map/local_gradients/pallas_call | solution.py:384
  60.7 1.3 %collective-permute-start.19 = (f32[64,128]{1,0:T(8,128)S(1)}, f32[64,128]{1,0:T(8,128)S(1)}, u32[]{:S(2)}, u32[]{:S(2)}) collective-permute-start(f32[64,128]{1,0:T(8,128)S(1)} %add.18.refs_2_.refs_0_), channel_id=1, source_target_pairs={{0,32},{4,36},{8,40},{12,44},{16,48},{20,52},{24,56},{28,60},{32,6... | collective-permute-start | bytes 98312 | tf_op jit(solution)/shard_map/ppermute | solution.py:91
  62.0 2.4 %local_gradients.5 = (bf16[1024,512]{1,0:T(8,128)(2,1)}, bf16[1024,512]{1,0:T(8,128)(2,1)}, f32[1024,128]{1,0:T(8,128)S(1)}, f32[1024,128]{1,0:T(8,128)S(1)}) custom-call(bf16[1024,512]{1,0:T(8,128)(2,1)S(1)} %copy-done, bf16[1024,512]{1,0:T(8,128)(2,1)S(1)} %get-tuple-element.57.k, ...), custom_call_target="tpu_custom_call", output_to_operand_aliasing={{0}: (10, {}), {1}: (11, {})} | custom-call | flops 805306368 | bytes 2621440 | tf_op jit(solution)/shard_map/local_gradients/pallas_call | solution.py:384
  64.6 1.3 %collective-permute-start.22 = (f32[64,128]{1,0:T(8,128)S(1)}, f32[64,128]{1,0:T(8,128)S(1)}, u32[]{:S(2)}, u32[]{:S(2)}) collective-permute-start(f32[64,128]{1,0:T(8,128)S(1)} %get-tuple-element.92), channel_id=1, source_target_pairs={{0,160},{4,164},{8,168},{12,172},{16,176},{20,180},{24,184},{28,18... | collective-permute-start | bytes 98312 | tf_op jit(solution)/shard_map/ppermute | solution.py:91
  66.0 2.2 %collective-permute-start.21 = (f32[64,128]{1,0:T(8,128)S(1)}, f32[64,128]{1,0:T(8,128)S(1)}, u32[]{:S(2)}, u32[]{:S(2)}) collective-permute-start(f32[64,128]{1,0:T(8,128)S(1)} %get-tuple-element.89.refs_2_), channel_id=1, source_target_pairs={{0,96},{4,100},{8,104},{12,108},{16,112},{20,116},{24,120},{28,124... | collective-permute-start | bytes 98312 | tf_op jit(solution)/shard_map/ppermute | solution.py:91
  68.2 2.4 %local_gradients.6 = (bf16[1024,512]{1,0:T(8,128)(2,1)}, bf16[1024,512]{1,0:T(8,128)(2,1)}, f32[1024,128]{1,0:T(8,128)S(1)}, f32[1024,128]{1,0:T(8,128)S(1)}) custom-call(bf16[1024,512]{1,0:T(8,128)(2,1)S(1)} %copy-done, bf16[1024,512]{1,0:T(8,128)(2,1)S(1)} %get-tuple-element.57.k, ...), custom_call_target="tpu_custom_call", output_to_operand_aliasing={{0}: (10, {}), {1}: (11, {})} | custom-call | flops 805306368 | bytes 2621440 | tf_op jit(solution)/shard_map/local_gradients/pallas_call | solution.py:384
  72.5 2.2 %collective-permute-start.24 = (f32[64,128]{1,0:T(8,128)S(1)}, f32[64,128]{1,0:T(8,128)S(1)}, u32[]{:S(2)}, u32[]{:S(2)}) collective-permute-start(f32[64,128]{1,0:T(8,128)S(1)} %get-tuple-element.103), channel_id=1, source_target_pairs={{0,16},{4,20},{8,24},{12,28},{16,0},{20,4},{24,8},{28,12},{32,48},... | collective-permute-start | bytes 98312 | tf_op jit(solution)/shard_map/ppermute | solution.py:91
  75.7 2.4 %local_gradients.7 = (bf16[1024,512]{1,0:T(8,128)(2,1)}, bf16[1024,512]{1,0:T(8,128)(2,1)}, f32[1024,128]{1,0:T(8,128)S(1)}, f32[1024,128]{1,0:T(8,128)S(1)}) custom-call(bf16[1024,512]{1,0:T(8,128)(2,1)S(1)} %copy-done, bf16[1024,512]{1,0:T(8,128)(2,1)S(1)} %get-tuple-element.57.k, ...), custom_call_target="tpu_custom_call", output_to_operand_aliasing={{0}: (10, {}), {1}: (11, {})} | custom-call | flops 805306368 | bytes 2621440 | tf_op jit(solution)/shard_map/local_gradients/pallas_call | solution.py:384
  78.2 5.8 %collective-permute-start.26 = (f32[256,128]{1,0:T(8,128)S(1)}, f32[256,128]{1,0:T(8,128)S(1)}, u32[]{:S(2)}, u32[]{:S(2)}) collective-permute-start(f32[256,128]{1,0:T(8,128)S(1)} %get-tuple-element.106), channel_id=1, source_target_pairs={{0,4},{4,0},{8,12},{12,8},{16,20},{20,16},{24,28},{28,24},{32,36},... | collective-permute-start | bytes 393224 | tf_op jit(solution)/shard_map/ppermute | solution.py:91
  84.9 1.7 %add_suffix.1 = (bf16[1024,512]{1,0:T(8,128)(2,1)}, bf16[1024,512]{1,0:T(8,128)(2,1)}) custom-call(bf16[1024,512]{1,0:T(8,128)(2,1)S(1)} %get-tuple-element.57.k, bf16[1024,512]{1,0:T(8,128)(2,1)S(1)} %get-tuple-element.58.v, f32[1024,128]{1,0:T(8,128)S(1)} %get-tuple-element.97.refs_0_, f32[1024,128]{1,0:T(8,128)S(1)} %get-tuple-element.98.refs_1_, ...), custom_call_target="tpu_custom_call" | custom-call | tf_op jit(solution)/shard_map/add_suffix/pallas_call | solution.py:426
  (59 shorter events, 19.8 us)
Async XLA Ops:
  2.7 4.3 %collective-permute-start = (f32[256,128]{1,0:T(8,128)S(1)}, f32[256,128]{1,0:T(8,128)S(1)}, u32[]{:S(2)}, u32[]{:S(2)}) collective-permute-start(f32[256,128]{1,0:T(8,128)S(1)} %get-tuple-element.60), channel_id=1, source_target_pairs={{0,4},{4,0},{8,12},{12,8},{16,20},{20,16},{24,28},{28,24},{32,36},... | collective-permute-start | bytes 393224 | tf_op jit(solution)/shard_map/ppermute | solution.py:91
  7.0 4.1 %collective-permute-start.1 = (f32[64,128]{1,0:T(8,128)S(1)}, f32[64,128]{1,0:T(8,128)S(1)}, u32[]{:S(2)}, u32[]{:S(2)}) collective-permute-start(f32[64,128]{1,0:T(8,128)S(1)} %get-tuple-element.62), channel_id=1, source_target_pairs={{0,8},{4,12},{8,16},{12,20},{16,24},{20,28},{24,0},{28,4},{32,40},... | collective-permute-start | bytes 98312 | tf_op jit(solution)/shard_map/ppermute | solution.py:91
  7.1 4.4 %collective-permute-start.2 = (f32[64,128]{1,0:T(8,128)S(1)}, f32[64,128]{1,0:T(8,128)S(1)}, u32[]{:S(2)}, u32[]{:S(2)}) collective-permute-start(f32[64,128]{1,0:T(8,128)S(1)} %get-tuple-element.63), channel_id=1, source_target_pairs={{0,16},{4,20},{8,24},{12,28},{16,0},{20,4},{24,8},{28,12},{32,48},... | collective-permute-start | bytes 98312 | tf_op jit(solution)/shard_map/ppermute | solution.py:91
  12.3 6.5 %collective-permute-start.5 = (f32[64,128]{1,0:T(8,128)S(1)}, f32[64,128]{1,0:T(8,128)S(1)}, u32[]{:S(2)}, u32[]{:S(2)}) collective-permute-start(f32[64,128]{1,0:T(8,128)S(1)} %add.17._.refs_0_), channel_id=1, source_target_pairs={{0,224},{4,228},{8,232},{12,236},{16,240},{20,244},{24,248},{28,25... | collective-permute-start | bytes 98312 | tf_op jit(solution)/shard_map/ppermute | solution.py:91
  17.8 4.0 %collective-permute-start.4 = (f32[64,128]{1,0:T(8,128)S(1)}, f32[64,128]{1,0:T(8,128)S(1)}, u32[]{:S(2)}, u32[]{:S(2)}) collective-permute-start(f32[64,128]{1,0:T(8,128)S(1)} %add.17._.refs_0_), channel_id=1, source_target_pairs={{0,32},{4,36},{8,40},{12,44},{16,48},{20,52},{24,56},{28,60},{32,6... | collective-permute-start | bytes 98312 | tf_op jit(solution)/shard_map/ppermute | solution.py:91
  21.8 4.7 %collective-permute-start.7 = (f32[64,128]{1,0:T(8,128)S(1)}, f32[64,128]{1,0:T(8,128)S(1)}, u32[]{:S(2)}, u32[]{:S(2)}) collective-permute-start(f32[64,128]{1,0:T(8,128)S(1)} %get-tuple-element.66), channel_id=1, source_target_pairs={{0,160},{4,164},{8,168},{12,172},{16,176},{20,180},{24,184},{28,18... | collective-permute-start | bytes 98312 | tf_op jit(solution)/shard_map/ppermute | solution.py:91
  22.2 6.0 %collective-permute-start.6 = (f32[64,128]{1,0:T(8,128)S(1)}, f32[64,128]{1,0:T(8,128)S(1)}, u32[]{:S(2)}, u32[]{:S(2)}) collective-permute-start(f32[64,128]{1,0:T(8,128)S(1)} %get-tuple-element.65._), channel_id=1, source_target_pairs={{0,96},{4,100},{8,104},{12,108},{16,112},{20,116},{24,120},{28,124... | collective-permute-start | bytes 98312 | tf_op jit(solution)/shard_map/ppermute | solution.py:91
  28.3 4.3 %collective-permute-start.8 = (f32[64,128]{1,0:T(8,128)S(1)}, f32[64,128]{1,0:T(8,128)S(1)}, u32[]{:S(2)}, u32[]{:S(2)}) collective-permute-start(f32[64,128]{1,0:T(8,128)S(1)} %get-tuple-element.68), channel_id=1, source_target_pairs={{0,8},{4,12},{8,16},{12,20},{16,24},{20,28},{24,0},{28,4},{32,40},... | collective-permute-start | bytes 98312 | tf_op jit(solution)/shard_map/ppermute | solution.py:91
  28.4 4.9 %collective-permute-start.9 = (f32[64,128]{1,0:T(8,128)S(1)}, f32[64,128]{1,0:T(8,128)S(1)}, u32[]{:S(2)}, u32[]{:S(2)}) collective-permute-start(f32[64,128]{1,0:T(8,128)S(1)} %get-tuple-element.69), channel_id=1, source_target_pairs={{0,16},{4,20},{8,24},{12,28},{16,0},{20,4},{24,8},{28,12},{32,48},... | collective-permute-start | bytes 98312 | tf_op jit(solution)/shard_map/ppermute | solution.py:91
  34.5 8.1 %collective-permute-start.11 = (f32[256,128]{1,0:T(8,128)S(1)}, f32[256,128]{1,0:T(8,128)S(1)}, u32[]{:S(2)}, u32[]{:S(2)}) collective-permute-start(f32[256,128]{1,0:T(8,128)S(1)} %get-tuple-element.72), channel_id=1, source_target_pairs={{0,4},{4,0},{8,12},{12,8},{16,20},{20,16},{24,28},{28,24},{32,36},... | collective-permute-start | bytes 393224 | tf_op jit(solution)/shard_map/ppermute | solution.py:91
  43.5 3.8 %collective-permute-start.14 = (f32[2,1024]{1,0:T(2,128)S(1)}, f32[2,1024]{1,0:T(2,128)S(1)}, u32[]{:S(2)}, u32[]{:S(2)}) collective-permute-start(f32[2,1024]{1,0:T(2,128)S(1)} %get-tuple-element.75), channel_id=1, source_target_pairs={{0,3},{1,0},{2,1},{3,2},{4,7},{5,4},{6,5},{7,6},{8,11},{9,8},{10,9... | collective-permute-start | bytes 24584 | tf_op jit(solution)/shard_map/ppermute | solution.py:441
  46.3 4.0 %collective-permute-start.13 = (f32[2,1024]{1,0:T(2,128)S(1)}, f32[2,1024]{1,0:T(2,128)S(1)}, u32[]{:S(2)}, u32[]{:S(2)}) collective-permute-start(f32[2,1024]{1,0:T(2,128)S(1)} %get-tuple-element.75), channel_id=1, source_target_pairs={{0,2},{1,3},{2,0},{3,1},{4,6},{5,7},{6,4},{7,5},{8,10},{9,11},{10,... | collective-permute-start | bytes 24584 | tf_op jit(solution)/shard_map/ppermute | solution.py:441
  46.7 3.7 %collective-permute-start.12 = (f32[2,1024]{1,0:T(2,128)S(1)}, f32[2,1024]{1,0:T(2,128)S(1)}, u32[]{:S(2)}, u32[]{:S(2)}) collective-permute-start(f32[2,1024]{1,0:T(2,128)S(1)} %get-tuple-element.75), channel_id=1, source_target_pairs={{0,1},{1,2},{2,3},{3,0},{4,5},{5,6},{6,7},{7,4},{8,9},{9,10},{10,1... | collective-permute-start | bytes 24584 | tf_op jit(solution)/shard_map/ppermute | solution.py:441
  54.6 5.8 %collective-permute-start.16 = (f32[64,128]{1,0:T(8,128)S(1)}, f32[64,128]{1,0:T(8,128)S(1)}, u32[]{:S(2)}, u32[]{:S(2)}) collective-permute-start(f32[64,128]{1,0:T(8,128)S(1)} %get-tuple-element.82), channel_id=1, source_target_pairs={{0,8},{4,12},{8,16},{12,20},{16,24},{20,28},{24,0},{28,4},{32,40},... | collective-permute-start | bytes 98312 | tf_op jit(solution)/shard_map/ppermute | solution.py:91
  54.7 5.7 %collective-permute-start.17 = (f32[64,128]{1,0:T(8,128)S(1)}, f32[64,128]{1,0:T(8,128)S(1)}, u32[]{:S(2)}, u32[]{:S(2)}) collective-permute-start(f32[64,128]{1,0:T(8,128)S(1)} %get-tuple-element.83), channel_id=1, source_target_pairs={{0,16},{4,20},{8,24},{12,28},{16,0},{20,4},{24,8},{28,12},{32,48},... | collective-permute-start | bytes 98312 | tf_op jit(solution)/shard_map/ppermute | solution.py:91
  56.8 3.6 %collective-permute-start.18 = (f32[64,128]{1,0:T(8,128)S(1)}, f32[64,128]{1,0:T(8,128)S(1)}, u32[]{:S(2)}, u32[]{:S(2)}) collective-permute-start(f32[64,128]{1,0:T(8,128)S(1)} %get-tuple-element.84), channel_id=1, source_target_pairs={{0,24},{4,28},{8,0},{12,4},{16,8},{20,12},{24,16},{28,20},{32,56},... | collective-permute-start | bytes 98312 | tf_op jit(solution)/shard_map/ppermute | solution.py:91
  60.4 3.9 %collective-permute-start.20 = (f32[64,128]{1,0:T(8,128)S(1)}, f32[64,128]{1,0:T(8,128)S(1)}, u32[]{:S(2)}, u32[]{:S(2)}) collective-permute-start(f32[64,128]{1,0:T(8,128)S(1)} %add.18.refs_2_.refs_0_), channel_id=1, source_target_pairs={{0,224},{4,228},{8,232},{12,236},{16,240},{20,244},{24,248},{28,25... | collective-permute-start | bytes 98312 | tf_op jit(solution)/shard_map/ppermute | solution.py:91
  60.7 4.0 %collective-permute-start.19 = (f32[64,128]{1,0:T(8,128)S(1)}, f32[64,128]{1,0:T(8,128)S(1)}, u32[]{:S(2)}, u32[]{:S(2)}) collective-permute-start(f32[64,128]{1,0:T(8,128)S(1)} %add.18.refs_2_.refs_0_), channel_id=1, source_target_pairs={{0,32},{4,36},{8,40},{12,44},{16,48},{20,52},{24,56},{28,60},{32,6... | collective-permute-start | bytes 98312 | tf_op jit(solution)/shard_map/ppermute | solution.py:91
  64.6 5.9 %collective-permute-start.22 = (f32[64,128]{1,0:T(8,128)S(1)}, f32[64,128]{1,0:T(8,128)S(1)}, u32[]{:S(2)}, u32[]{:S(2)}) collective-permute-start(f32[64,128]{1,0:T(8,128)S(1)} %get-tuple-element.92), channel_id=1, source_target_pairs={{0,160},{4,164},{8,168},{12,172},{16,176},{20,180},{24,184},{28,18... | collective-permute-start | bytes 98312 | tf_op jit(solution)/shard_map/ppermute | solution.py:91
  66.0 5.8 %collective-permute-start.21 = (f32[64,128]{1,0:T(8,128)S(1)}, f32[64,128]{1,0:T(8,128)S(1)}, u32[]{:S(2)}, u32[]{:S(2)}) collective-permute-start(f32[64,128]{1,0:T(8,128)S(1)} %get-tuple-element.89.refs_2_), channel_id=1, source_target_pairs={{0,96},{4,100},{8,104},{12,108},{16,112},{20,116},{24,120},{28,124... | collective-permute-start | bytes 98312 | tf_op jit(solution)/shard_map/ppermute | solution.py:91
  71.8 6.3 %collective-permute-start.23 = (f32[64,128]{1,0:T(8,128)S(1)}, f32[64,128]{1,0:T(8,128)S(1)}, u32[]{:S(2)}, u32[]{:S(2)}) collective-permute-start(f32[64,128]{1,0:T(8,128)S(1)} %get-tuple-element.102), channel_id=1, source_target_pairs={{0,8},{4,12},{8,16},{12,20},{16,24},{20,28},{24,0},{28,4},{32,40},... | collective-permute-start | bytes 98312 | tf_op jit(solution)/shard_map/ppermute | solution.py:91
  72.5 5.6 %collective-permute-start.24 = (f32[64,128]{1,0:T(8,128)S(1)}, f32[64,128]{1,0:T(8,128)S(1)}, u32[]{:S(2)}, u32[]{:S(2)}) collective-permute-start(f32[64,128]{1,0:T(8,128)S(1)} %get-tuple-element.103), channel_id=1, source_target_pairs={{0,16},{4,20},{8,24},{12,28},{16,0},{20,4},{24,8},{28,12},{32,48},... | collective-permute-start | bytes 98312 | tf_op jit(solution)/shard_map/ppermute | solution.py:91
  74.7 3.4 %collective-permute-start.25 = (f32[64,128]{1,0:T(8,128)S(1)}, f32[64,128]{1,0:T(8,128)S(1)}, u32[]{:S(2)}, u32[]{:S(2)}) collective-permute-start(f32[64,128]{1,0:T(8,128)S(1)} %get-tuple-element.104), channel_id=1, source_target_pairs={{0,24},{4,28},{8,0},{12,4},{16,8},{20,12},{24,16},{28,20},{32,56},... | collective-permute-start | bytes 98312 | tf_op jit(solution)/shard_map/ppermute | solution.py:91
  78.2 6.7 %collective-permute-start.26 = (f32[256,128]{1,0:T(8,128)S(1)}, f32[256,128]{1,0:T(8,128)S(1)}, u32[]{:S(2)}, u32[]{:S(2)}) collective-permute-start(f32[256,128]{1,0:T(8,128)S(1)} %get-tuple-element.106), channel_id=1, source_target_pairs={{0,4},{4,0},{8,12},{12,8},{16,20},{20,16},{24,28},{28,24},{32,36},... | collective-permute-start | bytes 393224 | tf_op jit(solution)/shard_map/ppermute | solution.py:91
  (6 other events, 40.5 us)

commit v3 on v2

--- a/solution.py
+++ b/solution.py
@@ -80,13 +80,14 @@
     return me // (LINE * CORES), me // CORES % LINE, me % CORES
 
 
-def shift(value, plane=0, line=0, swap=False):
+def shift(value, plane=0, line=0, swap=False, pair=False):
     pairs = []
     for z in range(PLANES):
         for x in range(LINE):
             for c in range(CORES):
                 source = (z * LINE + x) * CORES + c
-                target = ((z + plane) % PLANES * LINE + (x + line) % LINE) * CORES + (1 - c if swap else c)
+                to = x ^ 1 if pair else (x + line) % LINE
+                target = ((z + plane) % PLANES * LINE + to) * CORES + (1 - c if swap else c)
                 pairs.append((source, target))
     return lax.ppermute(value, "seq", pairs)
 
@@ -114,18 +115,18 @@
         return other > me if reverse else other < me
 
     half = mine.shape[0]
-    piece = half // LINE
+    piece = half // 2
     partner = shift(theirs, swap=True)
 
-    def split(mine, partner, *outs):
+    def split(mine, partner, same, opposite):
         _, x, _ = places()
-        for k, out in enumerate(outs):
-            at = pl.ds(pl.multiple_of((x + k) % LINE * piece, piece), piece)
+        for out, at in ((same, x % 2), (opposite, 1 - x % 2)):
+            at = pl.ds(pl.multiple_of(at * piece, piece), piece)
             out[...] = mine[at] + partner[at]
 
-    parts = small(split, LINE, piece, "split", (mine, partner))
-    done = beside_rounds[0](parts[0])
-    parts = [parts[0]] + [shift(parts[k], line=k) for k in range(1, LINE)]
+    same, opposite = small(split, 2, piece, "split", (mine, partner))
+    done = beside_rounds[0](same)
+    parts = [same, shift(opposite, line=1), shift(same, line=2), shift(opposite, line=3)]
 
     def add(a, b, c, d, out):
         out[...] = a[...] + b[...] + c[...] + d[...]
@@ -137,15 +138,15 @@
     def windows(plane, below, above, to_up, to_down):
         z, _, _ = places()
         before, after = (z + PLANES - 1) % PLANES, (z + 1) % PLANES
-        up, down = (z + 3) % PLANES, (z + PLANES - 3) % PLANES
-        to_up[...] = (
-            when(ahead(before, up), below[...]) + when(ahead(z, up), plane[...]) + when(ahead(after, up), above[...])
+        up, down = (z + 2) % PLANES, (z + PLANES - 3) % PLANES
+        to_up[...] = when(ahead(before, up), below[...]) + when(ahead(z, up), plane[...])
+        to_down[...] = (
+            when(ahead(before, down), below[...]) + when(ahead(z, down), plane[...]) + when(ahead(after, down), above[...])
         )
-        to_down[...] = when(ahead(before, down), below[...]) + when(ahead(z, down), plane[...])
 
     to_up, to_down = small(windows, 2, piece, "windows", (plane, below, above), done)
     done = beside_rounds[2](to_up)
-    from_down, from_up = shift(to_up, plane=3), shift(to_down, plane=-3)
+    from_down, from_up = shift(to_up, plane=2), shift(to_down, plane=-3)
 
     def spread(below, above, from_down, from_up, *refs):
         parts, outs = refs[:LINE], refs[LINE:]
@@ -154,26 +155,24 @@
         planes = (
             when(ahead(before, z), below[...]) + when(ahead(after, z), above[...]) + from_down[...] + from_up[...]
         )
-        for j, out in enumerate(outs):
-            target = (x + j) % LINE
+        for target, out in zip((x, x + 1 - x % 2 * 2), outs):
             total = planes
             for k, part in enumerate(parts):
                 total += when(ahead((x + LINE - k) % LINE, target), part[...])
             out[...] = total
 
-    sent = small(spread, LINE, piece, "spread", (below, above, from_down, from_up, *parts), done)
-    done = beside_rounds[3](sent[0])
-    got = [sent[0]] + [shift(sent[j], line=j) for j in range(1, LINE)]
-
-    def collect(mine, partner, *refs):
-        got, (kept, other) = refs[:LINE], refs[LINE:]
+    own, sent = small(spread, 2, piece, "spread", (below, above, from_down, from_up, *parts), done)
+    done = beside_rounds[3](sent)
+    got = shift(sent, pair=True)
+
+    def collect(mine, partner, own, got, kept, other):
         _, x, c = places()
-        for k, part in enumerate(got):
-            at = pl.ds(pl.multiple_of((x + LINE - k) % LINE * piece, piece), piece)
+        for at, part in ((x % 2, own), (1 - x % 2, got)):
+            at = pl.ds(pl.multiple_of(at * piece, piece), piece)
             kept[at] = part[...] + when(ahead(1 - c, c), partner[at])
             other[at] = part[...] + when(ahead(c, 1 - c), mine[at])
 
-    kept, other = small(collect, 2, half, "collect", (mine, partner, *got), done)
+    kept, other = small(collect, 2, half, "collect", (mine, partner, own, got), done)
     return kept, shift(other, swap=True)
 
 

time: 86.9 us -> 82.4 us (0.948)
  starting transfers between devices: 49.9 us -> 37.5 us
  waiting for transfers between devices: 17.7 us -> 25.5 us
    ppermute x24 -> x20, starting transfers between devices: 46 us -> 33.7 us  [shift(): return lax.ppermute(value, 'seq', pairs)]
    ppermute x24 -> x20, waiting for transfers between devices: 14.6 us -> 22.3 us  [shift(): return lax.ppermute(value, 'seq', pairs)]
  transfers between devices with their start and end apart: 27 -> 23, of which waited for: 18 -> 17; matrix products, arithmetic and copies ran while one was open for 0% -> 0% of each run, Pallas kernels for 14% -> 15%
where the time goes in v3:
time: 82.4 us; the launch traced here: 82.3 us
  starting transfers between devices  37.5 us (46%)
  waiting for transfers between devices  25.5 us (31%)
  Pallas kernels  18.2 us (22%)
  between operations  1.02 us (1%)
    ppermute x20, starting transfers between devices, shift(): return lax.ppermute(value, 'seq', pairs)  33.7 us
    ppermute x20, waiting for transfers between devices, shift(): return lax.ppermute(value, 'seq', pairs)  22.3 us
    pallas_call x4, Pallas kernels, local_gradients(): pl.pallas_call(body, in_specs=[VMEM] * 10 + [HBM] * len(outs) + [ANY], ou...  9.46 us
    ppermute x3, starting transfers between devices, head_sum(): lax.ppermute(part, 'head', [(i, (i + k) % count) for i in range(count)])  3.86 us
    ppermute x3, waiting for transfers between devices, head_sum(): lax.ppermute(part, 'head', [(i, (i + k) % count) for i in range(count)])  3.13 us
    pallas_call x4, Pallas kernels, local_attention(): pl.pallas_call(body, in_specs=[VMEM, VMEM, VMEM, ANY], out_specs=VMEM, ou...  2.75 us
    pallas_call x1, Pallas kernels, products(): pl.pallas_call(body, in_specs=[HBM, HBM], out_specs=[VMEM] * 5, out_shape...  2.05 us
    pallas_call x1, Pallas kernels, add_suffix(): pl.pallas_call(body, in_specs=[VMEM] * (5 + 2 * heads), out_specs=[HBM, H...  1.68 us
  transfers between devices with their start and end apart: 23, of which 17 were waited for; matrix products, arithmetic and copies ran while one was open for 0% of the time, Pallas kernels for 15%

profile of v3, /device:TPU:1, one launch (start us, length us, event | category | flops | bytes accessed | tf_op | source)
XLA Modules:
  0.0 82.3 jit_solution(8671015579973508753)
XLA Ops:
  0.6 2.1 %products.1 = (bf16[1024,512]{1,0:T(8,128)(2,1)S(1)}, bf16[1024,512]{1,0:T(8,128)(2,1)S(1)}, f32[512,128]{1,0:T(8,128)S(1)}, f32[256,128]{1,0:T(8,128)S(1)}, f32[256,128]{1,0:T(8,128)S(1)}) custom-call(bf16[1024,512]{1,0:T(8,128)(2,1)} %left_hbm.1, bf16[1024,512]{1,0:T(8,128)(2,1)} %right_hbm.1), custom_call_target="tpu_custom_call" | custom-call | tf_op jit(solution)/shard_map/products/pallas_call | solution.py:217
  2.7 3.3 %collective-permute-start = (f32[256,128]{1,0:T(8,128)S(1)}, f32[256,128]{1,0:T(8,128)S(1)}, u32[]{:S(2)}, u32[]{:S(2)}) collective-permute-start(f32[256,128]{1,0:T(8,128)S(1)} %get-tuple-element.52), channel_id=1, source_target_pairs={{0,4},{4,0},{8,12},{12,8},{16,20},{20,16},{24,28},{28,24},{32,36},... | collective-permute-start | bytes 393224 | tf_op jit(solution)/shard_map/ppermute | solution.py:92
  10.3 1.9 %collective-permute-done.1.refs_1_.refs_5_ = f32[128,128]{1,0:T(8,128)S(1)} collective-permute-done((f32[128,128]{1,0:T(8,128)S(1)}, f32[128,128]{1,0:T(8,128)S(1)}, u32[]{:S(2)}, u32[]{:S(2)}) %collective-permute-start.1) | collective-permute-done | bytes 65568 | tf_op jit(solution)/shard_map/ppermute | solution.py:92
  13.3 5.9 %collective-permute-start.5 = (f32[128,128]{1,0:T(8,128)S(1)}, f32[128,128]{1,0:T(8,128)S(1)}, u32[]{:S(2)}, u32[]{:S(2)}) collective-permute-start(f32[128,128]{1,0:T(8,128)S(1)} %add.17._.refs_0_), channel_id=1, source_target_pairs={{0,224},{4,228},{8,232},{12,236},{16,240},{20,244},{24,248},{28,25... | collective-permute-start | bytes 196616 | tf_op jit(solution)/shard_map/ppermute | solution.py:92
  20.5 3.0 %collective-permute-done.4.refs_1_.refs_0_ = f32[128,128]{1,0:T(8,128)S(1)} collective-permute-done((f32[128,128]{1,0:T(8,128)S(1)}, f32[128,128]{1,0:T(8,128)S(1)}, u32[]{:S(2)}, u32[]{:S(2)}) %collective-permute-start.4) | collective-permute-done | bytes 65568 | tf_op jit(solution)/shard_map/ppermute | solution.py:92
  24.0 1.7 %collective-permute-start.6 = (f32[128,128]{1,0:T(8,128)S(1)}, f32[128,128]{1,0:T(8,128)S(1)}, u32[]{:S(2)}, u32[]{:S(2)}) collective-permute-start(f32[128,128]{1,0:T(8,128)S(1)} %get-tuple-element.55._), channel_id=1, source_target_pairs={{0,64},{4,68},{8,72},{12,76},{16,80},{20,84},{24,88},{28,92},{32,9... | collective-permute-start | bytes 196616 | tf_op jit(solution)/shard_map/ppermute | solution.py:92
  26.4 2.1 %collective-permute-done.7.refs_3_ = f32[128,128]{1,0:T(8,128)S(1)} collective-permute-done((f32[128,128]{1,0:T(8,128)S(1)}, f32[128,128]{1,0:T(8,128)S(1)}, u32[]{:S(2)}, u32[]{:S(2)}) %collective-permute-start.7) | collective-permute-done | bytes 65568 | tf_op jit(solution)/shard_map/ppermute | solution.py:92
  28.5 1.4 %collective-permute-done.6.refs_2_ = f32[128,128]{1,0:T(8,128)S(1)} collective-permute-done((f32[128,128]{1,0:T(8,128)S(1)}, f32[128,128]{1,0:T(8,128)S(1)}, u32[]{:S(2)}, u32[]{:S(2)}) %collective-permute-start.6) | collective-permute-done | bytes 65568 | tf_op jit(solution)/shard_map/ppermute | solution.py:92
  30.8 2.7 %collective-permute-done.8.refs_3_ = f32[128,128]{1,0:T(8,128)S(1)} collective-permute-done((f32[128,128]{1,0:T(8,128)S(1)}, f32[128,128]{1,0:T(8,128)S(1)}, u32[]{:S(2)}, u32[]{:S(2)}) %collective-permute-start.8) | collective-permute-done | bytes 65568 | tf_op jit(solution)/shard_map/ppermute | solution.py:92
  33.5 5.0 %collective-permute-start.9 = (f32[256,128]{1,0:T(8,128)S(1)}, f32[256,128]{1,0:T(8,128)S(1)}, u32[]{:S(2)}, u32[]{:S(2)}) collective-permute-start(f32[256,128]{1,0:T(8,128)S(1)} %get-tuple-element.60), channel_id=1, source_target_pairs={{0,4},{4,0},{8,12},{12,8},{16,20},{20,16},{24,28},{28,24},{32,36},... | collective-permute-start | bytes 393224 | tf_op jit(solution)/shard_map/ppermute | solution.py:92
  40.5 2.8 %collective-permute-start.12 = (f32[2,1024]{1,0:T(2,128)S(1)}, f32[2,1024]{1,0:T(2,128)S(1)}, u32[]{:S(2)}, u32[]{:S(2)}) collective-permute-start(f32[2,1024]{1,0:T(2,128)S(1)} %get-tuple-element.63), channel_id=1, source_target_pairs={{0,3},{1,0},{2,1},{3,2},{4,7},{5,4},{6,5},{7,6},{8,11},{9,8},{10,9... | collective-permute-start | bytes 24584 | tf_op jit(solution)/shard_map/ppermute | solution.py:440
  44.3 3.0 %collective-permute-done.11 = f32[2,1024]{1,0:T(2,128)S(1)} collective-permute-done((f32[2,1024]{1,0:T(2,128)S(1)}, f32[2,1024]{1,0:T(2,128)S(1)}, u32[]{:S(2)}, u32[]{:S(2)}) %collective-permute-start.11) | collective-permute-done | bytes 8224 | tf_op jit(solution)/shard_map/ppermute | solution.py:440
  48.5 2.0 %collective-permute-start.13 = (f32[256,128]{1,0:T(8,128)S(1)}, f32[256,128]{1,0:T(8,128)S(1)}, u32[]{:S(2)}, u32[]{:S(2)}) collective-permute-start(f32[256,128]{1,0:T(8,128)S(1)} %get-tuple-element.66), channel_id=1, source_target_pairs={{0,4},{4,0},{8,12},{12,8},{16,20},{20,16},{24,28},{28,24},{32,36},... | collective-permute-start | bytes 393224 | tf_op jit(solution)/shard_map/ppermute | solution.py:92
  51.6 2.3 %collective-permute-start.16 = (f32[128,128]{1,0:T(8,128)S(1)}, f32[128,128]{1,0:T(8,128)S(1)}, u32[]{:S(2)}, u32[]{:S(2)}) collective-permute-start(f32[128,128]{1,0:T(8,128)S(1)} %get-tuple-element.70), channel_id=1, source_target_pairs={{0,24},{4,28},{8,0},{12,4},{16,8},{20,12},{24,16},{28,20},{32,56},... | collective-permute-start | bytes 196616 | tf_op jit(solution)/shard_map/ppermute | solution.py:92
  55.2 2.4 %local_gradients.4 = (bf16[1024,512]{1,0:T(8,128)(2,1)}, bf16[1024,512]{1,0:T(8,128)(2,1)}, f32[1024,128]{1,0:T(8,128)S(1)}, f32[1024,128]{1,0:T(8,128)S(1)}) custom-call(bf16[1024,512]{1,0:T(8,128)(2,1)S(1)} %copy-done, bf16[1024,512]{1,0:T(8,128)(2,1)S(1)} %get-tuple-element.49.k, bf16[1024,512]{1,0:T(8,128)(2,1)S(1)} %get-tuple-element.50.v, ...), custom_call_target="tpu_custom_call" | custom-call | flops 805306368 | bytes 2621440 | tf_op jit(solution)/shard_map/local_gradients/pallas_call | solution.py:383
  57.6 2.7 %collective-permute-done.14.refs_1_.refs_5_ = f32[128,128]{1,0:T(8,128)S(1)} collective-permute-done((f32[128,128]{1,0:T(8,128)S(1)}, f32[128,128]{1,0:T(8,128)S(1)}, u32[]{:S(2)}, u32[]{:S(2)}) %collective-permute-start.14) | collective-permute-done | bytes 65568 | tf_op jit(solution)/shard_map/ppermute | solution.py:92
  60.3 1.5 %collective-permute-start.17 = (f32[128,128]{1,0:T(8,128)S(1)}, f32[128,128]{1,0:T(8,128)S(1)}, u32[]{:S(2)}, u32[]{:S(2)}) collective-permute-start(f32[128,128]{1,0:T(8,128)S(1)} %add.18.refs_2_.refs_0_), channel_id=1, source_target_pairs={{0,32},{4,36},{8,40},{12,44},{16,48},{20,52},{24,56},{28,60},{32,6... | collective-permute-start | bytes 196616 | tf_op jit(solution)/shard_map/ppermute | solution.py:92
  61.8 2.4 %local_gradients.5 = (bf16[1024,512]{1,0:T(8,128)(2,1)}, bf16[1024,512]{1,0:T(8,128)(2,1)}, f32[1024,128]{1,0:T(8,128)S(1)}, f32[1024,128]{1,0:T(8,128)S(1)}) custom-call(bf16[1024,512]{1,0:T(8,128)(2,1)S(1)} %copy-done, bf16[1024,512]{1,0:T(8,128)(2,1)S(1)} %get-tuple-element.49.k, ...), custom_call_target="tpu_custom_call", output_to_operand_aliasing={{0}: (10, {}), {1}: (11, {})} | custom-call | flops 805306368 | bytes 2621440 | tf_op jit(solution)/shard_map/local_gradients/pallas_call | solution.py:383
  64.8 1.7 %collective-permute-start.20 = (f32[128,128]{1,0:T(8,128)S(1)}, f32[128,128]{1,0:T(8,128)S(1)}, u32[]{:S(2)}, u32[]{:S(2)}) collective-permute-start(f32[128,128]{1,0:T(8,128)S(1)} %get-tuple-element.78), channel_id=1, source_target_pairs={{0,160},{4,164},{8,168},{12,172},{16,176},{20,180},{24,184},{28,18... | collective-permute-start | bytes 196616 | tf_op jit(solution)/shard_map/ppermute | solution.py:92
  67.7 2.4 %local_gradients.6 = (bf16[1024,512]{1,0:T(8,128)(2,1)}, bf16[1024,512]{1,0:T(8,128)(2,1)}, f32[1024,128]{1,0:T(8,128)S(1)}, f32[1024,128]{1,0:T(8,128)S(1)}) custom-call(bf16[1024,512]{1,0:T(8,128)(2,1)S(1)} %copy-done, bf16[1024,512]{1,0:T(8,128)(2,1)S(1)} %get-tuple-element.49.k, ...), custom_call_target="tpu_custom_call", output_to_operand_aliasing={{0}: (10, {}), {1}: (11, {})} | custom-call | flops 805306368 | bytes 2621440 | tf_op jit(solution)/shard_map/local_gradients/pallas_call | solution.py:383
  70.1 1.6 %collective-permute-done.19.refs_2_ = f32[128,128]{1,0:T(8,128)S(1)} collective-permute-done((f32[128,128]{1,0:T(8,128)S(1)}, f32[128,128]{1,0:T(8,128)S(1)}, u32[]{:S(2)}, u32[]{:S(2)}) %collective-permute-start.19) | collective-permute-done | bytes 65568 | tf_op jit(solution)/shard_map/ppermute | solution.py:92
  71.8 2.4 %local_gradients.7 = (bf16[1024,512]{1,0:T(8,128)(2,1)}, bf16[1024,512]{1,0:T(8,128)(2,1)}, f32[1024,128]{1,0:T(8,128)S(1)}, f32[1024,128]{1,0:T(8,128)S(1)}) custom-call(bf16[1024,512]{1,0:T(8,128)(2,1)S(1)} %copy-done, bf16[1024,512]{1,0:T(8,128)(2,1)S(1)} %get-tuple-element.49.k, ...), custom_call_target="tpu_custom_call", output_to_operand_aliasing={{0}: (10, {}), {1}: (11, {})} | custom-call | flops 805306368 | bytes 2621440 | tf_op jit(solution)/shard_map/local_gradients/pallas_call | solution.py:383
  75.0 4.4 %collective-permute-start.22 = (f32[256,128]{1,0:T(8,128)S(1)}, f32[256,128]{1,0:T(8,128)S(1)}, u32[]{:S(2)}, u32[]{:S(2)}) collective-permute-start(f32[256,128]{1,0:T(8,128)S(1)} %get-tuple-element.90), channel_id=1, source_target_pairs={{0,4},{4,0},{8,12},{12,8},{16,20},{20,16},{24,28},{28,24},{32,36},... | collective-permute-start | bytes 393224 | tf_op jit(solution)/shard_map/ppermute | solution.py:92
  80.4 1.7 %add_suffix.1 = (bf16[1024,512]{1,0:T(8,128)(2,1)}, bf16[1024,512]{1,0:T(8,128)(2,1)}) custom-call(bf16[1024,512]{1,0:T(8,128)(2,1)S(1)} %get-tuple-element.49.k, bf16[1024,512]{1,0:T(8,128)(2,1)S(1)} %get-tuple-element.50.v, f32[1024,128]{1,0:T(8,128)S(1)} %get-tuple-element.83.refs_0_, f32[1024,128]{1,0:T(8,128)S(1)} %get-tuple-element.84.refs_1_, ...), custom_call_target="tpu_custom_call" | custom-call | tf_op jit(solution)/shard_map/add_suffix/pallas_call | solution.py:425
  (51 shorter events, 19.1 us)
Async XLA Ops:
  2.7 4.3 %collective-permute-start = (f32[256,128]{1,0:T(8,128)S(1)}, f32[256,128]{1,0:T(8,128)S(1)}, u32[]{:S(2)}, u32[]{:S(2)}) collective-permute-start(f32[256,128]{1,0:T(8,128)S(1)} %get-tuple-element.52), channel_id=1, source_target_pairs={{0,4},{4,0},{8,12},{12,8},{16,20},{20,16},{24,28},{28,24},{32,36},... | collective-permute-start | bytes 393224 | tf_op jit(solution)/shard_map/ppermute | solution.py:92
  7.0 3.3 %collective-permute-start.3 = (f32[128,128]{1,0:T(8,128)S(1)}, f32[128,128]{1,0:T(8,128)S(1)}, u32[]{:S(2)}, u32[]{:S(2)}) collective-permute-start(f32[128,128]{1,0:T(8,128)S(1)} %get-tuple-element.54), channel_id=1, source_target_pairs={{0,24},{4,28},{8,0},{12,4},{16,8},{20,12},{24,16},{28,20},{32,56},... | collective-permute-start | bytes 196616 | tf_op jit(solution)/shard_map/ppermute | solution.py:92
  7.9 4.3 %collective-permute-start.1 = (f32[128,128]{1,0:T(8,128)S(1)}, f32[128,128]{1,0:T(8,128)S(1)}, u32[]{:S(2)}, u32[]{:S(2)}) collective-permute-start(f32[128,128]{1,0:T(8,128)S(1)} %get-tuple-element.54), channel_id=1, source_target_pairs={{0,8},{4,12},{8,16},{12,20},{16,24},{20,28},{24,0},{28,4},{32,40},... | collective-permute-start | bytes 196616 | tf_op jit(solution)/shard_map/ppermute | solution.py:92
  8.6 4.7 %collective-permute-start.2 = (f32[128,128]{1,0:T(8,128)S(1)}, f32[128,128]{1,0:T(8,128)S(1)}, u32[]{:S(2)}, u32[]{:S(2)}) collective-permute-start(f32[128,128]{1,0:T(8,128)S(1)} %get-tuple-element.53._.refs_0_.refs_4_), channel_id=1, source_target_pairs={{0,16},{4,20},{8,24},{12,28},{16,0},{20,4},{24,8},{28,12},{32,48},... | collective-permute-start | bytes 196616 | tf_op jit(solution)/shard_map/ppermute | solution.py:92
  13.3 7.2 %collective-permute-start.5 = (f32[128,128]{1,0:T(8,128)S(1)}, f32[128,128]{1,0:T(8,128)S(1)}, u32[]{:S(2)}, u32[]{:S(2)}) collective-permute-start(f32[128,128]{1,0:T(8,128)S(1)} %add.17._.refs_0_), channel_id=1, source_target_pairs={{0,224},{4,228},{8,232},{12,236},{16,240},{20,244},{24,248},{28,25... | collective-permute-start | bytes 196616 | tf_op jit(solution)/shard_map/ppermute | solution.py:92
  19.1 4.3 %collective-permute-start.4 = (f32[128,128]{1,0:T(8,128)S(1)}, f32[128,128]{1,0:T(8,128)S(1)}, u32[]{:S(2)}, u32[]{:S(2)}) collective-permute-start(f32[128,128]{1,0:T(8,128)S(1)} %add.17._.refs_0_), channel_id=1, source_target_pairs={{0,32},{4,36},{8,40},{12,44},{16,48},{20,52},{24,56},{28,60},{32,6... | collective-permute-start | bytes 196616 | tf_op jit(solution)/shard_map/ppermute | solution.py:92
  23.5 5.0 %collective-permute-start.7 = (f32[128,128]{1,0:T(8,128)S(1)}, f32[128,128]{1,0:T(8,128)S(1)}, u32[]{:S(2)}, u32[]{:S(2)}) collective-permute-start(f32[128,128]{1,0:T(8,128)S(1)} %get-tuple-element.56), channel_id=1, source_target_pairs={{0,160},{4,164},{8,168},{12,172},{16,176},{20,180},{24,184},{28,18... | collective-permute-start | bytes 196616 | tf_op jit(solution)/shard_map/ppermute | solution.py:92
  24.0 5.9 %collective-permute-start.6 = (f32[128,128]{1,0:T(8,128)S(1)}, f32[128,128]{1,0:T(8,128)S(1)}, u32[]{:S(2)}, u32[]{:S(2)}) collective-permute-start(f32[128,128]{1,0:T(8,128)S(1)} %get-tuple-element.55._), channel_id=1, source_target_pairs={{0,64},{4,68},{8,72},{12,76},{16,80},{20,84},{24,88},{28,92},{32,9... | collective-permute-start | bytes 196616 | tf_op jit(solution)/shard_map/ppermute | solution.py:92
  30.0 9.6 %copy-start.1 = (bf16[1024,512]{1,0:T(8,128)(2,1)S(1)}, bf16[1024,512]{1,0:T(8,128)(2,1)}, u32[]{:S(2)}) copy-start(bf16[1024,512]{1,0:T(8,128)(2,1)} %grad.3) | copy-start | bytes 3145732
  30.0 3.5 %collective-permute-start.8 = (f32[128,128]{1,0:T(8,128)S(1)}, f32[128,128]{1,0:T(8,128)S(1)}, u32[]{:S(2)}, u32[]{:S(2)}) collective-permute-start(f32[128,128]{1,0:T(8,128)S(1)} %get-tuple-element.57._), channel_id=1, source_target_pairs={{0,8},{4,12},{8,0},{12,4},{16,24},{20,28},{24,16},{28,20},{32,40},... | collective-permute-start | bytes 196616 | tf_op jit(solution)/shard_map/ppermute | solution.py:92
  33.5 6.0 %collective-permute-start.9 = (f32[256,128]{1,0:T(8,128)S(1)}, f32[256,128]{1,0:T(8,128)S(1)}, u32[]{:S(2)}, u32[]{:S(2)}) collective-permute-start(f32[256,128]{1,0:T(8,128)S(1)} %get-tuple-element.60), channel_id=1, source_target_pairs={{0,4},{4,0},{8,12},{12,8},{16,20},{20,16},{24,28},{28,24},{32,36},... | collective-permute-start | bytes 393224 | tf_op jit(solution)/shard_map/ppermute | solution.py:92
  40.5 3.9 %collective-permute-start.12 = (f32[2,1024]{1,0:T(2,128)S(1)}, f32[2,1024]{1,0:T(2,128)S(1)}, u32[]{:S(2)}, u32[]{:S(2)}) collective-permute-start(f32[2,1024]{1,0:T(2,128)S(1)} %get-tuple-element.63), channel_id=1, source_target_pairs={{0,3},{1,0},{2,1},{3,2},{4,7},{5,4},{6,5},{7,6},{8,11},{9,8},{10,9... | collective-permute-start | bytes 24584 | tf_op jit(solution)/shard_map/ppermute | solution.py:440
  43.3 4.0 %collective-permute-start.11 = (f32[2,1024]{1,0:T(2,128)S(1)}, f32[2,1024]{1,0:T(2,128)S(1)}, u32[]{:S(2)}, u32[]{:S(2)}) collective-permute-start(f32[2,1024]{1,0:T(2,128)S(1)} %get-tuple-element.63), channel_id=1, source_target_pairs={{0,2},{1,3},{2,0},{3,1},{4,6},{5,7},{6,4},{7,5},{8,10},{9,11},{10,... | collective-permute-start | bytes 24584 | tf_op jit(solution)/shard_map/ppermute | solution.py:440
  43.7 3.7 %collective-permute-start.10 = (f32[2,1024]{1,0:T(2,128)S(1)}, f32[2,1024]{1,0:T(2,128)S(1)}, u32[]{:S(2)}, u32[]{:S(2)}) collective-permute-start(f32[2,1024]{1,0:T(2,128)S(1)} %get-tuple-element.63), channel_id=1, source_target_pairs={{0,1},{1,2},{2,3},{3,0},{4,5},{5,6},{6,7},{7,4},{8,9},{9,10},{10,1... | collective-permute-start | bytes 24584 | tf_op jit(solution)/shard_map/ppermute | solution.py:440
  48.5 3.0 %collective-permute-start.13 = (f32[256,128]{1,0:T(8,128)S(1)}, f32[256,128]{1,0:T(8,128)S(1)}, u32[]{:S(2)}, u32[]{:S(2)}) collective-permute-start(f32[256,128]{1,0:T(8,128)S(1)} %get-tuple-element.66), channel_id=1, source_target_pairs={{0,4},{4,0},{8,12},{12,8},{16,20},{20,16},{24,28},{28,24},{32,36},... | collective-permute-start | bytes 393224 | tf_op jit(solution)/shard_map/ppermute | solution.py:92
  51.6 6.0 %collective-permute-start.16 = (f32[128,128]{1,0:T(8,128)S(1)}, f32[128,128]{1,0:T(8,128)S(1)}, u32[]{:S(2)}, u32[]{:S(2)}) collective-permute-start(f32[128,128]{1,0:T(8,128)S(1)} %get-tuple-element.70), channel_id=1, source_target_pairs={{0,24},{4,28},{8,0},{12,4},{16,8},{20,12},{24,16},{28,20},{32,56},... | collective-permute-start | bytes 196616 | tf_op jit(solution)/shard_map/ppermute | solution.py:92
  53.9 6.3 %collective-permute-start.14 = (f32[128,128]{1,0:T(8,128)S(1)}, f32[128,128]{1,0:T(8,128)S(1)}, u32[]{:S(2)}, u32[]{:S(2)}) collective-permute-start(f32[128,128]{1,0:T(8,128)S(1)} %get-tuple-element.70), channel_id=1, source_target_pairs={{0,8},{4,12},{8,16},{12,20},{16,24},{20,28},{24,0},{28,4},{32,40},... | collective-permute-start | bytes 196616 | tf_op jit(solution)/shard_map/ppermute | solution.py:92
  53.9 6.3 %collective-permute-start.15 = (f32[128,128]{1,0:T(8,128)S(1)}, f32[128,128]{1,0:T(8,128)S(1)}, u32[]{:S(2)}, u32[]{:S(2)}) collective-permute-start(f32[128,128]{1,0:T(8,128)S(1)} %get-tuple-element.67.refs_0_.refs_4_), channel_id=1, source_target_pairs={{0,16},{4,20},{8,24},{12,28},{16,0},{20,4},{24,8},{28,12},{32,48},... | collective-permute-start | bytes 196616 | tf_op jit(solution)/shard_map/ppermute | solution.py:92
  60.2 3.9 %collective-permute-start.18 = (f32[128,128]{1,0:T(8,128)S(1)}, f32[128,128]{1,0:T(8,128)S(1)}, u32[]{:S(2)}, u32[]{:S(2)}) collective-permute-start(f32[128,128]{1,0:T(8,128)S(1)} %add.18.refs_2_.refs_0_), channel_id=1, source_target_pairs={{0,224},{4,228},{8,232},{12,236},{16,240},{20,244},{24,248},{28,25... | collective-permute-start | bytes 196616 | tf_op jit(solution)/shard_map/ppermute | solution.py:92
  60.3 4.4 %collective-permute-start.17 = (f32[128,128]{1,0:T(8,128)S(1)}, f32[128,128]{1,0:T(8,128)S(1)}, u32[]{:S(2)}, u32[]{:S(2)}) collective-permute-start(f32[128,128]{1,0:T(8,128)S(1)} %add.18.refs_2_.refs_0_), channel_id=1, source_target_pairs={{0,32},{4,36},{8,40},{12,44},{16,48},{20,52},{24,56},{28,60},{32,6... | collective-permute-start | bytes 196616 | tf_op jit(solution)/shard_map/ppermute | solution.py:92
  64.8 5.3 %collective-permute-start.20 = (f32[128,128]{1,0:T(8,128)S(1)}, f32[128,128]{1,0:T(8,128)S(1)}, u32[]{:S(2)}, u32[]{:S(2)}) collective-permute-start(f32[128,128]{1,0:T(8,128)S(1)} %get-tuple-element.78), channel_id=1, source_target_pairs={{0,160},{4,164},{8,168},{12,172},{16,176},{20,180},{24,184},{28,18... | collective-permute-start | bytes 196616 | tf_op jit(solution)/shard_map/ppermute | solution.py:92
  66.4 5.2 %collective-permute-start.19 = (f32[128,128]{1,0:T(8,128)S(1)}, f32[128,128]{1,0:T(8,128)S(1)}, u32[]{:S(2)}, u32[]{:S(2)}) collective-permute-start(f32[128,128]{1,0:T(8,128)S(1)} %get-tuple-element.75.refs_2_), channel_id=1, source_target_pairs={{0,64},{4,68},{8,72},{12,76},{16,80},{20,84},{24,88},{28,92},{32,9... | collective-permute-start | bytes 196616 | tf_op jit(solution)/shard_map/ppermute | solution.py:92
  71.7 3.2 %collective-permute-start.21 = (f32[128,128]{1,0:T(8,128)S(1)}, f32[128,128]{1,0:T(8,128)S(1)}, u32[]{:S(2)}, u32[]{:S(2)}) collective-permute-start(f32[128,128]{1,0:T(8,128)S(1)} %get-tuple-element.80.refs_2_), channel_id=1, source_target_pairs={{0,8},{4,12},{8,0},{12,4},{16,24},{20,28},{24,16},{28,20},{32,40},... | collective-permute-start | bytes 196616 | tf_op jit(solution)/shard_map/ppermute | solution.py:92
  75.0 5.4 %collective-permute-start.22 = (f32[256,128]{1,0:T(8,128)S(1)}, f32[256,128]{1,0:T(8,128)S(1)}, u32[]{:S(2)}, u32[]{:S(2)}) collective-permute-start(f32[256,128]{1,0:T(8,128)S(1)} %get-tuple-element.90), channel_id=1, source_target_pairs={{0,4},{4,0},{8,12},{12,8},{16,20},{20,16},{24,28},{28,24},{32,36},... | collective-permute-start | bytes 393224 | tf_op jit(solution)/shard_map/ppermute | solution.py:92
  (2 other events, 18.5 us)

commit v4 on v3

v4 whole, which is shorter than its diff:
```python
import jax
import jax.numpy as jnp
from jax import lax
from jax.experimental import pallas as pl
from jax.experimental.pallas import tpu as pltpu
from jax.sharding import PartitionSpec as P

D = 128
BLOCK = 512
HALF = 256
F32 = jnp.float32
BF16 = jnp.bfloat16
PLANES, LINE, CORES = 8, 4, 2


def dot_nn(a, b):
    return lax.dot_general(a, b, (((1,), (0,)), ((), ())), preferred_element_type=F32)


def dot_nt(a, b):
    return lax.dot_general(a, b, (((1,), (1,)), ((), ())), preferred_element_type=F32)


def dot_tn(a, b):
    return lax.dot_general(a, b, (((0,), (0,)), ((), ())), preferred_element_type=F32)


def head_cols(h):
    return slice(h * D, (h + 1) * D)


def params(mib):
    return pltpu.CompilerParams(vmem_limit_bytes=mib * 2**20)


def lower(x):
    t = lax.broadcasted_iota(jnp.int32, x.shape, 0)
    s = lax.broadcasted_iota(jnp.int32, x.shape, 1)
    return jnp.where(t >= s, x, 0.0).astype(BF16)


def upper(x):
    s = lax.broadcasted_iota(jnp.int32, x.shape, 0)
    t = lax.broadcasted_iota(jnp.int32, x.shape, 1)
    return jnp.where(t >= s, x, 0.0).astype(BF16)


TOP, BOTTOM = slice(0, HALF), slice(HALF, BLOCK)
VMEM = pl.BlockSpec(memory_space=pltpu.VMEM)
HBM = pl.BlockSpec(memory_space=pltpu.HBM)
ANY = pl.BlockSpec(memory_space=pl.ANY)


def lower_product(left, right):
    full = dot_nt(left[BOTTOM], right)
    first = lower(dot_nt(left[TOP], right[TOP]))
    return first, full[:, :HALF].astype(BF16), lower(full[:, HALF:])


def upper_product(left, right):
    full = dot_nt(left[TOP], right)
    last = upper(dot_nt(left[BOTTOM], right[BOTTOM]))
    return upper(full[:, :HALF]), full[:, HALF:].astype(BF16), last


def per_token(row):
    return jnp.transpose(jnp.broadcast_to(row, (D, row.shape[1])))


def beside(a, b):
    return jnp.concatenate([a, b], axis=1)


def block_rows(c):
    return slice(c * BLOCK, (c + 1) * BLOCK)


def places():
    me = lax.axis_index("seq")
    return me // (LINE * CORES), me // CORES % LINE, me % CORES


def shift(value, plane=0, line=0, swap=False, pair=False):
    pairs = []
    for z in range(PLANES):
        for x in range(LINE):
            for c in range(CORES):
                source = (z * LINE + x) * CORES + c
                to = x ^ 1 if pair else (x + line) % LINE
                target = ((z + plane) % PLANES * LINE + to) * CORES + (1 - c if swap else c)
                pairs.append((source, target))
    return lax.ppermute(value, "seq", pairs)


def small(body, outs, rows, name, args, after=()):
    def waiting(*refs):
        body(*refs[: len(args)], *refs[len(args) + len(after) :])

    return pl.pallas_call(
        waiting,
        in_specs=[VMEM] * len(args) + [ANY] * len(after),
        out_specs=[VMEM] * outs,
        out_shape=[jax.ShapeDtypeStruct((rows, D), F32)] * outs,
        compiler_params=params(4),
        name=name,
    )(*args, *after)


def when(condition, value):
    return jnp.where(condition, value, 0.0)


def entering(mine, theirs, reverse, beside_rounds):
    def ahead(other, me):
        return other > me if reverse else other < me

    half = mine.shape[0]
    piece = half // 2
    partner = shift(theirs, swap=True)

    def split(mine, partner, same, opposite):
        _, x, _ = places()
        for out, at in ((same, x % 2), (opposite, 1 - x % 2)):
            at = pl.ds(pl.multiple_of(at * piece, piece), piece)
            out[...] = mine[at] + partner[at]

    same, opposite = small(split, 2, piece, "split", (mine, partner))
    done = beside_rounds[0](same)
    parts = [same, shift(opposite, line=1), shift(same, line=2), shift(opposite, line=3)]

    def add(a, b, c, d, out):
        out[...] = a[...] + b[...] + c[...] + d[...]

    (plane,) = small(add, 1, piece, "add", parts, done)
    done = beside_rounds[1](plane)
    below, above = shift(plane, plane=1), shift(plane, plane=-1)

    def windows(plane, below, above, to_up, to_down):
        z, _, _ = places()
        before, after = (z + PLANES - 1) % PLANES, (z + 1) % PLANES
        up, down = (z + 2) % PLANES, (z + PLANES - 3) % PLANES
        to_up[...] = when(ahead(before, up), below[...]) + when(ahead(z, up), plane[...])
        to_down[...] = (
            when(ahead(before, down), below[...]) + when(ahead(z, down), plane[...]) + when(ahead(after, down), above[...])
        )

    to_up, to_down = small(windows, 2, piece, "windows", (plane, below, above), done)
    done = beside_rounds[2](to_up)
    from_down, from_up = shift(to_up, plane=2), shift(to_down, plane=-3)

    def spread(below, above, from_down, from_up, *refs):
        parts, outs = refs[:LINE], refs[LINE:]
        z, x, _ = places()
        before, after = (z + PLANES - 1) % PLANES, (z + 1) % PLANES
        planes = (
            when(ahead(before, z), below[...]) + when(ahead(after, z), above[...]) + from_down[...] + from_up[...]
        )
        for target, out in zip((x, x + 1 - x % 2 * 2), outs):
            total = planes
            for k, part in enumerate(parts):
                total += when(ahead((x + LINE - k) % LINE, target), part[...])
            out[...] = total

    own, sent = small(spread, 2, piece, "spread", (below, above, from_down, from_up, *parts), done)
    done = beside_rounds[3](sent)
    got = shift(sent, pair=True)

    def collect(mine, partner, own, got, kept, other):
        _, x, c = places()
        for at, part in ((x % 2, own), (1 - x % 2, got)):
            at = pl.ds(pl.multiple_of(at * piece, piece), piece)
            kept[at] = part[...] + when(ahead(1 - c, c), partner[at])
            other[at] = part[...] + when(ahead(c, 1 - c), mine[at])

    kept, other = small(collect, 2, half, "collect", (mine, partner, own, got), done)
    return kept, shift(other, swap=True)


def columns(is_mine, i, per_core):
    _, _, c = places()
    half = c if is_mine else 1 - c
    return pl.ds(pl.multiple_of((half * per_core + i) * D, D), D)


def bring(left, right):
    length, width = left.shape
    per_core = width // D // CORES

    def body(left_hbm, right_hbm, left, right, first, total, sems):
        _, _, c = places()
        copies = []
        for i, half in enumerate((1 - c, c)):
            cols = pl.ds(pl.multiple_of(half * per_core * D, per_core * D), per_core * D)
            for j, (source, target) in enumerate(((left_hbm, left), (right_hbm, right))):
                copy = pltpu.make_async_copy(source.at[:, cols], target.at[:, cols], sems.at[i, j])
                copy.start()
                copies.append(copy)
        copies[0].wait()
        copies[1].wait()
        multiply(left, right, False, per_core, first, total)
        copies[2].wait()
        copies[3].wait()

    state = jax.ShapeDtypeStruct((width // CORES, D), F32)
    return pl.pallas_call(
        body,
        in_specs=[HBM, HBM],
        out_specs=[VMEM] * 4,
        out_shape=[jax.ShapeDtypeStruct(left.shape, BF16), jax.ShapeDtypeStruct(right.shape, BF16), state, state],
        scratch_shapes=[pltpu.SemaphoreType.DMA((CORES, 2))],
        compiler_params=params(12),
        name="bring",
    )(pltpu.with_memory_space_constraint(left, pltpu.HBM), pltpu.with_memory_space_constraint(right, pltpu.HBM))


def multiply(left, right, is_mine, per_core, first, total):
    for i in range(per_core):
        cols = columns(is_mine, i, per_core)
        one = dot_tn(left[:BLOCK, cols], right[:BLOCK, cols])
        first[head_cols(i)] = one
        total[head_cols(i)] = one + dot_tn(left[BLOCK:, cols], right[BLOCK:, cols])


def products(left, right):
    width = left.shape[1]

    def body(left, right, first, total):
        multiply(left, right, True, width // D // CORES, first, total)

    state = jax.ShapeDtypeStruct((width // CORES, D), F32)
    return pl.pallas_call(
        body,
        in_specs=[VMEM] * 2,
        out_specs=[VMEM] * 2,
        out_shape=[state, state],
        compiler_params=params(12),
        name="products",
    )(left, right)


def local_attention(q, k, v, is_mine, i, after):
    length, width = q.shape

    def body(q, k, v, _, out):
        cols = columns(is_mine, i, width // D // CORES)
        for c in range(length // BLOCK):
            rows = block_rows(c)
            qv, kv, vv = (x[rows, cols] for x in (q, k, v))
            a, b, d = lower_product(qv, kv)
            out[c * BLOCK : c * BLOCK + HALF] = dot_nn(a, vv[TOP])
            out[c * BLOCK + HALF : (c + 1) * BLOCK] = dot_nn(beside(b, d), vv)

    return pl.pallas_call(
        body,
        in_specs=[VMEM, VMEM, VMEM, ANY],
        out_specs=VMEM,
        out_shape=jax.ShapeDtypeStruct((length, D), F32),
        compiler_params=params(12),
        cost_estimate=pl.CostEstimate(
            flops=length // BLOCK * 4 * BLOCK * BLOCK * D, bytes_accessed=length * D * 10, transcendentals=0
        ),
        name="local_attention",
    )(q, k, v, after)


def attention_sums(q, grad, local, gain, state, first, is_mine, sums):
    length = q.shape[0]
    per_core = len(local)

    def body(q, grad, *refs):
        local, (gain, state, first, *before, attn, sums) = refs[:per_core], refs[per_core:]
        for c in range(length // BLOCK):
            rows = block_rows(c)
            square = jnp.zeros((BLOCK, D), F32)
            inner = jnp.zeros((BLOCK, D), F32)
            for i in range(per_core):
                cols = columns(is_mine, i, per_core)
                prefix = state[head_cols(i)]
                if c > 0:
                    prefix += first[head_cols(i)]
                a = local[i][rows] + dot_nn(q[rows, cols], prefix.astype(BF16))
                attn[rows, head_cols(i)] = a
                square += a * a
                inner += a * (gain[:, cols] * grad[rows, cols].astype(F32))
            for j, part in enumerate((square, inner)):
                row = jnp.sum(jnp.transpose(part), axis=0, keepdims=True)
                sums[j : j + 1, rows] = row + before[0][j : j + 1, rows] if before else row

    return pl.pallas_call(
        body,
        in_specs=[VMEM] * (5 + per_core + len(sums)),
        out_specs=[VMEM] * 2,
        out_shape=[
            jax.ShapeDtypeStruct((length, per_core * D), F32),
            jax.ShapeDtypeStruct((2, length), F32),
        ],
        compiler_params=params(16),
        name="attention_sums",
    )(q, grad, *local, gain, state, first, *sums)


def gradient(q, grad, attn, gain, sums, features, is_mine):
    length, width = attn.shape
    per_core = width // D
    blocks = length // BLOCK

    def body(q, grad, attn, gain, sums, out, last, total):
        for c in range(blocks):
            rows = block_rows(c)
            root = jnp.sqrt(sums[0:1, rows] / features + 1e-05)
            inverse = per_token(1.0 / root)
            weight = per_token(sums[1:2, rows] / (features * root**3))
            for i in range(per_core):
                cols = columns(is_mine, i, per_core)
                scaled = gain[:, cols] * grad[rows, cols].astype(F32)
                g = (scaled * inverse - attn[rows, head_cols(i)] * weight).astype(BF16)
                out[rows, head_cols(i)] = g
                term = dot_tn(q[rows, cols], g)
                total[head_cols(i)] = term if c == 0 else total[head_cols(i)] + term
                if c == blocks - 1:
                    last[head_cols(i)] = term

    state = jax.ShapeDtypeStruct((width, D), F32)
    return pl.pallas_call(
        body,
        in_specs=[VMEM] * 5,
        out_specs=[VMEM] * 3,
        out_shape=[jax.ShapeDtypeStruct((length, width), BF16), state, state],
        compiler_params=params(16),
        name="gradient",
    )(q, grad, attn, gain, sums)


def local_gradients(q, k, v, g, attn, gain, sums, state, first, features, is_mine, i, outs, after):
    length, width = q.shape
    blocks = length // BLOCK
    here = head_cols(i)

    def body(q, k, v, g, attn, gain, sums, state, first, *refs):
        normed, dq, dk, dv, normed_here, dq_here, sems = refs[len(outs) + 1 :]
        cols = columns(is_mine, i, width // D // CORES)
        copies = []

        def send(source, out, j, c):
            copy = pltpu.make_async_copy(source.at[block_rows(c)], out.at[block_rows(c), cols], sems.at[j, c])
            copy.start()
            copies.append(copy)

        for c in range(blocks):
            rows = block_rows(c)
            root = jnp.sqrt(sums[0:1, rows] / features + 1e-05)
            normed_here[rows] = (gain[:, cols] * (attn[rows, here] * per_token(1.0 / root))).astype(BF16)
            send(normed_here, normed, 0, c)
            qv, kv, vv, gv = q[rows, cols], k[rows, cols], v[rows, cols], g[rows, here]
            prefix = state[here] + first[here] if c > 0 else state[here]
            carried = dot_nt(gv, prefix.astype(BF16))
            a, b, d = lower_product(gv, vv)
            top, bottom = slice(c * BLOCK, c * BLOCK + HALF), slice(c * BLOCK + HALF, (c + 1) * BLOCK)
            dq_here[top] = (dot_nn(a, kv[TOP]) + carried[TOP]).astype(BF16)
            dq_here[bottom] = (dot_nn(beside(b, d), kv) + carried[BOTTOM]).astype(BF16)
            send(dq_here, dq, 1, c)
            a, b, d = upper_product(vv, gv)
            dk[top] = dot_nn(beside(a, b), qv)
            dk[bottom] = dot_nn(d, qv[BOTTOM])
            a, b, d = upper_product(kv, qv)
            dv[top] = dot_nn(beside(a, b), gv)
            dv[bottom] = dot_nn(d, gv[BOTTOM])
        for copy in copies:
            copy.wait()

    return pl.pallas_call(
        body,
        in_specs=[VMEM] * 9 + [HBM] * len(outs) + [ANY],
        out_specs=[HBM, HBM, VMEM, VMEM],
        out_shape=[jax.ShapeDtypeStruct((length, width), BF16)] * 2 + [jax.ShapeDtypeStruct((length, D), F32)] * 2,
        scratch_shapes=[pltpu.VMEM((length, D), BF16)] * 2 + [pltpu.SemaphoreType.DMA((2, blocks))],
        input_output_aliases={9 + j: j for j in range(len(outs))},
        compiler_params=params(20),
        cost_estimate=pl.CostEstimate(
            flops=blocks * 12 * BLOCK * BLOCK * D, bytes_accessed=length * D * 20, transcendentals=0
        ),
        name="local_gradients",
    )(q, k, v, g, attn, gain, sums, state, first, *outs, after)


def add_suffix(k, v, dk, dv, state, last, is_mine, outs):
    length, width = k.shape
    per_core = len(dk)
    steps = 2
    part = length // steps

    def body(k, v, *refs):
        dk, dv = refs[:per_core], refs[per_core : 2 * per_core]
        state, last = refs[2 * per_core : 2 * per_core + 2]
        out_k, out_v, here_k, here_v, sems = refs[2 * per_core + 2 + len(outs) :]
        _, _, c = places()
        half = c if is_mine else 1 - c
        target = pl.ds(pl.multiple_of(half * per_core * D, per_core * D), per_core * D)
        copies = []
        for step in range(steps):
            rows = slice(step * part, (step + 1) * part)
            for i in range(per_core):
                cols, here = columns(is_mine, i, per_core), head_cols(i)
                suffix = state[here]
                if step * part < length - BLOCK:
                    suffix += last[here]
                suffix = suffix.astype(BF16)
                here_k[rows, here] = (dk[i][rows] + dot_nt(v[rows, cols], suffix)).astype(BF16)
                here_v[rows, here] = (dv[i][rows] + dot_nn(k[rows, cols], suffix)).astype(BF16)
            for j, (source, out) in enumerate(((here_k, out_k), (here_v, out_v))):
                copy = pltpu.make_async_copy(source.at[rows], out.at[rows, target], sems.at[j, step])
                copy.start()
                copies.append(copy)
        for copy in copies:
            copy.wait()

    shape = jax.ShapeDtypeStruct((length, width), BF16)
    inputs = 4 + 2 * per_core
    return pl.pallas_call(
        body,
        in_specs=[VMEM] * inputs + [HBM] * len(outs),
        out_specs=[HBM, HBM],
        out_shape=[shape, shape],
        scratch_shapes=[pltpu.VMEM((length, per_core * D), BF16)] * 2 + [pltpu.SemaphoreType.DMA((2, steps))],
        input_output_aliases={inputs + j: j for j in range(len(outs))},
        compiler_params=params(16),
        name="add_suffix",
    )(k, v, *dk, *dv, state, last, *outs)


def head_sum(part):
    count = lax.axis_size("head")
    total = part
    for k in range(1, count):
        total = total + lax.ppermute(part, "head", [(i, (i + k) % count) for i in range(count)])
    return total


def on_device(queries, token_keys, values, norm_gain, out_grad):
    heads = queries.shape[1] // D
    features = lax.axis_size("head") * heads * D
    gain = norm_gain.reshape(1, heads * D)
    per_core = heads // CORES
    order = [(is_mine, i) for is_mine in (True, False) for i in range(per_core)]
    keys, vals, first_theirs, theirs = bring(token_keys, values)
    first_mine, mine = products(keys, vals)
    first = {True: first_mine, False: first_theirs}
    local = {True: [], False: []}

    def attend(is_mine, i):
        def run(after):
            local[is_mine].append(local_attention(queries, keys, vals, is_mine, i, after))
            return local[is_mine][-1:]

        return run

    kept, other = entering(mine, theirs, False, [attend(*head) for head in order])
    before = {True: kept, False: other}
    attn, sums = {}, ()
    for is_mine in (True, False):
        attn[is_mine], part = attention_sums(
            queries, out_grad, local[is_mine], gain, before[is_mine], first[is_mine], is_mine, sums
        )
        sums = (part,)
    sums = head_sum(part)
    grad_attn, last, total = {}, {}, {}
    for is_mine in (False, True):
        grad_attn[is_mine], last[is_mine], total[is_mine] = gradient(
            queries, out_grad, attn[is_mine], gain, sums, features, is_mine
        )
    outs, key_parts, value_parts = [], {True: [], False: []}, {True: [], False: []}

    def differentiate(is_mine, i):
        def run(after):
            normed, query, key, value = local_gradients(
                queries,
                keys,
                vals,
                grad_attn[is_mine],
                attn[is_mine],
                gain,
                sums,
                before[is_mine],
                first[is_mine],
                features,
                is_mine,
                i,
                tuple(outs),
                after,
            )
            outs[:] = [normed, query]
            key_parts[is_mine].append(key)
            value_parts[is_mine].append(value)
            return [value]

        return run

    kept, other = entering(total[True], total[False], True, [differentiate(*head) for head in order])
    normed_out, grad_query = outs
    outs = ()
    for is_mine, state in ((True, kept), (False, other)):
        outs = add_suffix(keys, vals, key_parts[is_mine], value_parts[is_mine], state, last[is_mine], is_mine, outs)
    grad_key, grad_value = outs
    return normed_out, grad_query, grad_key, grad_value


def solution(mesh):
    placed = (P("seq", "head"), P("seq", "head"), P("seq", "head"), P("head"), P("seq", "head"))
    return jax.shard_map(
        on_device,
        mesh=mesh,
        in_specs=placed,
        out_specs=(P("seq", "head"), P("seq", "head"), P("seq", "head"), P("seq", "head")),
        check_vma=False,
    )
```

time: 82.4 us -> 81.2 us (0.985)
  waiting for transfers between devices: 25.5 us -> 22.3 us
  Pallas kernels: 18.2 us -> 19.8 us
    ppermute x20, waiting for transfers between devices: 22.3 us -> 19.1 us  [shift(): return lax.ppermute(value, 'seq', pairs)]
    pallas_call x8 -> x12, Pallas kernels: 15.2 us -> 16.7 us  [the longest x4 9.53 us: local_gradients(): pl.pallas_call(body, in_specs=[VMEM] * 9 + [HBM] * len(outs) + [ANY], out...]
  transfers between devices with their start and end apart: 23 -> 23, of which waited for: 17 -> 15; matrix products, arithmetic and copies ran while one was open for 0% -> 0% of each run, Pallas kernels for 15% -> 19%
where the time goes in v4:
time: 81.2 us; the launch traced here: 81.1 us
  starting transfers between devices  37.3 us (46%)
  waiting for transfers between devices  22.3 us (27%)
  Pallas kernels  19.8 us (24%)
  between operations  1.03 us (1%)
    ppermute x20, starting transfers between devices, shift(): return lax.ppermute(value, 'seq', pairs)  33.4 us
    ppermute x20, waiting for transfers between devices, shift(): return lax.ppermute(value, 'seq', pairs)  19.1 us
    pallas_call x4, Pallas kernels, local_gradients(): pl.pallas_call(body, in_specs=[VMEM] * 9 + [HBM] * len(outs) + [ANY], out...  9.53 us
    ppermute x3, starting transfers between devices, head_sum(): lax.ppermute(part, 'head', [(i, (i + k) % count) for i in range(count)])  3.86 us
    ppermute x3, waiting for transfers between devices, head_sum(): lax.ppermute(part, 'head', [(i, (i + k) % count) for i in range(count)])  3.12 us
    pallas_call x4, Pallas kernels, local_attention(): pl.pallas_call(body, in_specs=[VMEM, VMEM, VMEM, ANY], out_specs=VMEM, ou...  2.76 us
    pallas_call x2, Pallas kernels, add_suffix(): pl.pallas_call(body, in_specs=[VMEM] * inputs + [HBM] * len(outs), out_sp...  2.59 us
  transfers between devices with their start and end apart: 23, of which 15 were waited for; matrix products, arithmetic and copies ran while one was open for 0% of the time, Pallas kernels for 19%

profile of v4, /device:TPU:1, one launch (start us, length us, event | category | flops | bytes accessed | tf_op | source)
XLA Modules:
  0.0 81.1 jit_solution(14862588758350488068)
XLA Ops:
  0.6 1.6 %bring.1 = (bf16[1024,512]{1,0:T(8,128)(2,1)S(1)}, bf16[1024,512]{1,0:T(8,128)(2,1)S(1)}, f32[256,128]{1,0:T(8,128)S(1)}, f32[256,128]{1,0:T(8,128)S(1)}) custom-call(bf16[1024,512]{1,0:T(8,128)(2,1)} %left_hbm.1, bf16[1024,512]{1,0:T(8,128)(2,1)} %right_hbm.1), custom_call_target="tpu_custom_call" | custom-call | tf_op jit(solution)/shard_map/bring/pallas_call | solution.py:205
  2.2 3.3 %collective-permute-start = (f32[256,128]{1,0:T(8,128)S(1)}, f32[256,128]{1,0:T(8,128)S(1)}, u32[]{:S(2)}, u32[]{:S(2)}) collective-permute-start(f32[256,128]{1,0:T(8,128)S(1)} %get-tuple-element.59), channel_id=1, source_target_pairs={{0,4},{4,0},{8,12},{12,8},{16,20},{20,16},{24,28},{28,24},{32,36},... | collective-permute-start | bytes 393224 | tf_op jit(solution)/shard_map/ppermute | solution.py:92
  9.8 1.9 %collective-permute-done.1.refs_1_.refs_5_ = f32[128,128]{1,0:T(8,128)S(1)} collective-permute-done((f32[128,128]{1,0:T(8,128)S(1)}, f32[128,128]{1,0:T(8,128)S(1)}, u32[]{:S(2)}, u32[]{:S(2)}) %collective-permute-start.1) | collective-permute-done | bytes 65568 | tf_op jit(solution)/shard_map/ppermute | solution.py:92
  12.8 5.9 %collective-permute-start.5 = (f32[128,128]{1,0:T(8,128)S(1)}, f32[128,128]{1,0:T(8,128)S(1)}, u32[]{:S(2)}, u32[]{:S(2)}) collective-permute-start(f32[128,128]{1,0:T(8,128)S(1)} %add.17._.refs_0_), channel_id=1, source_target_pairs={{0,224},{4,228},{8,232},{12,236},{16,240},{20,244},{24,248},{28,25... | collective-permute-start | bytes 196616 | tf_op jit(solution)/shard_map/ppermute | solution.py:92
  20.0 3.0 %collective-permute-done.4.refs_1_.refs_0_ = f32[128,128]{1,0:T(8,128)S(1)} collective-permute-done((f32[128,128]{1,0:T(8,128)S(1)}, f32[128,128]{1,0:T(8,128)S(1)}, u32[]{:S(2)}, u32[]{:S(2)}) %collective-permute-start.4) | collective-permute-done | bytes 65568 | tf_op jit(solution)/shard_map/ppermute | solution.py:92
  23.5 1.7 %collective-permute-start.6 = (f32[128,128]{1,0:T(8,128)S(1)}, f32[128,128]{1,0:T(8,128)S(1)}, u32[]{:S(2)}, u32[]{:S(2)}) collective-permute-start(f32[128,128]{1,0:T(8,128)S(1)} %get-tuple-element.62._), channel_id=1, source_target_pairs={{0,64},{4,68},{8,72},{12,76},{16,80},{20,84},{24,88},{28,92},{32,9... | collective-permute-start | bytes 196616 | tf_op jit(solution)/shard_map/ppermute | solution.py:92
  25.9 2.1 %collective-permute-done.7.refs_3_ = f32[128,128]{1,0:T(8,128)S(1)} collective-permute-done((f32[128,128]{1,0:T(8,128)S(1)}, f32[128,128]{1,0:T(8,128)S(1)}, u32[]{:S(2)}, u32[]{:S(2)}) %collective-permute-start.7) | collective-permute-done | bytes 65568 | tf_op jit(solution)/shard_map/ppermute | solution.py:92
  28.1 1.4 %collective-permute-done.6.refs_2_ = f32[128,128]{1,0:T(8,128)S(1)} collective-permute-done((f32[128,128]{1,0:T(8,128)S(1)}, f32[128,128]{1,0:T(8,128)S(1)}, u32[]{:S(2)}, u32[]{:S(2)}) %collective-permute-start.6) | collective-permute-done | bytes 65568 | tf_op jit(solution)/shard_map/ppermute | solution.py:92
  30.3 2.7 %collective-permute-done.8.refs_3_ = f32[128,128]{1,0:T(8,128)S(1)} collective-permute-done((f32[128,128]{1,0:T(8,128)S(1)}, f32[128,128]{1,0:T(8,128)S(1)}, u32[]{:S(2)}, u32[]{:S(2)}) %collective-permute-start.8) | collective-permute-done | bytes 65568 | tf_op jit(solution)/shard_map/ppermute | solution.py:92
  33.1 5.0 %collective-permute-start.9 = (f32[256,128]{1,0:T(8,128)S(1)}, f32[256,128]{1,0:T(8,128)S(1)}, u32[]{:S(2)}, u32[]{:S(2)}) collective-permute-start(f32[256,128]{1,0:T(8,128)S(1)} %get-tuple-element.66), channel_id=1, source_target_pairs={{0,4},{4,0},{8,12},{12,8},{16,20},{20,16},{24,28},{28,24},{32,36},... | collective-permute-start | bytes 393224 | tf_op jit(solution)/shard_map/ppermute | solution.py:92
  39.9 2.8 %collective-permute-start.12 = (f32[2,1024]{1,0:T(2,128)S(1)}, f32[2,1024]{1,0:T(2,128)S(1)}, u32[]{:S(2)}, u32[]{:S(2)}) collective-permute-start(f32[2,1024]{1,0:T(2,128)S(1)} %get-tuple-element.72), channel_id=1, source_target_pairs={{0,3},{1,0},{2,1},{3,2},{4,7},{5,4},{6,5},{7,6},{8,11},{9,8},{10,9... | collective-permute-start | bytes 24584 | tf_op jit(solution)/shard_map/ppermute | solution.py:435
  43.8 3.0 %collective-permute-done.11 = f32[2,1024]{1,0:T(2,128)S(1)} collective-permute-done((f32[2,1024]{1,0:T(2,128)S(1)}, f32[2,1024]{1,0:T(2,128)S(1)}, u32[]{:S(2)}, u32[]{:S(2)}) %collective-permute-start.11) | collective-permute-done | bytes 8224 | tf_op jit(solution)/shard_map/ppermute | solution.py:435
  47.7 1.8 %collective-permute-start.13 = (f32[256,128]{1,0:T(8,128)S(1)}, f32[256,128]{1,0:T(8,128)S(1)}, u32[]{:S(2)}, u32[]{:S(2)}) collective-permute-start(f32[256,128]{1,0:T(8,128)S(1)} %get-tuple-element.77), channel_id=1, source_target_pairs={{0,4},{4,0},{8,12},{12,8},{16,20},{20,16},{24,28},{28,24},{32,36},... | collective-permute-start | bytes 393224 | tf_op jit(solution)/shard_map/ppermute | solution.py:92
  50.5 2.3 %collective-permute-start.16 = (f32[128,128]{1,0:T(8,128)S(1)}, f32[128,128]{1,0:T(8,128)S(1)}, u32[]{:S(2)}, u32[]{:S(2)}) collective-permute-start(f32[128,128]{1,0:T(8,128)S(1)} %get-tuple-element.81), channel_id=1, source_target_pairs={{0,24},{4,28},{8,0},{12,4},{16,8},{20,12},{24,16},{28,20},{32,56},... | collective-permute-start | bytes 196616 | tf_op jit(solution)/shard_map/ppermute | solution.py:92
  54.0 2.4 %local_gradients.4 = (bf16[1024,512]{1,0:T(8,128)(2,1)}, bf16[1024,512]{1,0:T(8,128)(2,1)}, f32[1024,128]{1,0:T(8,128)S(1)}, f32[1024,128]{1,0:T(8,128)S(1)}) custom-call(bf16[1024,512]{1,0:T(8,128)(2,1)S(1)} %copy-done, bf16[1024,512]{1,0:T(8,128)(2,1)S(1)} %get-tuple-element.56.left.k, bf16[1024,512]{1,0:T(8,128)(2,1)S(1)} %get-tuple-element.57.right.v, ...), custom_call_target="tpu_custom_call" | custom-call | flops 805306368 | bytes 2621440 | tf_op jit(solution)/shard_map/local_gradients/pallas_call | solution.py:371
  56.4 2.6 %collective-permute-done.14.refs_1_.refs_5_ = f32[128,128]{1,0:T(8,128)S(1)} collective-permute-done((f32[128,128]{1,0:T(8,128)S(1)}, f32[128,128]{1,0:T(8,128)S(1)}, u32[]{:S(2)}, u32[]{:S(2)}) %collective-permute-start.14) | collective-permute-done | bytes 65568 | tf_op jit(solution)/shard_map/ppermute | solution.py:92
  59.2 1.5 %collective-permute-start.17 = (f32[128,128]{1,0:T(8,128)S(1)}, f32[128,128]{1,0:T(8,128)S(1)}, u32[]{:S(2)}, u32[]{:S(2)}) collective-permute-start(f32[128,128]{1,0:T(8,128)S(1)} %add.18.refs_2_.refs_0_), channel_id=1, source_target_pairs={{0,32},{4,36},{8,40},{12,44},{16,48},{20,52},{24,56},{28,60},{32,6... | collective-permute-start | bytes 196616 | tf_op jit(solution)/shard_map/ppermute | solution.py:92
  60.7 2.4 %local_gradients.5 = (bf16[1024,512]{1,0:T(8,128)(2,1)}, bf16[1024,512]{1,0:T(8,128)(2,1)}, f32[1024,128]{1,0:T(8,128)S(1)}, f32[1024,128]{1,0:T(8,128)S(1)}) custom-call(bf16[1024,512]{1,0:T(8,128)(2,1)S(1)} %copy-done, bf16[1024,512]{1,0:T(8,128)(2,1)S(1)} %get-tuple-element.56.left.k, ...), custom_call_target="tpu_custom_call", output_to_operand_aliasing={{0}: (9, {}), {1}: (10, {})} | custom-call | flops 805306368 | bytes 2621440 | tf_op jit(solution)/shard_map/local_gradients/pallas_call | solution.py:371
  63.6 1.7 %collective-permute-start.20 = (f32[128,128]{1,0:T(8,128)S(1)}, f32[128,128]{1,0:T(8,128)S(1)}, u32[]{:S(2)}, u32[]{:S(2)}) collective-permute-start(f32[128,128]{1,0:T(8,128)S(1)} %get-tuple-element.89), channel_id=1, source_target_pairs={{0,160},{4,164},{8,168},{12,172},{16,176},{20,180},{24,184},{28,18... | collective-permute-start | bytes 196616 | tf_op jit(solution)/shard_map/ppermute | solution.py:92
  66.6 2.4 %local_gradients.6 = (bf16[1024,512]{1,0:T(8,128)(2,1)}, bf16[1024,512]{1,0:T(8,128)(2,1)}, f32[1024,128]{1,0:T(8,128)S(1)}, f32[1024,128]{1,0:T(8,128)S(1)}) custom-call(bf16[1024,512]{1,0:T(8,128)(2,1)S(1)} %copy-done, bf16[1024,512]{1,0:T(8,128)(2,1)S(1)} %get-tuple-element.56.left.k, ...), custom_call_target="tpu_custom_call", output_to_operand_aliasing={{0}: (9, {}), {1}: (10, {})} | custom-call | flops 805306368 | bytes 2621440 | tf_op jit(solution)/shard_map/local_gradients/pallas_call | solution.py:371
  69.0 1.6 %collective-permute-done.19.refs_2_ = f32[128,128]{1,0:T(8,128)S(1)} collective-permute-done((f32[128,128]{1,0:T(8,128)S(1)}, f32[128,128]{1,0:T(8,128)S(1)}, u32[]{:S(2)}, u32[]{:S(2)}) %collective-permute-start.19) | collective-permute-done | bytes 65568 | tf_op jit(solution)/shard_map/ppermute | solution.py:92
  70.7 2.4 %local_gradients.7 = (bf16[1024,512]{1,0:T(8,128)(2,1)}, bf16[1024,512]{1,0:T(8,128)(2,1)}, f32[1024,128]{1,0:T(8,128)S(1)}, f32[1024,128]{1,0:T(8,128)S(1)}) custom-call(bf16[1024,512]{1,0:T(8,128)(2,1)S(1)} %copy-done, bf16[1024,512]{1,0:T(8,128)(2,1)S(1)} %get-tuple-element.56.left.k, ...), custom_call_target="tpu_custom_call", output_to_operand_aliasing={{0}: (9, {}), {1}: (10, {})} | custom-call | flops 805306368 | bytes 2621440 | tf_op jit(solution)/shard_map/local_gradients/pallas_call | solution.py:371
  73.9 4.4 %collective-permute-start.22 = (f32[256,128]{1,0:T(8,128)S(1)}, f32[256,128]{1,0:T(8,128)S(1)}, u32[]{:S(2)}, u32[]{:S(2)}) collective-permute-start(f32[256,128]{1,0:T(8,128)S(1)} %get-tuple-element.98), channel_id=1, source_target_pairs={{0,4},{4,0},{8,12},{12,8},{16,20},{20,16},{24,28},{28,24},{32,36},... | collective-permute-start | bytes 393224 | tf_op jit(solution)/shard_map/ppermute | solution.py:92
  79.6 1.3 %add_suffix.3 = (bf16[1024,512]{1,0:T(8,128)(2,1)}, bf16[1024,512]{1,0:T(8,128)(2,1)}) custom-call(bf16[1024,512]{1,0:T(8,128)(2,1)S(1)} %get-tuple-element.56.left.k, bf16[1024,512]{1,0:T(8,128)(2,1)S(1)} %get-tuple-element.57.right.v, f32[1024,128]{1,0:T(8,128)S(1)} %get-tuple-element.94.refs_0_, ...), custom_call_target="tpu_custom_call", output_to_operand_aliasing={{0}: (8, {}), {1}: (9, {})} | custom-call | tf_op jit(solution)/shard_map/add_suffix/pallas_call | solution.py:419
  (55 shorter events, 19.0 us)
Async XLA Ops:
  2.2 4.3 %collective-permute-start = (f32[256,128]{1,0:T(8,128)S(1)}, f32[256,128]{1,0:T(8,128)S(1)}, u32[]{:S(2)}, u32[]{:S(2)}) collective-permute-start(f32[256,128]{1,0:T(8,128)S(1)} %get-tuple-element.59), channel_id=1, source_target_pairs={{0,4},{4,0},{8,12},{12,8},{16,20},{20,16},{24,28},{28,24},{32,36},... | collective-permute-start | bytes 393224 | tf_op jit(solution)/shard_map/ppermute | solution.py:92
  6.6 3.2 %collective-permute-start.3 = (f32[128,128]{1,0:T(8,128)S(1)}, f32[128,128]{1,0:T(8,128)S(1)}, u32[]{:S(2)}, u32[]{:S(2)}) collective-permute-start(f32[128,128]{1,0:T(8,128)S(1)} %get-tuple-element.61), channel_id=1, source_target_pairs={{0,24},{4,28},{8,0},{12,4},{16,8},{20,12},{24,16},{28,20},{32,56},... | collective-permute-start | bytes 196616 | tf_op jit(solution)/shard_map/ppermute | solution.py:92
  7.4 4.3 %collective-permute-start.1 = (f32[128,128]{1,0:T(8,128)S(1)}, f32[128,128]{1,0:T(8,128)S(1)}, u32[]{:S(2)}, u32[]{:S(2)}) collective-permute-start(f32[128,128]{1,0:T(8,128)S(1)} %get-tuple-element.61), channel_id=1, source_target_pairs={{0,8},{4,12},{8,16},{12,20},{16,24},{20,28},{24,0},{28,4},{32,40},... | collective-permute-start | bytes 196616 | tf_op jit(solution)/shard_map/ppermute | solution.py:92
  8.1 4.7 %collective-permute-start.2 = (f32[128,128]{1,0:T(8,128)S(1)}, f32[128,128]{1,0:T(8,128)S(1)}, u32[]{:S(2)}, u32[]{:S(2)}) collective-permute-start(f32[128,128]{1,0:T(8,128)S(1)} %get-tuple-element.60._.refs_0_.refs_4_), channel_id=1, source_target_pairs={{0,16},{4,20},{8,24},{12,28},{16,0},{20,4},{24,8},{28,12},{32,48},... | collective-permute-start | bytes 196616 | tf_op jit(solution)/shard_map/ppermute | solution.py:92
  12.8 7.2 %collective-permute-start.5 = (f32[128,128]{1,0:T(8,128)S(1)}, f32[128,128]{1,0:T(8,128)S(1)}, u32[]{:S(2)}, u32[]{:S(2)}) collective-permute-start(f32[128,128]{1,0:T(8,128)S(1)} %add.17._.refs_0_), channel_id=1, source_target_pairs={{0,224},{4,228},{8,232},{12,236},{16,240},{20,244},{24,248},{28,25... | collective-permute-start | bytes 196616 | tf_op jit(solution)/shard_map/ppermute | solution.py:92
  18.7 4.3 %collective-permute-start.4 = (f32[128,128]{1,0:T(8,128)S(1)}, f32[128,128]{1,0:T(8,128)S(1)}, u32[]{:S(2)}, u32[]{:S(2)}) collective-permute-start(f32[128,128]{1,0:T(8,128)S(1)} %add.17._.refs_0_), channel_id=1, source_target_pairs={{0,32},{4,36},{8,40},{12,44},{16,48},{20,52},{24,56},{28,60},{32,6... | collective-permute-start | bytes 196616 | tf_op jit(solution)/shard_map/ppermute | solution.py:92
  23.0 5.0 %collective-permute-start.7 = (f32[128,128]{1,0:T(8,128)S(1)}, f32[128,128]{1,0:T(8,128)S(1)}, u32[]{:S(2)}, u32[]{:S(2)}) collective-permute-start(f32[128,128]{1,0:T(8,128)S(1)} %get-tuple-element.63), channel_id=1, source_target_pairs={{0,160},{4,164},{8,168},{12,172},{16,176},{20,180},{24,184},{28,18... | collective-permute-start | bytes 196616 | tf_op jit(solution)/shard_map/ppermute | solution.py:92
  23.5 5.9 %collective-permute-start.6 = (f32[128,128]{1,0:T(8,128)S(1)}, f32[128,128]{1,0:T(8,128)S(1)}, u32[]{:S(2)}, u32[]{:S(2)}) collective-permute-start(f32[128,128]{1,0:T(8,128)S(1)} %get-tuple-element.62._), channel_id=1, source_target_pairs={{0,64},{4,68},{8,72},{12,76},{16,80},{20,84},{24,88},{28,92},{32,9... | collective-permute-start | bytes 196616 | tf_op jit(solution)/shard_map/ppermute | solution.py:92
  29.5 3.5 %collective-permute-start.8 = (f32[128,128]{1,0:T(8,128)S(1)}, f32[128,128]{1,0:T(8,128)S(1)}, u32[]{:S(2)}, u32[]{:S(2)}) collective-permute-start(f32[128,128]{1,0:T(8,128)S(1)} %get-tuple-element.64._), channel_id=1, source_target_pairs={{0,8},{4,12},{8,0},{12,4},{16,24},{20,28},{24,16},{28,20},{32,40},... | collective-permute-start | bytes 196616 | tf_op jit(solution)/shard_map/ppermute | solution.py:92
  29.6 8.5 %copy-start.1 = (bf16[1024,512]{1,0:T(8,128)(2,1)S(1)}, bf16[1024,512]{1,0:T(8,128)(2,1)}, u32[]{:S(2)}) copy-start(bf16[1024,512]{1,0:T(8,128)(2,1)} %grad.7) | copy-start | bytes 3145732
  33.1 6.3 %collective-permute-start.9 = (f32[256,128]{1,0:T(8,128)S(1)}, f32[256,128]{1,0:T(8,128)S(1)}, u32[]{:S(2)}, u32[]{:S(2)}) collective-permute-start(f32[256,128]{1,0:T(8,128)S(1)} %get-tuple-element.66), channel_id=1, source_target_pairs={{0,4},{4,0},{8,12},{12,8},{16,20},{20,16},{24,28},{28,24},{32,36},... | collective-permute-start | bytes 393224 | tf_op jit(solution)/shard_map/ppermute | solution.py:92
  39.9 3.9 %collective-permute-start.12 = (f32[2,1024]{1,0:T(2,128)S(1)}, f32[2,1024]{1,0:T(2,128)S(1)}, u32[]{:S(2)}, u32[]{:S(2)}) collective-permute-start(f32[2,1024]{1,0:T(2,128)S(1)} %get-tuple-element.72), channel_id=1, source_target_pairs={{0,3},{1,0},{2,1},{3,2},{4,7},{5,4},{6,5},{7,6},{8,11},{9,8},{10,9... | collective-permute-start | bytes 24584 | tf_op jit(solution)/shard_map/ppermute | solution.py:435
  42.8 4.0 %collective-permute-start.11 = (f32[2,1024]{1,0:T(2,128)S(1)}, f32[2,1024]{1,0:T(2,128)S(1)}, u32[]{:S(2)}, u32[]{:S(2)}) collective-permute-start(f32[2,1024]{1,0:T(2,128)S(1)} %get-tuple-element.72), channel_id=1, source_target_pairs={{0,2},{1,3},{2,0},{3,1},{4,6},{5,7},{6,4},{7,5},{8,10},{9,11},{10,... | collective-permute-start | bytes 24584 | tf_op jit(solution)/shard_map/ppermute | solution.py:435
  43.2 3.7 %collective-permute-start.10 = (f32[2,1024]{1,0:T(2,128)S(1)}, f32[2,1024]{1,0:T(2,128)S(1)}, u32[]{:S(2)}, u32[]{:S(2)}) collective-permute-start(f32[2,1024]{1,0:T(2,128)S(1)} %get-tuple-element.72), channel_id=1, source_target_pairs={{0,1},{1,2},{2,3},{3,0},{4,5},{5,6},{6,7},{7,4},{8,9},{9,10},{10,1... | collective-permute-start | bytes 24584 | tf_op jit(solution)/shard_map/ppermute | solution.py:435
  47.7 2.7 %collective-permute-start.13 = (f32[256,128]{1,0:T(8,128)S(1)}, f32[256,128]{1,0:T(8,128)S(1)}, u32[]{:S(2)}, u32[]{:S(2)}) collective-permute-start(f32[256,128]{1,0:T(8,128)S(1)} %get-tuple-element.77), channel_id=1, source_target_pairs={{0,4},{4,0},{8,12},{12,8},{16,20},{20,16},{24,28},{28,24},{32,36},... | collective-permute-start | bytes 393224 | tf_op jit(solution)/shard_map/ppermute | solution.py:92
  50.5 6.0 %collective-permute-start.16 = (f32[128,128]{1,0:T(8,128)S(1)}, f32[128,128]{1,0:T(8,128)S(1)}, u32[]{:S(2)}, u32[]{:S(2)}) collective-permute-start(f32[128,128]{1,0:T(8,128)S(1)} %get-tuple-element.81), channel_id=1, source_target_pairs={{0,24},{4,28},{8,0},{12,4},{16,8},{20,12},{24,16},{28,20},{32,56},... | collective-permute-start | bytes 196616 | tf_op jit(solution)/shard_map/ppermute | solution.py:92
  52.8 6.3 %collective-permute-start.14 = (f32[128,128]{1,0:T(8,128)S(1)}, f32[128,128]{1,0:T(8,128)S(1)}, u32[]{:S(2)}, u32[]{:S(2)}) collective-permute-start(f32[128,128]{1,0:T(8,128)S(1)} %get-tuple-element.81), channel_id=1, source_target_pairs={{0,8},{4,12},{8,16},{12,20},{16,24},{20,28},{24,0},{28,4},{32,40},... | collective-permute-start | bytes 196616 | tf_op jit(solution)/shard_map/ppermute | solution.py:92
  52.8 6.3 %collective-permute-start.15 = (f32[128,128]{1,0:T(8,128)S(1)}, f32[128,128]{1,0:T(8,128)S(1)}, u32[]{:S(2)}, u32[]{:S(2)}) collective-permute-start(f32[128,128]{1,0:T(8,128)S(1)} %get-tuple-element.78.refs_0_.refs_4_), channel_id=1, source_target_pairs={{0,16},{4,20},{8,24},{12,28},{16,0},{20,4},{24,8},{28,12},{32,48},... | collective-permute-start | bytes 196616 | tf_op jit(solution)/shard_map/ppermute | solution.py:92
  59.1 3.9 %collective-permute-start.18 = (f32[128,128]{1,0:T(8,128)S(1)}, f32[128,128]{1,0:T(8,128)S(1)}, u32[]{:S(2)}, u32[]{:S(2)}) collective-permute-start(f32[128,128]{1,0:T(8,128)S(1)} %add.18.refs_2_.refs_0_), channel_id=1, source_target_pairs={{0,224},{4,228},{8,232},{12,236},{16,240},{20,244},{24,248},{28,25... | collective-permute-start | bytes 196616 | tf_op jit(solution)/shard_map/ppermute | solution.py:92
  59.2 4.4 %collective-permute-start.17 = (f32[128,128]{1,0:T(8,128)S(1)}, f32[128,128]{1,0:T(8,128)S(1)}, u32[]{:S(2)}, u32[]{:S(2)}) collective-permute-start(f32[128,128]{1,0:T(8,128)S(1)} %add.18.refs_2_.refs_0_), channel_id=1, source_target_pairs={{0,32},{4,36},{8,40},{12,44},{16,48},{20,52},{24,56},{28,60},{32,6... | collective-permute-start | bytes 196616 | tf_op jit(solution)/shard_map/ppermute | solution.py:92
  63.6 5.3 %collective-permute-start.20 = (f32[128,128]{1,0:T(8,128)S(1)}, f32[128,128]{1,0:T(8,128)S(1)}, u32[]{:S(2)}, u32[]{:S(2)}) collective-permute-start(f32[128,128]{1,0:T(8,128)S(1)} %get-tuple-element.89), channel_id=1, source_target_pairs={{0,160},{4,164},{8,168},{12,172},{16,176},{20,180},{24,184},{28,18... | collective-permute-start | bytes 196616 | tf_op jit(solution)/shard_map/ppermute | solution.py:92
  65.3 5.2 %collective-permute-start.19 = (f32[128,128]{1,0:T(8,128)S(1)}, f32[128,128]{1,0:T(8,128)S(1)}, u32[]{:S(2)}, u32[]{:S(2)}) collective-permute-start(f32[128,128]{1,0:T(8,128)S(1)} %get-tuple-element.86.refs_2_), channel_id=1, source_target_pairs={{0,64},{4,68},{8,72},{12,76},{16,80},{20,84},{24,88},{28,92},{32,9... | collective-permute-start | bytes 196616 | tf_op jit(solution)/shard_map/ppermute | solution.py:92
  70.6 3.2 %collective-permute-start.21 = (f32[128,128]{1,0:T(8,128)S(1)}, f32[128,128]{1,0:T(8,128)S(1)}, u32[]{:S(2)}, u32[]{:S(2)}) collective-permute-start(f32[128,128]{1,0:T(8,128)S(1)} %get-tuple-element.91.refs_2_), channel_id=1, source_target_pairs={{0,8},{4,12},{8,0},{12,4},{16,24},{20,28},{24,16},{28,20},{32,40},... | collective-permute-start | bytes 196616 | tf_op jit(solution)/shard_map/ppermute | solution.py:92
  73.9 5.7 %collective-permute-start.22 = (f32[256,128]{1,0:T(8,128)S(1)}, f32[256,128]{1,0:T(8,128)S(1)}, u32[]{:S(2)}, u32[]{:S(2)}) collective-permute-start(f32[256,128]{1,0:T(8,128)S(1)} %get-tuple-element.98), channel_id=1, source_target_pairs={{0,4},{4,0},{8,12},{12,8},{16,20},{20,16},{24,28},{28,24},{32,36},... | collective-permute-start | bytes 393224 | tf_op jit(solution)/shard_map/ppermute | solution.py:92
  (2 other events, 4.2 us)

commit v5 on v4

--- a/solution.py
+++ b/solution.py
@@ -191,15 +191,23 @@
         copies = []
         for i, half in enumerate((1 - c, c)):
             cols = pl.ds(pl.multiple_of(half * per_core * D, per_core * D), per_core * D)
-            for j, (source, target) in enumerate(((left_hbm, left), (right_hbm, right))):
-                copy = pltpu.make_async_copy(source.at[:, cols], target.at[:, cols], sems.at[i, j])
-                copy.start()
-                copies.append(copy)
-        copies[0].wait()
-        copies[1].wait()
-        multiply(left, right, False, per_core, first, total)
-        copies[2].wait()
-        copies[3].wait()
+            for b in range(length // BLOCK):
+                at = (pl.ds(b * BLOCK, BLOCK), cols)
+                pair = []
+                for j, (source, target) in enumerate(((left_hbm, left), (right_hbm, right))):
+                    pair.append(pltpu.make_async_copy(source.at[at], target.at[at], sems.at[i, b, j]))
+                    pair[-1].start()
+                copies.append(pair)
+        for b, pair in enumerate(copies):
+            for copy in pair:
+                copy.wait()
+            if b < length // BLOCK:
+                for i in range(per_core):
+                    here, cols = head_cols(i), columns(False, i, per_core)
+                    term = dot_tn(left[block_rows(b), cols], right[block_rows(b), cols])
+                    if b == 0:
+                        first[here] = term
+                    total[here] = term if b == 0 else total[here] + term
 
     state = jax.ShapeDtypeStruct((width // CORES, D), F32)
     return pl.pallas_call(
@@ -207,25 +215,22 @@
         in_specs=[HBM, HBM],
         out_specs=[VMEM] * 4,
         out_shape=[jax.ShapeDtypeStruct(left.shape, BF16), jax.ShapeDtypeStruct(right.shape, BF16), state, state],
-        scratch_shapes=[pltpu.SemaphoreType.DMA((CORES, 2))],
+        scratch_shapes=[pltpu.SemaphoreType.DMA((CORES, length // BLOCK, 2))],
         compiler_params=params(12),
         name="bring",
     )(pltpu.with_memory_space_constraint(left, pltpu.HBM), pltpu.with_memory_space_constraint(right, pltpu.HBM))
 
 
-def multiply(left, right, is_mine, per_core, first, total):
-    for i in range(per_core):
-        cols = columns(is_mine, i, per_core)
-        one = dot_tn(left[:BLOCK, cols], right[:BLOCK, cols])
-        first[head_cols(i)] = one
-        total[head_cols(i)] = one + dot_tn(left[BLOCK:, cols], right[BLOCK:, cols])
-
-
 def products(left, right):
     width = left.shape[1]
+    per_core = width // D // CORES
 
     def body(left, right, first, total):
-        multiply(left, right, True, width // D // CORES, first, total)
+        for i in range(per_core):
+            here, cols = head_cols(i), columns(True, i, per_core)
+            one = dot_tn(left[:BLOCK, cols], right[:BLOCK, cols])
+            first[here] = one
+            total[here] = one + dot_tn(left[BLOCK:, cols], right[BLOCK:, cols])
 
     state = jax.ShapeDtypeStruct((width // CORES, D), F32)
     return pl.pallas_call(
@@ -241,11 +246,12 @@
 def local_attention(q, k, v, is_mine, i, after):
     length, width = q.shape
 
-    def body(q, k, v, _, out):
+    def body(q, k, v, _, out, turned):
         cols = columns(is_mine, i, width // D // CORES)
         for c in range(length // BLOCK):
             rows = block_rows(c)
             qv, kv, vv = (x[rows, cols] for x in (q, k, v))
+            turned[:, rows] = jnp.transpose(qv)
             a, b, d = lower_product(qv, kv)
             out[c * BLOCK : c * BLOCK + HALF] = dot_nn(a, vv[TOP])
             out[c * BLOCK + HALF : (c + 1) * BLOCK] = dot_nn(beside(b, d), vv)
@@ -253,8 +259,8 @@
     return pl.pallas_call(
         body,
         in_specs=[VMEM, VMEM, VMEM, ANY],
-        out_specs=VMEM,
-        out_shape=jax.ShapeDtypeStruct((length, D), F32),
+        out_specs=[VMEM] * 2,
+        out_shape=[jax.ShapeDtypeStruct((length, D), F32), jax.ShapeDtypeStruct((D, length), BF16)],
         compiler_params=params(12),
         cost_estimate=pl.CostEstimate(
             flops=length // BLOCK * 4 * BLOCK * BLOCK * D, bytes_accessed=length * D * 10, transcendentals=0
@@ -299,12 +305,13 @@
     )(q, grad, *local, gain, state, first, *sums)
 
 
-def gradient(q, grad, attn, gain, sums, features, is_mine):
+def gradient(turned, grad, attn, gain, sums, features, is_mine):
     length, width = attn.shape
     per_core = width // D
     blocks = length // BLOCK
 
-    def body(q, grad, attn, gain, sums, out, last, total):
+    def body(*refs):
+        turned, (grad, attn, gain, sums, out, last, total) = refs[:per_core], refs[per_core:]
         for c in range(blocks):
             rows = block_rows(c)
             root = jnp.sqrt(sums[0:1, rows] / features + 1e-05)
@@ -315,7 +322,7 @@
                 scaled = gain[:, cols] * grad[rows, cols].astype(F32)
                 g = (scaled * inverse - attn[rows, head_cols(i)] * weight).astype(BF16)
                 out[rows, head_cols(i)] = g
-                term = dot_tn(q[rows, cols], g)
+                term = dot_nn(turned[i][:, rows], g)
                 total[head_cols(i)] = term if c == 0 else total[head_cols(i)] + term
                 if c == blocks - 1:
                     last[head_cols(i)] = term
@@ -323,12 +330,12 @@
     state = jax.ShapeDtypeStruct((width, D), F32)
     return pl.pallas_call(
         body,
-        in_specs=[VMEM] * 5,
+        in_specs=[VMEM] * (4 + per_core),
         out_specs=[VMEM] * 3,
         out_shape=[jax.ShapeDtypeStruct((length, width), BF16), state, state],
         compiler_params=params(16),
         name="gradient",
-    )(q, grad, attn, gain, sums)
+    )(*turned, grad, attn, gain, sums)
 
 
 def local_gradients(q, k, v, g, attn, gain, sums, state, first, features, is_mine, i, outs, after):
@@ -445,12 +452,14 @@
     keys, vals, first_theirs, theirs = bring(token_keys, values)
     first_mine, mine = products(keys, vals)
     first = {True: first_mine, False: first_theirs}
-    local = {True: [], False: []}
+    local, turned = {True: [], False: []}, {True: [], False: []}
 
     def attend(is_mine, i):
         def run(after):
-            local[is_mine].append(local_attention(queries, keys, vals, is_mine, i, after))
-            return local[is_mine][-1:]
+            out, query = local_attention(queries, keys, vals, is_mine, i, after)
+            local[is_mine].append(out)
+            turned[is_mine].append(query)
+            return [out]
 
         return run
 
@@ -466,7 +475,7 @@
     grad_attn, last, total = {}, {}, {}
     for is_mine in (False, True):
         grad_attn[is_mine], last[is_mine], total[is_mine] = gradient(
-            queries, out_grad, attn[is_mine], gain, sums, features, is_mine
+            turned[is_mine], out_grad, attn[is_mine], gain, sums, features, is_mine
         )
     outs, key_parts, value_parts = [], {True: [], False: []}, {True: [], False: []}
 

time: 81.2 us -> 81.3 us (level)
  no operation moved by 1% of the time
where the time goes in v5:
time: 81.3 us; the launch traced here: 81.2 us
  starting transfers between devices  37.5 us (46%)
  waiting for transfers between devices  22.3 us (27%)
  Pallas kernels  19.6 us (24%)
  between operations  1.03 us (1%)
    ppermute x20, starting transfers between devices, shift(): return lax.ppermute(value, 'seq', pairs)  33.4 us
    ppermute x20, waiting for transfers between devices, shift(): return lax.ppermute(value, 'seq', pairs)  19.3 us
    pallas_call x4, Pallas kernels, local_gradients(): pl.pallas_call(body, in_specs=[VMEM] * 9 + [HBM] * len(outs) + [ANY], out...  9.54 us
    ppermute x3, starting transfers between devices, head_sum(): lax.ppermute(part, 'head', [(i, (i + k) % count) for i in range(count)])  4.02 us
    ppermute x3, waiting for transfers between devices, head_sum(): lax.ppermute(part, 'head', [(i, (i + k) % count) for i in range(count)])  3.05 us
    pallas_call x4, Pallas kernels, local_attention(): pl.pallas_call(body, in_specs=[VMEM, VMEM, VMEM, ANY], out_specs=[VMEM] *...  2.74 us
    pallas_call x2, Pallas kernels, add_suffix(): pl.pallas_call(body, in_specs=[VMEM] * inputs + [HBM] * len(outs), out_sp...  2.59 us
    pallas_call x1, Pallas kernels, bring(): pl.pallas_call(body, in_specs=[HBM, HBM], out_specs=[VMEM] * 4, out_shape...  1.68 us
  transfers between devices with their start and end apart: 23, of which 15 were waited for; matrix products, arithmetic and copies ran while one was open for 0% of the time, Pallas kernels for 19%

profile of v5, /device:TPU:1, one launch (start us, length us, event | category | flops | bytes accessed | tf_op | source)
XLA Modules:
  0.0 81.2 jit_solution(1941327082342635356)
XLA Ops:
  0.6 1.7 %bring.1 = (bf16[1024,512]{1,0:T(8,128)(2,1)S(1)}, bf16[1024,512]{1,0:T(8,128)(2,1)S(1)}, f32[256,128]{1,0:T(8,128)S(1)}, f32[256,128]{1,0:T(8,128)S(1)}) custom-call(bf16[1024,512]{1,0:T(8,128)(2,1)} %left_hbm.1, bf16[1024,512]{1,0:T(8,128)(2,1)} %right_hbm.1), custom_call_target="tpu_custom_call" | custom-call | tf_op jit(solution)/shard_map/bring/pallas_call | solution.py:213
  2.3 3.3 %collective-permute-start = (f32[256,128]{1,0:T(8,128)S(1)}, f32[256,128]{1,0:T(8,128)S(1)}, u32[]{:S(2)}, u32[]{:S(2)}) collective-permute-start(f32[256,128]{1,0:T(8,128)S(1)} %get-tuple-element.67), channel_id=1, source_target_pairs={{0,4},{4,0},{8,12},{12,8},{16,20},{20,16},{24,28},{28,24},{32,36},... | collective-permute-start | bytes 393224 | tf_op jit(solution)/shard_map/ppermute | solution.py:92
  9.9 1.9 %collective-permute-done.1.refs_1_.refs_5_ = f32[128,128]{1,0:T(8,128)S(1)} collective-permute-done((f32[128,128]{1,0:T(8,128)S(1)}, f32[128,128]{1,0:T(8,128)S(1)}, u32[]{:S(2)}, u32[]{:S(2)}) %collective-permute-start.1) | collective-permute-done | bytes 65568 | tf_op jit(solution)/shard_map/ppermute | solution.py:92
  12.9 5.9 %collective-permute-start.5 = (f32[128,128]{1,0:T(8,128)S(1)}, f32[128,128]{1,0:T(8,128)S(1)}, u32[]{:S(2)}, u32[]{:S(2)}) collective-permute-start(f32[128,128]{1,0:T(8,128)S(1)} %add.17._.refs_0_), channel_id=1, source_target_pairs={{0,224},{4,228},{8,232},{12,236},{16,240},{20,244},{24,248},{28,25... | collective-permute-start | bytes 196616 | tf_op jit(solution)/shard_map/ppermute | solution.py:92
  20.1 3.0 %collective-permute-done.4.refs_1_.refs_0_ = f32[128,128]{1,0:T(8,128)S(1)} collective-permute-done((f32[128,128]{1,0:T(8,128)S(1)}, f32[128,128]{1,0:T(8,128)S(1)}, u32[]{:S(2)}, u32[]{:S(2)}) %collective-permute-start.4) | collective-permute-done | bytes 65568 | tf_op jit(solution)/shard_map/ppermute | solution.py:92
  23.6 1.7 %collective-permute-start.6 = (f32[128,128]{1,0:T(8,128)S(1)}, f32[128,128]{1,0:T(8,128)S(1)}, u32[]{:S(2)}, u32[]{:S(2)}) collective-permute-start(f32[128,128]{1,0:T(8,128)S(1)} %get-tuple-element.72._), channel_id=1, source_target_pairs={{0,64},{4,68},{8,72},{12,76},{16,80},{20,84},{24,88},{28,92},{32,9... | collective-permute-start | bytes 196616 | tf_op jit(solution)/shard_map/ppermute | solution.py:92
  26.0 2.1 %collective-permute-done.7.refs_3_ = f32[128,128]{1,0:T(8,128)S(1)} collective-permute-done((f32[128,128]{1,0:T(8,128)S(1)}, f32[128,128]{1,0:T(8,128)S(1)}, u32[]{:S(2)}, u32[]{:S(2)}) %collective-permute-start.7) | collective-permute-done | bytes 65568 | tf_op jit(solution)/shard_map/ppermute | solution.py:92
  28.1 1.4 %collective-permute-done.6.refs_2_ = f32[128,128]{1,0:T(8,128)S(1)} collective-permute-done((f32[128,128]{1,0:T(8,128)S(1)}, f32[128,128]{1,0:T(8,128)S(1)}, u32[]{:S(2)}, u32[]{:S(2)}) %collective-permute-start.6) | collective-permute-done | bytes 65568 | tf_op jit(solution)/shard_map/ppermute | solution.py:92
  30.4 2.7 %collective-permute-done.8.refs_3_ = f32[128,128]{1,0:T(8,128)S(1)} collective-permute-done((f32[128,128]{1,0:T(8,128)S(1)}, f32[128,128]{1,0:T(8,128)S(1)}, u32[]{:S(2)}, u32[]{:S(2)}) %collective-permute-start.8) | collective-permute-done | bytes 65568 | tf_op jit(solution)/shard_map/ppermute | solution.py:92
  33.1 5.0 %collective-permute-start.9 = (f32[256,128]{1,0:T(8,128)S(1)}, f32[256,128]{1,0:T(8,128)S(1)}, u32[]{:S(2)}, u32[]{:S(2)}) collective-permute-start(f32[256,128]{1,0:T(8,128)S(1)} %get-tuple-element.80), channel_id=1, source_target_pairs={{0,4},{4,0},{8,12},{12,8},{16,20},{20,16},{24,28},{28,24},{32,36},... | collective-permute-start | bytes 393224 | tf_op jit(solution)/shard_map/ppermute | solution.py:92
  40.0 3.0 %collective-permute-start.12 = (f32[2,1024]{1,0:T(2,128)S(1)}, f32[2,1024]{1,0:T(2,128)S(1)}, u32[]{:S(2)}, u32[]{:S(2)}) collective-permute-start(f32[2,1024]{1,0:T(2,128)S(1)} %get-tuple-element.86), channel_id=1, source_target_pairs={{0,3},{1,0},{2,1},{3,2},{4,7},{5,4},{6,5},{7,6},{8,11},{9,8},{10,9... | collective-permute-start | bytes 24584 | tf_op jit(solution)/shard_map/ppermute | solution.py:442
  44.0 3.0 %collective-permute-done.11 = f32[2,1024]{1,0:T(2,128)S(1)} collective-permute-done((f32[2,1024]{1,0:T(2,128)S(1)}, f32[2,1024]{1,0:T(2,128)S(1)}, u32[]{:S(2)}, u32[]{:S(2)}) %collective-permute-start.11) | collective-permute-done | bytes 8224 | tf_op jit(solution)/shard_map/ppermute | solution.py:442
  47.7 1.8 %collective-permute-start.13 = (f32[256,128]{1,0:T(8,128)S(1)}, f32[256,128]{1,0:T(8,128)S(1)}, u32[]{:S(2)}, u32[]{:S(2)}) collective-permute-start(f32[256,128]{1,0:T(8,128)S(1)} %get-tuple-element.93), channel_id=1, source_target_pairs={{0,4},{4,0},{8,12},{12,8},{16,20},{20,16},{24,28},{28,24},{32,36},... | collective-permute-start | bytes 393224 | tf_op jit(solution)/shard_map/ppermute | solution.py:92
  50.5 2.3 %collective-permute-start.16 = (f32[128,128]{1,0:T(8,128)S(1)}, f32[128,128]{1,0:T(8,128)S(1)}, u32[]{:S(2)}, u32[]{:S(2)}) collective-permute-start(f32[128,128]{1,0:T(8,128)S(1)} %get-tuple-element.97), channel_id=1, source_target_pairs={{0,24},{4,28},{8,0},{12,4},{16,8},{20,12},{24,16},{28,20},{32,56},... | collective-permute-start | bytes 196616 | tf_op jit(solution)/shard_map/ppermute | solution.py:92
  54.1 2.4 %local_gradients.4 = (bf16[1024,512]{1,0:T(8,128)(2,1)}, bf16[1024,512]{1,0:T(8,128)(2,1)}, f32[1024,128]{1,0:T(8,128)S(1)}, f32[1024,128]{1,0:T(8,128)S(1)}) custom-call(bf16[1024,512]{1,0:T(8,128)(2,1)S(1)} %copy-done, bf16[1024,512]{1,0:T(8,128)(2,1)S(1)} %get-tuple-element.64.left.k, bf16[1024,512]{1,0:T(8,128)(2,1)S(1)} %get-tuple-element.65.right.v, ...), custom_call_target="tpu_custom_call" | custom-call | flops 805306368 | bytes 2621440 | tf_op jit(solution)/shard_map/local_gradients/pallas_call | solution.py:378
  56.5 2.6 %collective-permute-done.14.refs_1_.refs_5_ = f32[128,128]{1,0:T(8,128)S(1)} collective-permute-done((f32[128,128]{1,0:T(8,128)S(1)}, f32[128,128]{1,0:T(8,128)S(1)}, u32[]{:S(2)}, u32[]{:S(2)}) %collective-permute-start.14) | collective-permute-done | bytes 65568 | tf_op jit(solution)/shard_map/ppermute | solution.py:92
  59.3 1.5 %collective-permute-start.17 = (f32[128,128]{1,0:T(8,128)S(1)}, f32[128,128]{1,0:T(8,128)S(1)}, u32[]{:S(2)}, u32[]{:S(2)}) collective-permute-start(f32[128,128]{1,0:T(8,128)S(1)} %add.18.refs_2_.refs_0_), channel_id=1, source_target_pairs={{0,32},{4,36},{8,40},{12,44},{16,48},{20,52},{24,56},{28,60},{32,6... | collective-permute-start | bytes 196616 | tf_op jit(solution)/shard_map/ppermute | solution.py:92
  60.7 2.4 %local_gradients.5 = (bf16[1024,512]{1,0:T(8,128)(2,1)}, bf16[1024,512]{1,0:T(8,128)(2,1)}, f32[1024,128]{1,0:T(8,128)S(1)}, f32[1024,128]{1,0:T(8,128)S(1)}) custom-call(bf16[1024,512]{1,0:T(8,128)(2,1)S(1)} %copy-done, bf16[1024,512]{1,0:T(8,128)(2,1)S(1)} %get-tuple-element.64.left.k, ...), custom_call_target="tpu_custom_call", output_to_operand_aliasing={{0}: (9, {}), {1}: (10, {})} | custom-call | flops 805306368 | bytes 2621440 | tf_op jit(solution)/shard_map/local_gradients/pallas_call | solution.py:378
  63.7 1.7 %collective-permute-start.20 = (f32[128,128]{1,0:T(8,128)S(1)}, f32[128,128]{1,0:T(8,128)S(1)}, u32[]{:S(2)}, u32[]{:S(2)}) collective-permute-start(f32[128,128]{1,0:T(8,128)S(1)} %get-tuple-element.105), channel_id=1, source_target_pairs={{0,160},{4,164},{8,168},{12,172},{16,176},{20,180},{24,184},{28,18... | collective-permute-start | bytes 196616 | tf_op jit(solution)/shard_map/ppermute | solution.py:92
  66.7 2.4 %local_gradients.6 = (bf16[1024,512]{1,0:T(8,128)(2,1)}, bf16[1024,512]{1,0:T(8,128)(2,1)}, f32[1024,128]{1,0:T(8,128)S(1)}, f32[1024,128]{1,0:T(8,128)S(1)}) custom-call(bf16[1024,512]{1,0:T(8,128)(2,1)S(1)} %copy-done, bf16[1024,512]{1,0:T(8,128)(2,1)S(1)} %get-tuple-element.64.left.k, ...), custom_call_target="tpu_custom_call", output_to_operand_aliasing={{0}: (9, {}), {1}: (10, {})} | custom-call | flops 805306368 | bytes 2621440 | tf_op jit(solution)/shard_map/local_gradients/pallas_call | solution.py:378
  69.1 1.6 %collective-permute-done.19.refs_2_ = f32[128,128]{1,0:T(8,128)S(1)} collective-permute-done((f32[128,128]{1,0:T(8,128)S(1)}, f32[128,128]{1,0:T(8,128)S(1)}, u32[]{:S(2)}, u32[]{:S(2)}) %collective-permute-start.19) | collective-permute-done | bytes 65568 | tf_op jit(solution)/shard_map/ppermute | solution.py:92
  70.8 2.4 %local_gradients.7 = (bf16[1024,512]{1,0:T(8,128)(2,1)}, bf16[1024,512]{1,0:T(8,128)(2,1)}, f32[1024,128]{1,0:T(8,128)S(1)}, f32[1024,128]{1,0:T(8,128)S(1)}) custom-call(bf16[1024,512]{1,0:T(8,128)(2,1)S(1)} %copy-done, bf16[1024,512]{1,0:T(8,128)(2,1)S(1)} %get-tuple-element.64.left.k, ...), custom_call_target="tpu_custom_call", output_to_operand_aliasing={{0}: (9, {}), {1}: (10, {})} | custom-call | flops 805306368 | bytes 2621440 | tf_op jit(solution)/shard_map/local_gradients/pallas_call | solution.py:378
  73.9 4.4 %collective-permute-start.22 = (f32[256,128]{1,0:T(8,128)S(1)}, f32[256,128]{1,0:T(8,128)S(1)}, u32[]{:S(2)}, u32[]{:S(2)}) collective-permute-start(f32[256,128]{1,0:T(8,128)S(1)} %get-tuple-element.114), channel_id=1, source_target_pairs={{0,4},{4,0},{8,12},{12,8},{16,20},{20,16},{24,28},{28,24},{32,36},... | collective-permute-start | bytes 393224 | tf_op jit(solution)/shard_map/ppermute | solution.py:92
  78.4 1.3 %add_suffix.2 = (bf16[1024,512]{1,0:T(8,128)(2,1)}, bf16[1024,512]{1,0:T(8,128)(2,1)}) custom-call(bf16[1024,512]{1,0:T(8,128)(2,1)S(1)} %get-tuple-element.64.left.k, bf16[1024,512]{1,0:T(8,128)(2,1)S(1)} %get-tuple-element.65.right.v, f32[1024,128]{1,0:T(8,128)S(1)} %get-tuple-element.116.refs_0_, f32[1024,128]{1,0:T(8,128)S(1)} %get-tuple-element.117.refs_1_, ...), custom_call_target="tpu_custom_call" | custom-call | tf_op jit(solution)/shard_map/add_suffix/pallas_call | solution.py:426
  (55 shorter events, 18.8 us)
Async XLA Ops:
  2.3 4.3 %collective-permute-start = (f32[256,128]{1,0:T(8,128)S(1)}, f32[256,128]{1,0:T(8,128)S(1)}, u32[]{:S(2)}, u32[]{:S(2)}) collective-permute-start(f32[256,128]{1,0:T(8,128)S(1)} %get-tuple-element.67), channel_id=1, source_target_pairs={{0,4},{4,0},{8,12},{12,8},{16,20},{20,16},{24,28},{28,24},{32,36},... | collective-permute-start | bytes 393224 | tf_op jit(solution)/shard_map/ppermute | solution.py:92
  6.6 3.2 %collective-permute-start.3 = (f32[128,128]{1,0:T(8,128)S(1)}, f32[128,128]{1,0:T(8,128)S(1)}, u32[]{:S(2)}, u32[]{:S(2)}) collective-permute-start(f32[128,128]{1,0:T(8,128)S(1)} %get-tuple-element.69), channel_id=1, source_target_pairs={{0,24},{4,28},{8,0},{12,4},{16,8},{20,12},{24,16},{28,20},{32,56},... | collective-permute-start | bytes 196616 | tf_op jit(solution)/shard_map/ppermute | solution.py:92
  7.5 4.3 %collective-permute-start.1 = (f32[128,128]{1,0:T(8,128)S(1)}, f32[128,128]{1,0:T(8,128)S(1)}, u32[]{:S(2)}, u32[]{:S(2)}) collective-permute-start(f32[128,128]{1,0:T(8,128)S(1)} %get-tuple-element.69), channel_id=1, source_target_pairs={{0,8},{4,12},{8,16},{12,20},{16,24},{20,28},{24,0},{28,4},{32,40},... | collective-permute-start | bytes 196616 | tf_op jit(solution)/shard_map/ppermute | solution.py:92
  8.2 4.7 %collective-permute-start.2 = (f32[128,128]{1,0:T(8,128)S(1)}, f32[128,128]{1,0:T(8,128)S(1)}, u32[]{:S(2)}, u32[]{:S(2)}) collective-permute-start(f32[128,128]{1,0:T(8,128)S(1)} %get-tuple-element.68._.refs_0_.refs_4_), channel_id=1, source_target_pairs={{0,16},{4,20},{8,24},{12,28},{16,0},{20,4},{24,8},{28,12},{32,48},... | collective-permute-start | bytes 196616 | tf_op jit(solution)/shard_map/ppermute | solution.py:92
  12.9 7.2 %collective-permute-start.5 = (f32[128,128]{1,0:T(8,128)S(1)}, f32[128,128]{1,0:T(8,128)S(1)}, u32[]{:S(2)}, u32[]{:S(2)}) collective-permute-start(f32[128,128]{1,0:T(8,128)S(1)} %add.17._.refs_0_), channel_id=1, source_target_pairs={{0,224},{4,228},{8,232},{12,236},{16,240},{20,244},{24,248},{28,25... | collective-permute-start | bytes 196616 | tf_op jit(solution)/shard_map/ppermute | solution.py:92
  18.8 4.3 %collective-permute-start.4 = (f32[128,128]{1,0:T(8,128)S(1)}, f32[128,128]{1,0:T(8,128)S(1)}, u32[]{:S(2)}, u32[]{:S(2)}) collective-permute-start(f32[128,128]{1,0:T(8,128)S(1)} %add.17._.refs_0_), channel_id=1, source_target_pairs={{0,32},{4,36},{8,40},{12,44},{16,48},{20,52},{24,56},{28,60},{32,6... | collective-permute-start | bytes 196616 | tf_op jit(solution)/shard_map/ppermute | solution.py:92
  23.1 5.0 %collective-permute-start.7 = (f32[128,128]{1,0:T(8,128)S(1)}, f32[128,128]{1,0:T(8,128)S(1)}, u32[]{:S(2)}, u32[]{:S(2)}) collective-permute-start(f32[128,128]{1,0:T(8,128)S(1)} %get-tuple-element.74), channel_id=1, source_target_pairs={{0,160},{4,164},{8,168},{12,172},{16,176},{20,180},{24,184},{28,18... | collective-permute-start | bytes 196616 | tf_op jit(solution)/shard_map/ppermute | solution.py:92
  23.6 5.9 %collective-permute-start.6 = (f32[128,128]{1,0:T(8,128)S(1)}, f32[128,128]{1,0:T(8,128)S(1)}, u32[]{:S(2)}, u32[]{:S(2)}) collective-permute-start(f32[128,128]{1,0:T(8,128)S(1)} %get-tuple-element.72._), channel_id=1, source_target_pairs={{0,64},{4,68},{8,72},{12,76},{16,80},{20,84},{24,88},{28,92},{32,9... | collective-permute-start | bytes 196616 | tf_op jit(solution)/shard_map/ppermute | solution.py:92
  29.6 3.5 %collective-permute-start.8 = (f32[128,128]{1,0:T(8,128)S(1)}, f32[128,128]{1,0:T(8,128)S(1)}, u32[]{:S(2)}, u32[]{:S(2)}) collective-permute-start(f32[128,128]{1,0:T(8,128)S(1)} %get-tuple-element.76._), channel_id=1, source_target_pairs={{0,8},{4,12},{8,0},{12,4},{16,24},{20,28},{24,16},{28,20},{32,40},... | collective-permute-start | bytes 196616 | tf_op jit(solution)/shard_map/ppermute | solution.py:92
  29.7 8.5 %copy-start.1 = (bf16[1024,512]{1,0:T(8,128)(2,1)S(1)}, bf16[1024,512]{1,0:T(8,128)(2,1)}, u32[]{:S(2)}) copy-start(bf16[1024,512]{1,0:T(8,128)(2,1)} %refs_2_.3) | copy-start | bytes 3145732
  33.1 6.3 %collective-permute-start.9 = (f32[256,128]{1,0:T(8,128)S(1)}, f32[256,128]{1,0:T(8,128)S(1)}, u32[]{:S(2)}, u32[]{:S(2)}) collective-permute-start(f32[256,128]{1,0:T(8,128)S(1)} %get-tuple-element.80), channel_id=1, source_target_pairs={{0,4},{4,0},{8,12},{12,8},{16,20},{20,16},{24,28},{28,24},{32,36},... | collective-permute-start | bytes 393224 | tf_op jit(solution)/shard_map/ppermute | solution.py:92
  40.0 4.0 %collective-permute-start.12 = (f32[2,1024]{1,0:T(2,128)S(1)}, f32[2,1024]{1,0:T(2,128)S(1)}, u32[]{:S(2)}, u32[]{:S(2)}) collective-permute-start(f32[2,1024]{1,0:T(2,128)S(1)} %get-tuple-element.86), channel_id=1, source_target_pairs={{0,3},{1,0},{2,1},{3,2},{4,7},{5,4},{6,5},{7,6},{8,11},{9,8},{10,9... | collective-permute-start | bytes 24584 | tf_op jit(solution)/shard_map/ppermute | solution.py:442
  43.0 4.0 %collective-permute-start.11 = (f32[2,1024]{1,0:T(2,128)S(1)}, f32[2,1024]{1,0:T(2,128)S(1)}, u32[]{:S(2)}, u32[]{:S(2)}) collective-permute-start(f32[2,1024]{1,0:T(2,128)S(1)} %get-tuple-element.86), channel_id=1, source_target_pairs={{0,2},{1,3},{2,0},{3,1},{4,6},{5,7},{6,4},{7,5},{8,10},{9,11},{10,... | collective-permute-start | bytes 24584 | tf_op jit(solution)/shard_map/ppermute | solution.py:442
  43.3 3.7 %collective-permute-start.10 = (f32[2,1024]{1,0:T(2,128)S(1)}, f32[2,1024]{1,0:T(2,128)S(1)}, u32[]{:S(2)}, u32[]{:S(2)}) collective-permute-start(f32[2,1024]{1,0:T(2,128)S(1)} %get-tuple-element.86), channel_id=1, source_target_pairs={{0,1},{1,2},{2,3},{3,0},{4,5},{5,6},{6,7},{7,4},{8,9},{9,10},{10,1... | collective-permute-start | bytes 24584 | tf_op jit(solution)/shard_map/ppermute | solution.py:442
  47.7 2.8 %collective-permute-start.13 = (f32[256,128]{1,0:T(8,128)S(1)}, f32[256,128]{1,0:T(8,128)S(1)}, u32[]{:S(2)}, u32[]{:S(2)}) collective-permute-start(f32[256,128]{1,0:T(8,128)S(1)} %get-tuple-element.93), channel_id=1, source_target_pairs={{0,4},{4,0},{8,12},{12,8},{16,20},{20,16},{24,28},{28,24},{32,36},... | collective-permute-start | bytes 393224 | tf_op jit(solution)/shard_map/ppermute | solution.py:92
  50.5 6.0 %collective-permute-start.16 = (f32[128,128]{1,0:T(8,128)S(1)}, f32[128,128]{1,0:T(8,128)S(1)}, u32[]{:S(2)}, u32[]{:S(2)}) collective-permute-start(f32[128,128]{1,0:T(8,128)S(1)} %get-tuple-element.97), channel_id=1, source_target_pairs={{0,24},{4,28},{8,0},{12,4},{16,8},{20,12},{24,16},{28,20},{32,56},... | collective-permute-start | bytes 196616 | tf_op jit(solution)/shard_map/ppermute | solution.py:92
  52.9 6.3 %collective-permute-start.14 = (f32[128,128]{1,0:T(8,128)S(1)}, f32[128,128]{1,0:T(8,128)S(1)}, u32[]{:S(2)}, u32[]{:S(2)}) collective-permute-start(f32[128,128]{1,0:T(8,128)S(1)} %get-tuple-element.97), channel_id=1, source_target_pairs={{0,8},{4,12},{8,16},{12,20},{16,24},{20,28},{24,0},{28,4},{32,40},... | collective-permute-start | bytes 196616 | tf_op jit(solution)/shard_map/ppermute | solution.py:92
  52.9 6.3 %collective-permute-start.15 = (f32[128,128]{1,0:T(8,128)S(1)}, f32[128,128]{1,0:T(8,128)S(1)}, u32[]{:S(2)}, u32[]{:S(2)}) collective-permute-start(f32[128,128]{1,0:T(8,128)S(1)} %get-tuple-element.94.refs_0_.refs_4_), channel_id=1, source_target_pairs={{0,16},{4,20},{8,24},{12,28},{16,0},{20,4},{24,8},{28,12},{32,48},... | collective-permute-start | bytes 196616 | tf_op jit(solution)/shard_map/ppermute | solution.py:92
  59.2 3.9 %collective-permute-start.18 = (f32[128,128]{1,0:T(8,128)S(1)}, f32[128,128]{1,0:T(8,128)S(1)}, u32[]{:S(2)}, u32[]{:S(2)}) collective-permute-start(f32[128,128]{1,0:T(8,128)S(1)} %add.18.refs_2_.refs_0_), channel_id=1, source_target_pairs={{0,224},{4,228},{8,232},{12,236},{16,240},{20,244},{24,248},{28,25... | collective-permute-start | bytes 196616 | tf_op jit(solution)/shard_map/ppermute | solution.py:92
  59.3 4.4 %collective-permute-start.17 = (f32[128,128]{1,0:T(8,128)S(1)}, f32[128,128]{1,0:T(8,128)S(1)}, u32[]{:S(2)}, u32[]{:S(2)}) collective-permute-start(f32[128,128]{1,0:T(8,128)S(1)} %add.18.refs_2_.refs_0_), channel_id=1, source_target_pairs={{0,32},{4,36},{8,40},{12,44},{16,48},{20,52},{24,56},{28,60},{32,6... | collective-permute-start | bytes 196616 | tf_op jit(solution)/shard_map/ppermute | solution.py:92
  63.7 5.3 %collective-permute-start.20 = (f32[128,128]{1,0:T(8,128)S(1)}, f32[128,128]{1,0:T(8,128)S(1)}, u32[]{:S(2)}, u32[]{:S(2)}) collective-permute-start(f32[128,128]{1,0:T(8,128)S(1)} %get-tuple-element.105), channel_id=1, source_target_pairs={{0,160},{4,164},{8,168},{12,172},{16,176},{20,180},{24,184},{28,18... | collective-permute-start | bytes 196616 | tf_op jit(solution)/shard_map/ppermute | solution.py:92
  65.4 5.2 %collective-permute-start.19 = (f32[128,128]{1,0:T(8,128)S(1)}, f32[128,128]{1,0:T(8,128)S(1)}, u32[]{:S(2)}, u32[]{:S(2)}) collective-permute-start(f32[128,128]{1,0:T(8,128)S(1)} %get-tuple-element.102.refs_2_), channel_id=1, source_target_pairs={{0,64},{4,68},{8,72},{12,76},{16,80},{20,84},{24,88},{28,92},{32,9... | collective-permute-start | bytes 196616 | tf_op jit(solution)/shard_map/ppermute | solution.py:92
  70.7 3.2 %collective-permute-start.21 = (f32[128,128]{1,0:T(8,128)S(1)}, f32[128,128]{1,0:T(8,128)S(1)}, u32[]{:S(2)}, u32[]{:S(2)}) collective-permute-start(f32[128,128]{1,0:T(8,128)S(1)} %get-tuple-element.107.refs_2_), channel_id=1, source_target_pairs={{0,8},{4,12},{8,0},{12,4},{16,24},{20,28},{24,16},{28,20},{32,40},... | collective-permute-start | bytes 196616 | tf_op jit(solution)/shard_map/ppermute | solution.py:92
  73.9 5.7 %collective-permute-start.22 = (f32[256,128]{1,0:T(8,128)S(1)}, f32[256,128]{1,0:T(8,128)S(1)}, u32[]{:S(2)}, u32[]{:S(2)}) collective-permute-start(f32[256,128]{1,0:T(8,128)S(1)} %get-tuple-element.114), channel_id=1, source_target_pairs={{0,4},{4,0},{8,12},{12,8},{16,20},{20,16},{24,28},{28,24},{32,36},... | collective-permute-start | bytes 393224 | tf_op jit(solution)/shard_map/ppermute | solution.py:92
  (2 other events, 4.2 us)
